TPU v7x, 32 devices: a whole 2x2x4 slice. The times are simulated.
32 devices in a mesh: gx: 2 (over y), gy: 4 (over x, core), dir: 4 (over z).
Axes of the slice: x: 2, y: 2, z: 4, core: 2. Of those that a mesh axis runs over, the one named last changes fastest.
Arguments:
- directions: float32 [32, 256, 1024], P('dir', 'gx', 'gy'), may hold values from -6 to 6
- velocity: float32 [2, 256, 1024], P(None, 'gx', 'gy'), may hold values from -6 to 6
- viscosity: float32 [256, 1024], P('gx', 'gy'), may hold values from 0.5 to 2
- basal_drag: float32 [256, 1024], P('gx', 'gy'), may hold values from 0.5 to 8
- misfit_weight: float32 [256, 1024], P('gx', 'gy'), may hold values from 1 to 10
- ice_mask: int32 [256, 1024], P('gx', 'gy'), may hold values 0 or 1
- grounded: int32 [256, 1024], P('gx', 'gy'), may hold values 0 or 1
Outputs:
- basis: float32 [32, 256, 1024], P('dir', 'gx', 'gy')
- upper: float32 [32, 32], replicated
All inputs are finite; a program needn't handle non-finite values. No bound on the sum of `ice_mask` or of `grounded` on one device may be relied on, other than what follows from the above.
Results may differ from a plain program's by a relative error of at most 0.00021.
Values sent between devices are 32-bit elements; how exact they have to be, the bound alone decides.
No kernel may reach another device: no remote copies, remote signals or barrier semaphores. Data moves between devices by JAX's collectives and lax.ppermute only.
A program may use at most 64 MiB of HBM per device.

v0:
```python
import functools

import jax
import jax.numpy as jnp
from jax import lax
from jax.experimental import pallas as pl
from jax.experimental.pallas import tpu as pltpu
from jax.sharding import PartitionSpec as P

SWEEPS = 6
damping = 0.8
KEEP_BACK = 1.0 - damping
REACH = 2 * (SWEEPS - 1)
PAD = 16
LANES = 128
BANDS = 4
SPANS = LANES // BANDS
PLANES = 8
FIELDS = 5
F32 = jnp.float32
BF16 = jnp.bfloat16
AXES = ("gx", "gy", "dir")
WEIGHTS = ((4.0, 1.0), (1.0, 4.0))


def iota(shape, dim):
    return lax.broadcasted_iota(jnp.int32, shape, dim)


def roll(value, shift):
    return pltpu.roll(value, shift % LANES, 1)


def pack(counts, place, *refs):
    count_x, count_y = counts
    sources, refs = refs[:7], refs[7:]
    fields, refs = refs[0], refs[1:]
    row_out, refs = refs[:count_x], refs[count_x:]
    col_out, refs = refs[:count_y], refs[count_y:]
    corner_out, refs = refs[: count_x * count_y], refs[count_x * count_y :]
    held, sems = refs[:7], refs[7]
    copies = [
        pltpu.make_async_copy(source, target, sems.at[i])
        for i, (source, target) in enumerate(zip(sources, held))
    ]
    for copy in copies:
        copy.start()
    for copy in copies[1:]:
        copy.wait()
    dirs, velocity, viscosity, drag, weight, mask, grounded = held
    rows, cols = viscosity.shape
    friction = drag[...] * grounded[...].astype(F32)
    fields[0] = friction * velocity[0]
    fields[1] = friction * velocity[1]
    fields[2] = friction
    fields[3] = viscosity[...]
    fields[4] = weight[...] * mask[...].astype(F32)
    copies[0].wait()

    for pairing, out in enumerate(row_out):
        send_last = place[0] % 2 == pairing
        base = pl.ds(pl.multiple_of(jnp.where(send_last, rows - PAD, 0), PAD), PAD)
        out[:PLANES] = dirs[:, base, :]
        out[PLANES:] = fields[:, base, :]

    lane = iota((8, LANES), 1)
    for g in range(rows // 8):
        span = slice(8 * g, 8 * g + 8)
        for q, (planes, count) in enumerate(((dirs, PLANES), (fields, FIELDS))):
            first = planes[0, span, :LANES]
            last = roll(planes[0, span, cols - LANES :], PAD)
            for p in range(1, count):
                here = lane >= PAD * p
                first = jnp.where(here, roll(planes[p, span, :LANES], PAD * p), first)
                last = jnp.where(
                    here, roll(planes[p, span, cols - LANES :], PAD * (p + 1)), last
                )
            for pairing, out in enumerate(col_out):
                send_last = place[1] % 2 == pairing
                out[q, g] = jnp.where(send_last, last, first)
    for i in range(count_x):
        send_last = place[0] % 2 == i
        base = pl.ds(jnp.where(send_last, (rows - PAD) // 8, 0), PAD // 8)
        for j in range(count_y):
            corner_out[i * count_y + j][...] = col_out[j][:, base]


def exchange_blocks(tiles):
    lane = iota((8, LANES), 1)
    for bit, width in ((1, SPANS), (2, 2 * SPANS)):
        low = (lane // width) % 2 == 0
        tiles = [
            jnp.where(low, tiles[a], roll(tiles[a ^ bit], width))
            if a & bit == 0
            else jnp.where(low, roll(tiles[a ^ bit], -width), tiles[a])
            for a in range(4)
        ]
    return tiles


def split_dot(value, places):
    total = None
    for step in range(3):
        part = value.astype(BF16)
        product = jnp.dot(part, places, preferred_element_type=F32)
        total = product if total is None else total + product
        if step < 2:
            value = value - part.astype(F32)
    return total


def solve(counts, place, *refs):
    count_x, count_y = counts
    got_rows, refs = refs[:count_x], refs[count_x:]
    got_cols, refs = refs[:count_y], refs[count_y:]
    got_corners, refs = refs[: count_x * count_y], refs[count_x * count_y :]
    dirs, fields, *refs = refs
    *outs, halo_rows, halo_cols, lined, turned, planes, coeffs, extras, base, ping, pong = refs
    rows, cols = dirs.shape[1:]
    tall = lined.shape[0]
    over = (tall - rows) // 2
    high = tall // BANDS
    wide = planes.shape[2]
    groups = (rows + 2 * PAD) // 8
    edge = PAD // 8
    even = [place[0] % 2 == 0, place[1] % 2 == 0]

    def sides(axis, one, two):
        return jnp.where(even[axis], two, one), jnp.where(even[axis], one, two)

    def pair(got, index):
        one = got[0][index]
        return one, (got[1][index] if len(got) > 1 else jnp.zeros_like(one))

    for p in range(PLANES + FIELDS):
        halo_rows[0, p], halo_rows[1, p] = sides(0, *pair(got_rows, p))
    for q in range(2):
        left, right = sides(1, *pair(got_cols, q))
        halo_cols[0, q, edge : groups - edge] = left
        halo_cols[1, q, edge : groups - edge] = right
        by_x = [
            sides(1, *pair(got_corners[i * count_y : (i + 1) * count_y], q))
            for i in range(count_x)
        ]
        for side in range(2):
            one = by_x[0][side]
            two = by_x[1][side] if count_x > 1 else jnp.zeros_like(one)
            above, below = sides(0, one, two)
            halo_cols[side, q, :edge] = above
            halo_cols[side, q, groups - edge :] = below

    def spread(shape, source, target):
        k, n = iota(shape, source), iota(shape, target)
        inner = k < cols
        slot = (k - cols) % PAD + jnp.where(k < cols + LANES, 0, cols + PAD)
        at = jnp.where(inner, k + PAD, slot)
        return jnp.where(
            (at == wide * (n % SPANS) + n // SPANS) & (n < wide * SPANS), 1.0, 0.0
        ).astype(BF16)

    lanes_out = turned.shape[2]
    places = spread((cols + 2 * LANES, lanes_out), 0, 1)
    lane = iota((8, LANES), 1)
    own_slot = lane // PAD == iota((8, LANES), 0)

    for q, (source, first, count) in enumerate(((dirs, 0, PLANES), (fields, PLANES, FIELDS))):
        for g in range(groups):
            inner = edge <= g < groups - edge
            side, at = (0, g) if g < edge else (1, g - groups + edge)
            stack = []
            for p in range(PLANES):
                if p >= count:
                    stack.append(jnp.zeros((8, cols), F32))
                elif inner:
                    stack.append(source[p, 8 * (g - edge) : 8 * (g - edge) + 8, :])
                else:
                    stack.append(halo_rows[side, first + p, 8 * at : 8 * at + 8, :])
            lines = jnp.swapaxes(jnp.stack(stack), 0, 1)
            for s in range(8):
                line = 8 * g + s - (PAD - over)
                if 0 <= line < tall:
                    lined[line, :, :cols] = lines[s]
                    for side_y in range(2):
                        begin = cols + LANES * side_y
                        lined[line, :, begin : begin + LANES] = jnp.where(
                            own_slot, halo_cols[side_y, q, g, s : s + 1, :], 0.0
                        )

        def turn(b, _):
            value = lined[pl.ds(high * b, high)].reshape(high * 8, cols + 2 * LANES)
            turned[pl.ds(high * b, high)] = split_dot(value, places).reshape(
                high, 8, lanes_out
            )
            return 0

        lax.fori_loop(0, BANDS, turn, 0)

        def band(i, _):
            for t in range(lanes_out // LANES):
                tiles = [
                    turned[high * b + i, :, LANES * t : LANES * t + LANES] for b in range(BANDS)
                ]
                tiles = exchange_blocks(tiles)
                for a in range(BANDS):
                    if BANDS * t + a < wide:
                        planes[q, i, BANDS * t + a] = tiles[a]
            return 0

        lax.fori_loop(0, high, band, 0)

    row_of = iota((8, LANES), 0)

    def weigh(i, above, below, turn_above, turn_below):
        def field(k, row, j):
            return jnp.broadcast_to(planes[1, row, j, k : k + 1, :], (8, LANES))

        mids = [field(3, i, j) for j in range(wide)]
        wests = [roll(mids[-1], 1)] + mids[:-1]
        easts = mids[1:] + [roll(mids[0], -1)]
        for j in range(wide):
            mid = mids[j]
            up, down = field(3, above, j), field(3, below, j)
            up = roll(up, SPANS) if turn_above else up
            down = roll(down, -SPANS) if turn_below else down
            east, west = 0.5 * (mid + down), 0.5 * (mid + up)
            north, south = 0.5 * (mid + easts[j]), 0.5 * (mid + wests[j])
            along_x, along_y = east + west, north + south
            friction, kept = field(2, i, j), field(4, i, j)

            def step(is_first):
                ax = jnp.where(is_first, WEIGHTS[0][0], WEIGHTS[1][0])
                ay = jnp.where(is_first, WEIGHTS[0][1], WEIGHTS[1][1])
                diagonal = ax * along_x + ay * along_y + friction
                return ax, ay, jnp.where(kept != 0.0, damping / diagonal, 0.0)

            ax, ay, gain = step(row_of < 4)
            kind = row_of % 4
            face = jnp.where(kind < 2, jnp.where(kind == 0, east, west), jnp.where(kind == 2, north, south))
            coeffs[i, j] = gain * jnp.where(kind < 2, ax, ay) * face
            _, _, gain = step(row_of % 2 == 0)
            pull = -jnp.where(row_of % 2 == 0, field(0, i, j), field(1, i, j))
            extras[i, j] = jnp.where(
                row_of < 4, gain * jnp.where(row_of < 2, pull, kept), pull
            )

    weigh(0, high - 1, 1, True, False)
    weigh(high - 1, high - 2, 0, False, True)

    def weigh_inner(i, _):
        weigh(i, i - 1, i + 1, False, False)
        return 0

    lax.fori_loop(1, high - 1, weigh_inner, 0)

    def put(ref, m, i, j, value, edges=True):
        ref[m, i + 1, j] = value
        if edges and isinstance(i, int):
            if i == 0:
                ref[m, high + 1, j] = roll(value, -SPANS)
            if i == high - 1:
                ref[m, 0, j] = roll(value, SPANS)

    def over_rows(body):
        body(0)
        body(high - 1)

        def two(i, _):
            body(2 * i + 1)
            body(2 * i + 2)
            return 0

        lax.fori_loop(0, (high - 2) // 2, two, 0)

    def start(i):
        for j in range(wide):
            for m in range(2):
                put(base, m, i, j, extras[i, j, m : m + 1, :] * planes[0, i, j])

    over_rows(start)

    def sweep(source, store):
        def body(i):
            for m in range(2):
                mids = [source[m, i + 1, j] for j in range(wide)]
                before = [roll(mids[-1], 1)] + mids[:-1]
                after = mids[1:] + [roll(mids[0], -1)]
                for j in range(wide):
                    e, w, n, s = (coeffs[i, j, 4 * m + d : 4 * m + d + 1, :] for d in range(4))
                    store(
                        m,
                        i,
                        j,
                        (base[m, i + 1, j] + KEEP_BACK * mids[j])
                        + (e * source[m, i + 2, j] + w * source[m, i, j])
                        + (n * after[j] + s * before[j]),
                    )

        over_rows(body)

    def to(ref):
        return lambda m, i, j, value: put(ref, m, i, j, value)

    def to_adjoint(m, i, j, value):
        pong[m, i + 1, j] = extras[i, j, 2 + m : 3 + m, :] * value

    def to_sketch(m, i, j, value):
        value = extras[i, j, 4 + m : 5 + m, :] * value
        planes[0, i, j] = value if m == 0 else planes[0, i, j] + value

    for part in range(2):
        source = base
        for step in range(SWEEPS - 2):
            target = ping if source is not ping else pong
            sweep(source, to(target))
            source = target
        if part == 0:
            target = ping if source is not ping else pong

            def adjoint(m, i, j, value, target=target):
                put(target, m, i, j, extras[i, j, 2 + m : 3 + m, :] * value)

            sweep(source, adjoint)
            base, ping, pong = target, base, source
        else:
            sweep(source, to_sketch)

    def unband(i, _):
        for t in range(lanes_out // LANES):
            tiles = [
                planes[0, i, BANDS * t + a] if BANDS * t + a < wide else jnp.zeros((8, LANES), F32)
                for a in range(BANDS)
            ]
            tiles = exchange_blocks(tiles)
            for b in range(BANDS):
                turned[high * b + i, :, LANES * t : LANES * t + LANES] = tiles[b]
        return 0

    lax.fori_loop(0, high, unband, 0)
    places = spread((lanes_out, cols), 1, 0)
    part = rows // len(outs)
    for k, out in enumerate(outs):
        value = turned[pl.ds(over + part * (place[2] ^ k), part)].reshape(part * 8, lanes_out)
        out[...] = split_dot(value, places).reshape(part, 8, cols)


def gram_of(place, *refs):
    parts, (whole, gram) = refs[:-2], refs[-2:]
    count = len(parts)
    for k, part in enumerate(parts):
        block = pl.multiple_of(8 * (place[2] ^ k), 8)
        for r in range(part.shape[0]):
            whole[r, pl.ds(block, 8), :] = part[r]
    total = jnp.zeros((8 * count, 8 * count), F32)
    for r in range(whole.shape[0]):
        total = total + lax.dot_general(
            whole[r],
            whole[r],
            (((1,), (1,)), ((), ())),
            precision=lax.Precision.HIGHEST,
            preferred_element_type=F32,
        )
    gram[...] = total


def factor(gram, size):
    lane = iota((size, LANES), 1)
    row_of = iota((size, LANES), 0)
    wide = jnp.concatenate([gram, jnp.zeros((size, LANES - size), F32)], axis=1)
    work = jnp.where(lane < size, wide, jnp.where(lane == row_of + size, 1.0, 0.0))
    pivots = jnp.ones((size, 1), F32)
    index = iota((size, 1), 0)
    for k in range(size):
        top = work[k : k + 1, :]
        pivot = top[:, k : k + 1]
        ratio = jnp.where(index > k, work[:, k : k + 1] / pivot, 0.0)
        pivots = jnp.where(index == k, pivot, pivots)
        work = work - ratio * top
    return work / jnp.sqrt(pivots), lane, row_of


def basis_of(cells, place, gram_ref, whole, *refs):
    outs, upper, scratch = refs[:-2], refs[-2], refs[-1]
    size = gram_ref.shape[0]
    count = len(outs)
    work, lane, row_of = factor(gram_ref[...] / cells, size)
    upper[...] = jnp.where(lane >= row_of, work, 0.0)[:, :size]
    scratch[...] = work
    inverse = jnp.concatenate(
        [
            scratch[pl.ds(pl.multiple_of(8 * (place[2] ^ k), 8), 8), :]
            for k in range(count)
        ],
        axis=0,
    )[:, size : 2 * size]
    for r in range(whole.shape[0]):
        value = jnp.dot(
            inverse, whole[r], precision=lax.Precision.HIGHEST, preferred_element_type=F32
        )
        for k, out in enumerate(outs):
            out[r] = value[8 * k : 8 * k + 8]


def assemble(place, *refs):
    parts, out = refs[:-1], refs[-1]
    for k, part in enumerate(parts):
        rows = part.shape[0]
        base = rows * (place[2] ^ k)
        for c in range(rows // 8):
            out[:, pl.ds(pl.multiple_of(base + 8 * c, 8), 8), :] = jnp.swapaxes(
                part[8 * c : 8 * c + 8], 0, 1
            )


def call(kernel, outs, *args, scratch=(), limit=56, space=pltpu.VMEM):
    smem = pl.BlockSpec(memory_space=pltpu.SMEM)
    vmem = pl.BlockSpec(memory_space=pltpu.VMEM)
    shapes = [jax.ShapeDtypeStruct(shape, F32) for shape in outs]
    return pl.pallas_call(
        kernel,
        out_shape=shapes,
        in_specs=[smem] + [pl.BlockSpec(memory_space=space)] * (len(args) - 1),
        out_specs=[vmem] * len(shapes),
        scratch_shapes=[
            pltpu.VMEM(shape, F32) if isinstance(shape, tuple) else shape for shape in scratch
        ],
        compiler_params=pltpu.CompilerParams(vmem_limit_bytes=limit << 20),
    )(*args)


def pairings(count):
    sets = []
    for first in (0, 1):
        pairs = [(i, i + 1) for i in range(first, count - 1, 2)]
        if pairs:
            sets.append(pairs + [(j, i) for i, j in pairs])
    return sets


def swap_bit(value, axis, bit):
    count = lax.axis_size(axis)
    return lax.ppermute(value, axis, [(i, i ^ bit) for i in range(count)])


def sum_all(value):
    for axis in ("gy", "gx", "dir"):
        bit = 1
        while bit < lax.axis_size(axis):
            value = value + swap_bit(value, axis, bit)
            bit *= 2
    return value


def on_device(directions, velocity, viscosity, basal_drag, misfit_weight, ice_mask, grounded):
    own, rows, cols = directions.shape
    across = lax.axis_size("dir")
    place = jnp.stack([lax.axis_index(axis) for axis in AXES]).astype(jnp.int32)
    args = (directions, velocity, viscosity, basal_drag, misfit_weight, ice_mask, grounded)

    count_y = lax.axis_size("gy")
    sets_x, sets_y = pairings(lax.axis_size("gx")), pairings(count_y)
    counts = (len(sets_x), len(sets_y))
    fields, *messages = call(
        functools.partial(pack, counts),
        [(FIELDS, rows, cols)]
        + [(PLANES + FIELDS, PAD, cols)] * counts[0]
        + [(2, rows // 8, 8, LANES)] * counts[1]
        + [(2, PAD // 8, 8, LANES)] * (counts[0] * counts[1]),
        place,
        *args,
        scratch=[pltpu.VMEM(a.shape, a.dtype) for a in args] + [pltpu.SemaphoreType.DMA((7,))],
        space=pl.ANY,
    )
    moves = [("gx", s) for s in sets_x] + [("gy", s) for s in sets_y]
    for set_x in sets_x:
        for set_y in sets_y:
            pairs = [(a * count_y + c, b * count_y + d) for a, b in set_x for c, d in set_y]
            moves.append((("gx", "gy"), pairs))
    got = [lax.ppermute(m, axis, pairs) for m, (axis, pairs) in zip(messages, moves)]

    over = REACH + 2
    tall = rows + 2 * over
    wide = pl.cdiv(cols + 2 * PAD, SPANS)
    groups = (rows + 2 * PAD) // 8
    high = tall // BANDS
    lanes_out = pl.cdiv(wide, BANDS) * LANES
    state = (2, high + 2, wide, 8, LANES)
    part = (rows // across, own, cols)
    parts = call(
        functools.partial(solve, counts),
        [part] * across,
        place,
        *got,
        directions,
        fields,
        scratch=[
            (2, PLANES + FIELDS, PAD, cols),
            (2, 2, groups, 8, LANES),
            (tall, 8, cols + 2 * LANES),
            (tall, 8, lanes_out),
            (2, high, wide, 8, LANES),
            (high, wide, 8, LANES),
            (high, wide, 8, LANES),
            state,
            state,
            state,
        ],
    )
    parts = [parts[0]] + [swap_bit(parts[k], "dir", k) for k in range(1, across)]
    total = own * across
    whole, gram = call(
        gram_of, [(rows // across, total, cols), (total, total)], place, *parts
    )
    gram = sum_all(gram)
    count = rows * cols * lax.axis_size("gx") * lax.axis_size("gy")
    *parts, upper = call(
        functools.partial(basis_of, float(count)),
        [part] * across + [(total, total)],
        place,
        gram,
        whole,
        scratch=[(total, LANES)],
    )
    parts = [parts[0]] + [swap_bit(parts[k], "dir", k) for k in range(1, across)]
    (basis,) = call(assemble, [(own, rows, cols)], place, *parts)
    return (basis, upper)


def solution(mesh):
    tile = P("gx", "gy")
    placed = (P("dir", "gx", "gy"), P(None, "gx", "gy")) + (tile,) * 5
    return jax.shard_map(
        on_device,
        mesh=mesh,
        in_specs=placed,
        out_specs=(P("dir", "gx", "gy"), P()),
        check_vma=False,
    )
```

profile of v0, /device:TPU:20, one launch (start us, length us, event | category | flops | bytes accessed | tf_op | source)
XLA Modules:
  0.0 140.4 jit_solution(5254088649251802643)
XLA Ops:
  0.6 0.6 pad_add_fusion.place
  1.2 3.4 %shard_map.86 = (f32[5,128,256]{2,1,0:T(8,128)}, f32[13,16,256]{2,1,0:T(8,128)}, f32[2,16,8,128]{3,2,1,0:T(8,128)}, f32[2,16,8,128]{3,2,1,0:T(8,128)}, f32[2,2,8...) custom-call(s32[3]{0:T(128)} %pad_add_fusion.place, f32[8,128,256]{2,1,0:T(8,128)} %refs_5_.3, f32[2,128,256]{2,1,0:T(8,128)} %refs_1_.1, ...), custom_call_target="tpu_custom_call" | custom-call | tf_op jit(solution)/shard_map/pallas_call | solution.py:418
  4.6 0.6 collective-permute-start
  5.2 0.0 collective-permute-start.1
  5.2 0.7 collective-permute-start.2
  5.9 4.0 %collective-permute-start.3 = (f32[2,2,8,128]{3,2,1,0:T(8,128)}, f32[2,2,8,128]{3,2,1,0:T(8,128)S(1)}, u32[]{:S(2)}, u32[]{:S(2)}) collective-permute-start(f32[2,2,8,128]{3,2,1,0:T(8,128)} %get-tuple-element.22), channel_id=1, source_target_pairs={{0,20},{8,28},{4,16},{12,24},{16,4},{24,12},{20,0},{28,8},{1,21},{... | collective-permute-start | bytes 49160 | tf_op jit(solution)/shard_map/ppermute | solution.py:478
  9.9 0.7 collective-permute-start.4
  10.6 1.2 collective-permute-done.3.refs_3_
  11.8 0.0 copy-start.9
  11.8 0.0 collective-permute-done.4.refs_4_
  11.8 0.0 copy-start.10
  11.8 0.0 collective-permute-done.1.refs_1_
  11.8 0.0 copy-start.7
  11.8 0.0 collective-permute-done.2.refs_2_
  11.8 0.0 copy-start.8
  11.8 0.3 collective-permute-done.refs_0_
  12.1 0.0 copy-start.6
  12.1 0.3 copy-done.9
  12.4 0.0 copy-done.10
  12.4 0.1 copy-done.7
  12.5 0.0 copy-done.8
  12.5 0.3 copy-done.6
  12.8 46.8 %shard_map.87 = (f32[32,8,256]{2,1,0:T(8,128)}, f32[32,8,256]{2,1,0:T(8,128)}, f32[32,8,256]{2,1,0:T(8,128)}, f32[32,8,256]{2,1,0:T(8,128)}) custom-call(s32[3]{0:T(128)} %pad_add_fusion.place, f32[13,16,256]{2,1,0:T(8,128)} %copy-done.6, f32[2,16,8,128]{3,2,1,0:T(8,128)} %copy-done.7, f32[2,16,8,128]{3,2,1,0:T(8,128)} %copy-done.8, ...), custom_call_target="tpu_custom_call" | custom-call | tf_op jit(solution)/shard_map/pallas_call | solution.py:418
  59.6 1.6 %collective-permute-start.5 = (f32[32,8,256]{2,1,0:T(8,128)}, f32[32,8,256]{2,1,0:T(8,128)S(1)}, u32[]{:S(2)}, u32[]{:S(2)}) collective-permute-start(f32[32,8,256]{2,1,0:T(8,128)} %get-tuple-element.26), channel_id=1, source_target_pairs={{0,1},{1,0},{2,3},{3,2},{4,5},{5,4},{6,7},{7,6},{8,9},{9,8},{10,11... | collective-permute-start | bytes 786440 | tf_op jit(solution)/shard_map/ppermute | solution.py:441
  61.2 0.3 collective-permute-start.6
  61.5 1.6 %collective-permute-start.7 = (f32[32,8,256]{2,1,0:T(8,128)}, f32[32,8,256]{2,1,0:T(8,128)S(1)}, u32[]{:S(2)}, u32[]{:S(2)}) collective-permute-start(f32[32,8,256]{2,1,0:T(8,128)} %get-tuple-element.28), channel_id=1, source_target_pairs={{0,3},{1,2},{2,1},{3,0},{4,7},{5,6},{6,5},{7,4},{8,11},{9,10},{10,... | collective-permute-start | bytes 786440 | tf_op jit(solution)/shard_map/ppermute | solution.py:441
  63.1 7.4 %collective-permute-done.5.refs_1_ = f32[32,8,256]{2,1,0:T(8,128)S(1)} collective-permute-done((f32[32,8,256]{2,1,0:T(8,128)}, f32[32,8,256]{2,1,0:T(8,128)S(1)}, u32[]{:S(2)}, u32[]{:S(2)}) %collective-permute-start.5) | collective-permute-done | bytes 262176 | tf_op jit(solution)/shard_map/ppermute | solution.py:441
  70.5 0.0 copy-start.3
  70.5 2.0 %collective-permute-done.6.refs_2_ = f32[32,8,256]{2,1,0:T(8,128)S(1)} collective-permute-done((f32[32,8,256]{2,1,0:T(8,128)}, f32[32,8,256]{2,1,0:T(8,128)S(1)}, u32[]{:S(2)}, u32[]{:S(2)}) %collective-permute-start.6) | collective-permute-done | bytes 262176 | tf_op jit(solution)/shard_map/ppermute | solution.py:441
  72.5 0.0 copy-start.4
  72.5 13.1 %collective-permute-done.7.refs_3_ = f32[32,8,256]{2,1,0:T(8,128)S(1)} collective-permute-done((f32[32,8,256]{2,1,0:T(8,128)}, f32[32,8,256]{2,1,0:T(8,128)S(1)}, u32[]{:S(2)}, u32[]{:S(2)}) %collective-permute-start.7) | collective-permute-done | bytes 262176 | tf_op jit(solution)/shard_map/ppermute | solution.py:441
  85.5 0.0 copy-start.5
  85.5 0.0 copy-done.3
  85.5 0.0 copy-done.4
  85.6 0.7 copy-done.5
  86.3 2.8 %shard_map.88 = (f32[32,32,256]{2,1,0:T(8,128)}, f32[32,32]{1,0:T(8,128)}) custom-call(s32[3]{0:T(128)} %pad_add_fusion.place, f32[32,8,256]{2,1,0:T(8,128)} %get-tuple-element.25.refs_0_, f32[32,8,256]{2,1,0:T(8,128)} %copy-done.3, f32[32,8,256]{2,1,0:T(8,128)} %copy-done.4, f32[32,8,256]{2,1,0:T(8,128)} %copy-done.5), custom_call_target="tpu_custom_call" | custom-call | tf_op jit(solution)/shard_map/pallas_call | solution.py:418
  89.1 1.6 %collective-permute-start.8 = (f32[32,32]{1,0:T(8,128)}, f32[32,32]{1,0:T(8,128)S(1)}, u32[]{:S(2)}, u32[]{:S(2)}) collective-permute-start(f32[32,32]{1,0:T(8,128)} %get-tuple-element.29), channel_id=1, source_target_pairs={{0,4},{4,0},{8,12},{12,8},{1,5},{5,1},{9,13},{13,9},{2,6},{6,2},{1... | collective-permute-start | bytes 12296 | tf_op jit(solution)/shard_map/ppermute | solution.py:441
  90.7 1.0 collective-permute-done.8
  91.8 0.7 add.15
  92.5 1.0 collective-permute-start.9
  93.5 2.8 %collective-permute-done.9 = f32[32,32]{1,0:T(8,128)S(1)} collective-permute-done((f32[32,32]{1,0:T(8,128)S(1)}, f32[32,32]{1,0:T(8,128)S(1)}, u32[]{:S(2)}, u32[]{:S(2)}) %collective-permute-start.9) | collective-permute-done | bytes 4128 | tf_op jit(solution)/shard_map/ppermute | solution.py:441
  96.2 0.5 collective-permute-start.10
  96.8 3.2 %collective-permute-done.10 = f32[32,32]{1,0:T(8,128)S(1)} collective-permute-done((f32[32,32]{1,0:T(8,128)S(1)}, f32[32,32]{1,0:T(8,128)S(1)}, u32[]{:S(2)}, u32[]{:S(2)}) %collective-permute-start.10) | collective-permute-done | bytes 4128 | tf_op jit(solution)/shard_map/ppermute | solution.py:441
  100.0 0.0 collective-permute-start.11
  100.0 3.7 %collective-permute-done.11 = f32[32,32]{1,0:T(8,128)S(1)} collective-permute-done((f32[32,32]{1,0:T(8,128)S(1)}, f32[32,32]{1,0:T(8,128)S(1)}, u32[]{:S(2)}, u32[]{:S(2)}) %collective-permute-start.11) | collective-permute-done | bytes 4128 | tf_op jit(solution)/shard_map/ppermute | solution.py:441
  103.7 0.0 collective-permute-start.12
  103.7 4.6 %collective-permute-done.12 = f32[32,32]{1,0:T(8,128)S(1)} collective-permute-done((f32[32,32]{1,0:T(8,128)S(1)}, f32[32,32]{1,0:T(8,128)S(1)}, u32[]{:S(2)}, u32[]{:S(2)}) %collective-permute-start.12) | collective-permute-done | bytes 4128 | tf_op jit(solution)/shard_map/ppermute | solution.py:441
  108.4 0.6 add.19.gram_ref
  109.0 6.0 %shard_map.89 = (f32[32,8,256]{2,1,0:T(8,128)}, f32[32,8,256]{2,1,0:T(8,128)}, f32[32,8,256]{2,1,0:T(8,128)}, f32[32,8,256]{2,1,0:T(8,128)}, f32[32,32]{1,0:T(8,128)}) custom-call(s32[3]{0:T(128)} %pad_add_fusion.place, f32[32,32]{1,0:T(8,128)} %add.19.gram_ref, f32[32,32,256]{2,1,0:T(8,128)} %get-tuple-element.30.whole), custom_call_target="tpu_custom_call" | custom-call | tf_op jit(solution)/shard_map/pallas_call | solution.py:418
  115.0 0.0 collective-permute-start.13
  115.0 1.9 %collective-permute-start.14 = (f32[32,8,256]{2,1,0:T(8,128)}, f32[32,8,256]{2,1,0:T(8,128)S(1)}, u32[]{:S(2)}, u32[]{:S(2)}) collective-permute-start(f32[32,8,256]{2,1,0:T(8,128)} %get-tuple-element.33), channel_id=1, source_target_pairs={{0,2},{1,3},{2,0},{3,1},{4,6},{5,7},{6,4},{7,5},{8,10},{9,11},{10,... | collective-permute-start | bytes 786440 | tf_op jit(solution)/shard_map/ppermute | solution.py:441
  116.9 1.6 %collective-permute-start.15 = (f32[32,8,256]{2,1,0:T(8,128)}, f32[32,8,256]{2,1,0:T(8,128)S(1)}, u32[]{:S(2)}, u32[]{:S(2)}) collective-permute-start(f32[32,8,256]{2,1,0:T(8,128)} %get-tuple-element.34), channel_id=1, source_target_pairs={{0,3},{1,2},{2,1},{3,0},{4,7},{5,6},{6,5},{7,4},{8,11},{9,10},{10,... | collective-permute-start | bytes 786440 | tf_op jit(solution)/shard_map/ppermute | solution.py:441
  118.5 6.0 %collective-permute-done.13.refs_1_ = f32[32,8,256]{2,1,0:T(8,128)S(1)} collective-permute-done((f32[32,8,256]{2,1,0:T(8,128)}, f32[32,8,256]{2,1,0:T(8,128)S(1)}, u32[]{:S(2)}, u32[]{:S(2)}) %collective-permute-start.13) | collective-permute-done | bytes 262176 | tf_op jit(solution)/shard_map/ppermute | solution.py:441
  124.5 0.0 copy-start
  124.5 8.1 %collective-permute-done.14.refs_2_ = f32[32,8,256]{2,1,0:T(8,128)S(1)} collective-permute-done((f32[32,8,256]{2,1,0:T(8,128)}, f32[32,8,256]{2,1,0:T(8,128)S(1)}, u32[]{:S(2)}, u32[]{:S(2)}) %collective-permute-start.14) | collective-permute-done | bytes 262176 | tf_op jit(solution)/shard_map/ppermute | solution.py:441
  132.5 0.0 copy-start.1
  132.5 4.8 %collective-permute-done.15.refs_3_ = f32[32,8,256]{2,1,0:T(8,128)S(1)} collective-permute-done((f32[32,8,256]{2,1,0:T(8,128)}, f32[32,8,256]{2,1,0:T(8,128)S(1)}, u32[]{:S(2)}, u32[]{:S(2)}) %collective-permute-start.15) | collective-permute-done | bytes 262176 | tf_op jit(solution)/shard_map/ppermute | solution.py:441
  137.3 0.0 copy-start.2
  137.3 0.0 copy-done
  137.3 0.0 copy-done.1
  137.3 0.7 copy-done.2
  138.0 2.4 %shard_map.90 = f32[8,128,256]{2,1,0:T(8,128)} custom-call(s32[3]{0:T(128)} %pad_add_fusion.place, f32[32,8,256]{2,1,0:T(8,128)} %get-tuple-element.31.refs_0_, f32[32,8,256]{2,1,0:T(8,128)} %copy-done, f32[32,8,256]{2,1,0:T(8,128)} %copy-done.1, f32[32,8,256]{2,1,0:T(8,128)} %copy-done.2), custom_call_target="tpu_custom_call" | custom-call | tf_op jit(solution)/shard_map/pallas_call | solution.py:418
  (3 shorter events, 0.0 us)
Async XLA Ops:
  4.6 7.4 %collective-permute-start = (f32[13,16,256]{2,1,0:T(8,128)}, f32[13,16,256]{2,1,0:T(8,128)S(1)}, u32[]{:S(2)}, u32[]{:S(2)}) collective-permute-start(f32[13,16,256]{2,1,0:T(8,128)} %get-tuple-element.19), channel_id=1, source_target_pairs={{0,16},{16,0},{1,17},{17,1},{2,18},{18,2},{3,19},{19,3},{4,20},{20... | collective-permute-start | bytes 638984 | tf_op jit(solution)/shard_map/ppermute | solution.py:478
  5.2 6.6 %collective-permute-start.1 = (f32[2,16,8,128]{3,2,1,0:T(8,128)}, f32[2,16,8,128]{3,2,1,0:T(8,128)S(1)}, u32[]{:S(2)}, u32[]{:S(2)}) collective-permute-start(f32[2,16,8,128]{3,2,1,0:T(8,128)} %get-tuple-element.20), channel_id=1, source_target_pairs={{0,4},{8,12},{4,0},{12,8},{1,5},{9,13},{5,1},{13,9},{2,6},{10,14},... | collective-permute-start | bytes 393224 | tf_op jit(solution)/shard_map/ppermute | solution.py:478
  5.2 6.6 %collective-permute-start.2 = (f32[2,16,8,128]{3,2,1,0:T(8,128)}, f32[2,16,8,128]{3,2,1,0:T(8,128)S(1)}, u32[]{:S(2)}, u32[]{:S(2)}) collective-permute-start(f32[2,16,8,128]{3,2,1,0:T(8,128)} %get-tuple-element.21), channel_id=1, source_target_pairs={{4,8},{8,4},{5,9},{9,5},{6,10},{10,6},{7,11},{11,7},{20,24},{24,20... | collective-permute-start | bytes 393224 | tf_op jit(solution)/shard_map/ppermute | solution.py:478
  5.9 5.9 %collective-permute-start.3 = (f32[2,2,8,128]{3,2,1,0:T(8,128)}, f32[2,2,8,128]{3,2,1,0:T(8,128)S(1)}, u32[]{:S(2)}, u32[]{:S(2)}) collective-permute-start(f32[2,2,8,128]{3,2,1,0:T(8,128)} %get-tuple-element.22), channel_id=1, source_target_pairs={{0,20},{8,28},{4,16},{12,24},{16,4},{24,12},{20,0},{28,8},{1,21},{... | collective-permute-start | bytes 49160 | tf_op jit(solution)/shard_map/ppermute | solution.py:478
  9.9 1.9 %collective-permute-start.4 = (f32[2,2,8,128]{3,2,1,0:T(8,128)}, f32[2,2,8,128]{3,2,1,0:T(8,128)S(1)}, u32[]{:S(2)}, u32[]{:S(2)}) collective-permute-start(f32[2,2,8,128]{3,2,1,0:T(8,128)} %get-tuple-element.23), channel_id=1, source_target_pairs={{4,24},{8,20},{20,8},{24,4},{5,25},{9,21},{21,9},{25,5},{6,26},{10... | collective-permute-start | bytes 49160 | tf_op jit(solution)/shard_map/ppermute | solution.py:478
  11.8 0.6 copy-start.9
  11.8 0.6 copy-start.10
  11.8 0.7 copy-start.7
  11.8 0.7 copy-start.8
  12.1 0.7 copy-start.6
  59.6 10.9 %collective-permute-start.5 = (f32[32,8,256]{2,1,0:T(8,128)}, f32[32,8,256]{2,1,0:T(8,128)S(1)}, u32[]{:S(2)}, u32[]{:S(2)}) collective-permute-start(f32[32,8,256]{2,1,0:T(8,128)} %get-tuple-element.26), channel_id=1, source_target_pairs={{0,1},{1,0},{2,3},{3,2},{4,5},{5,4},{6,7},{7,6},{8,9},{9,8},{10,11... | collective-permute-start | bytes 786440 | tf_op jit(solution)/shard_map/ppermute | solution.py:441
  61.2 11.3 %collective-permute-start.6 = (f32[32,8,256]{2,1,0:T(8,128)}, f32[32,8,256]{2,1,0:T(8,128)S(1)}, u32[]{:S(2)}, u32[]{:S(2)}) collective-permute-start(f32[32,8,256]{2,1,0:T(8,128)} %get-tuple-element.27), channel_id=1, source_target_pairs={{0,2},{1,3},{2,0},{3,1},{4,6},{5,7},{6,4},{7,5},{8,10},{9,11},{10,... | collective-permute-start | bytes 786440 | tf_op jit(solution)/shard_map/ppermute | solution.py:441
  61.5 24.0 %collective-permute-start.7 = (f32[32,8,256]{2,1,0:T(8,128)}, f32[32,8,256]{2,1,0:T(8,128)S(1)}, u32[]{:S(2)}, u32[]{:S(2)}) collective-permute-start(f32[32,8,256]{2,1,0:T(8,128)} %get-tuple-element.28), channel_id=1, source_target_pairs={{0,3},{1,2},{2,1},{3,0},{4,7},{5,6},{6,5},{7,4},{8,11},{9,10},{10,... | collective-permute-start | bytes 786440 | tf_op jit(solution)/shard_map/ppermute | solution.py:441
  70.5 15.1 %copy-start.3 = (f32[32,8,256]{2,1,0:T(8,128)}, f32[32,8,256]{2,1,0:T(8,128)S(1)}, u32[]{:S(2)}) copy-start(f32[32,8,256]{2,1,0:T(8,128)S(1)} %collective-permute-done.5.refs_1_) | copy-start | bytes 786436
  72.5 13.1 %copy-start.4 = (f32[32,8,256]{2,1,0:T(8,128)}, f32[32,8,256]{2,1,0:T(8,128)S(1)}, u32[]{:S(2)}) copy-start(f32[32,8,256]{2,1,0:T(8,128)S(1)} %collective-permute-done.6.refs_2_) | copy-start | bytes 786436
  85.5 0.7 copy-start.5
  89.1 2.7 %collective-permute-start.8 = (f32[32,32]{1,0:T(8,128)}, f32[32,32]{1,0:T(8,128)S(1)}, u32[]{:S(2)}, u32[]{:S(2)}) collective-permute-start(f32[32,32]{1,0:T(8,128)} %get-tuple-element.29), channel_id=1, source_target_pairs={{0,4},{4,0},{8,12},{12,8},{1,5},{5,1},{9,13},{13,9},{2,6},{6,2},{1... | collective-permute-start | bytes 12296 | tf_op jit(solution)/shard_map/ppermute | solution.py:441
  92.5 3.7 %collective-permute-start.9 = (f32[32,32]{1,0:T(8,128)S(1)}, f32[32,32]{1,0:T(8,128)S(1)}, u32[]{:S(2)}, u32[]{:S(2)}) collective-permute-start(f32[32,32]{1,0:T(8,128)S(1)} %add.15), channel_id=1, source_target_pairs={{0,8},{4,12},{8,0},{12,4},{1,9},{5,13},{9,1},{13,5},{2,10},{6,14},... | collective-permute-start | bytes 12296 | tf_op jit(solution)/shard_map/ppermute | solution.py:441
  96.2 3.7 %collective-permute-start.10 = (f32[32,32]{1,0:T(8,128)S(1)}, f32[32,32]{1,0:T(8,128)S(1)}, u32[]{:S(2)}, u32[]{:S(2)}) collective-permute-start(f32[32,32]{1,0:T(8,128)S(1)} %add.16), channel_id=1, source_target_pairs={{0,16},{16,0},{1,17},{17,1},{2,18},{18,2},{3,19},{19,3},{4,20},{20... | collective-permute-start | bytes 12296 | tf_op jit(solution)/shard_map/ppermute | solution.py:441
  100.0 3.7 %collective-permute-start.11 = (f32[32,32]{1,0:T(8,128)S(1)}, f32[32,32]{1,0:T(8,128)S(1)}, u32[]{:S(2)}, u32[]{:S(2)}) collective-permute-start(f32[32,32]{1,0:T(8,128)S(1)} %add.17), channel_id=1, source_target_pairs={{0,1},{1,0},{2,3},{3,2},{4,5},{5,4},{6,7},{7,6},{8,9},{9,8},{10,11... | collective-permute-start | bytes 12296 | tf_op jit(solution)/shard_map/ppermute | solution.py:441
  103.7 4.6 %collective-permute-start.12 = (f32[32,32]{1,0:T(8,128)S(1)}, f32[32,32]{1,0:T(8,128)S(1)}, u32[]{:S(2)}, u32[]{:S(2)}) collective-permute-start(f32[32,32]{1,0:T(8,128)S(1)} %add.18), channel_id=1, source_target_pairs={{0,2},{1,3},{2,0},{3,1},{4,6},{5,7},{6,4},{7,5},{8,10},{9,11},{10,... | collective-permute-start | bytes 12296 | tf_op jit(solution)/shard_map/ppermute | solution.py:441
  115.0 9.5 %collective-permute-start.13 = (f32[32,8,256]{2,1,0:T(8,128)}, f32[32,8,256]{2,1,0:T(8,128)S(1)}, u32[]{:S(2)}, u32[]{:S(2)}) collective-permute-start(f32[32,8,256]{2,1,0:T(8,128)} %get-tuple-element.32), channel_id=1, source_target_pairs={{0,1},{1,0},{2,3},{3,2},{4,5},{5,4},{6,7},{7,6},{8,9},{9,8},{10,11... | collective-permute-start | bytes 786440 | tf_op jit(solution)/shard_map/ppermute | solution.py:441
  115.0 17.5 %collective-permute-start.14 = (f32[32,8,256]{2,1,0:T(8,128)}, f32[32,8,256]{2,1,0:T(8,128)S(1)}, u32[]{:S(2)}, u32[]{:S(2)}) collective-permute-start(f32[32,8,256]{2,1,0:T(8,128)} %get-tuple-element.33), channel_id=1, source_target_pairs={{0,2},{1,3},{2,0},{3,1},{4,6},{5,7},{6,4},{7,5},{8,10},{9,11},{10,... | collective-permute-start | bytes 786440 | tf_op jit(solution)/shard_map/ppermute | solution.py:441
  116.9 20.4 %collective-permute-start.15 = (f32[32,8,256]{2,1,0:T(8,128)}, f32[32,8,256]{2,1,0:T(8,128)S(1)}, u32[]{:S(2)}, u32[]{:S(2)}) collective-permute-start(f32[32,8,256]{2,1,0:T(8,128)} %get-tuple-element.34), channel_id=1, source_target_pairs={{0,3},{1,2},{2,1},{3,0},{4,7},{5,6},{6,5},{7,4},{8,11},{9,10},{10,... | collective-permute-start | bytes 786440 | tf_op jit(solution)/shard_map/ppermute | solution.py:441
  124.5 12.8 %copy-start = (f32[32,8,256]{2,1,0:T(8,128)}, f32[32,8,256]{2,1,0:T(8,128)S(1)}, u32[]{:S(2)}) copy-start(f32[32,8,256]{2,1,0:T(8,128)S(1)} %collective-permute-done.13.refs_1_) | copy-start | bytes 786436
  132.5 4.8 %copy-start.1 = (f32[32,8,256]{2,1,0:T(8,128)}, f32[32,8,256]{2,1,0:T(8,128)S(1)}, u32[]{:S(2)}) copy-start(f32[32,8,256]{2,1,0:T(8,128)S(1)} %collective-permute-done.14.refs_2_) | copy-start | bytes 786436
  137.3 0.7 copy-start.2
where the time goes:
time: 141 us; the launch traced here: 140 us
  Pallas kernels  61.5 us (44%)
  waiting for transfers between devices  58.1 us (41%)
  starting transfers between devices  16 us (11%)
  local copies, waits for them, and re-layouts  2.12 us (2%)
  other arithmetic  1.9 us (1%)
    pallas_call x5, Pallas kernels, call(): pl.pallas_call(kernel, out_shape=shapes, in_specs=[smem] + [pl.BlockSpec(...  61.5 us
    ppermute x11, waiting for transfers between devices, swap_bit(): return lax.ppermute(value, axis, [(i, i ^ bit) for i in range(count)])  56.7 us
    ppermute x11, starting transfers between devices, swap_bit(): return lax.ppermute(value, axis, [(i, i ^ bit) for i in range(count)])  10.1 us
    ppermute x5, starting transfers between devices, on_device(): lax.ppermute(m, axis, pairs)  5.92 us
  transfers between devices with their start and end apart: 16, of which 13 were waited for; matrix products, arithmetic and copies ran while one was open for 0% of the time, Pallas kernels for 0%

commit v1 on v0

--- a/solution.py
+++ b/solution.py
@@ -2,6 +2,7 @@
 
 import jax
 import jax.numpy as jnp
+import numpy as np
 from jax import lax
 from jax.experimental import pallas as pl
 from jax.experimental.pallas import tpu as pltpu
@@ -10,6 +11,7 @@
 SWEEPS = 6
 damping = 0.8
 KEEP_BACK = 1.0 - damping
+GROWN, SHRUNK = 1.0 + KEEP_BACK, 1.0 - KEEP_BACK
 REACH = 2 * (SWEEPS - 1)
 PAD = 16
 LANES = 128
@@ -21,6 +23,8 @@
 BF16 = jnp.bfloat16
 AXES = ("gx", "gy", "dir")
 WEIGHTS = ((4.0, 1.0), (1.0, 4.0))
+PARTS = 2
+UNROLL = 3
 
 
 def iota(shape, dim):
@@ -85,26 +89,52 @@
             corner_out[i * count_y + j][...] = col_out[j][:, base]
 
 
-def exchange_blocks(tiles):
-    lane = iota((8, LANES), 1)
-    for bit, width in ((1, SPANS), (2, 2 * SPANS)):
-        low = (lane // width) % 2 == 0
-        tiles = [
-            jnp.where(low, tiles[a], roll(tiles[a ^ bit], width))
-            if a & bit == 0
-            else jnp.where(low, roll(tiles[a ^ bit], -width), tiles[a])
-            for a in range(4)
-        ]
-    return tiles
-
-
-def split_dot(value, places):
+def from_bands(tiles):
+    block = iota((8, LANES), 1) // SPANS
+    out = []
+    for column in range(BANDS):
+        value = tiles[0]
+        for band in range(1, BANDS):
+            value = jnp.where(block == (column + band) % BANDS, tiles[band], value)
+        out.append(roll(value, -SPANS * column) if column else value)
+    return out
+
+
+def to_bands(tiles):
+    block = iota((8, LANES), 1) // SPANS
+    turned = [roll(tile, SPANS * column) if column else tile for column, tile in enumerate(tiles)]
+    out = []
+    for band in range(BANDS):
+        value = turned[0]
+        for column in range(1, BANDS):
+            value = jnp.where(block == (column + band) % BANDS, turned[column], value)
+        out.append(value)
+    return out
+
+
+def band_places(cols, wide):
+    slot = np.arange(LANES) % PAD
+    column = np.concatenate([np.arange(cols) + PAD, slot, slot + cols + PAD])
+    span, j = column // wide, column % wide
+    out = np.zeros((BANDS, column.size, pl.cdiv(wide, BANDS) * LANES), np.float32)
+    for band in range(BANDS):
+        lane = LANES * (j // BANDS) + SPANS * ((j + band) % BANDS) + span
+        out[band, np.arange(column.size), lane] = 1.0
+    return out.astype(BF16)
+
+
+def split_dot(value, places, transposed=False):
     total = None
-    for step in range(3):
+    for step in range(PARTS):
         part = value.astype(BF16)
-        product = jnp.dot(part, places, preferred_element_type=F32)
+        product = lax.dot_general(
+            part,
+            places,
+            (((1,), (1 if transposed else 0,)), ((), ())),
+            preferred_element_type=F32,
+        )
         total = product if total is None else total + product
-        if step < 2:
+        if step < PARTS - 1:
             value = value - part.astype(F32)
     return total
 
@@ -114,7 +144,7 @@
     got_rows, refs = refs[:count_x], refs[count_x:]
     got_cols, refs = refs[:count_y], refs[count_y:]
     got_corners, refs = refs[: count_x * count_y], refs[count_x * count_y :]
-    dirs, fields, *refs = refs
+    dirs, fields, places, *refs = refs
     *outs, halo_rows, halo_cols, lined, turned, planes, coeffs, extras, base, ping, pong = refs
     rows, cols = dirs.shape[1:]
     tall = lined.shape[0]
@@ -149,19 +179,17 @@
             halo_cols[side, q, :edge] = above
             halo_cols[side, q, groups - edge :] = below
 
-    def spread(shape, source, target):
-        k, n = iota(shape, source), iota(shape, target)
-        inner = k < cols
-        slot = (k - cols) % PAD + jnp.where(k < cols + LANES, 0, cols + PAD)
-        at = jnp.where(inner, k + PAD, slot)
-        return jnp.where(
-            (at == wide * (n % SPANS) + n // SPANS) & (n < wide * SPANS), 1.0, 0.0
-        ).astype(BF16)
-
     lanes_out = turned.shape[2]
-    places = spread((cols + 2 * LANES, lanes_out), 0, 1)
     lane = iota((8, LANES), 1)
     own_slot = lane // PAD == iota((8, LANES), 0)
+
+    def over_pairs(body):
+        def two(i, _):
+            body(2 * i)
+            body(2 * i + 1)
+            return 0
+
+        lax.fori_loop(0, high // 2, two, 0)
 
     for q, (source, first, count) in enumerate(((dirs, 0, PLANES), (fields, PLANES, FIELDS))):
         for g in range(groups):
@@ -188,27 +216,28 @@
 
         def turn(b, _):
             value = lined[pl.ds(high * b, high)].reshape(high * 8, cols + 2 * LANES)
-            turned[pl.ds(high * b, high)] = split_dot(value, places).reshape(
+            turned[pl.ds(high * b, high)] = split_dot(value, places[b]).reshape(
                 high, 8, lanes_out
             )
             return 0
 
         lax.fori_loop(0, BANDS, turn, 0)
 
-        def band(i, _):
+        def band(i):
             for t in range(lanes_out // LANES):
                 tiles = [
                     turned[high * b + i, :, LANES * t : LANES * t + LANES] for b in range(BANDS)
                 ]
-                tiles = exchange_blocks(tiles)
-                for a in range(BANDS):
-                    if BANDS * t + a < wide:
-                        planes[q, i, BANDS * t + a] = tiles[a]
-            return 0
-
-        lax.fori_loop(0, high, band, 0)
+                for j, tile in enumerate(from_bands(tiles)[: wide - BANDS * t], BANDS * t):
+                    planes[q, i, j] = tile
+
+        over_pairs(band)
 
     row_of = iota((8, LANES), 0)
+    kind = row_of % 4
+    ax = jnp.where(row_of < 4, WEIGHTS[0][0], WEIGHTS[1][0])
+    ay = jnp.where(row_of < 4, WEIGHTS[0][1], WEIGHTS[1][1])
+    along = jnp.where(kind < 2, ax, ay)
 
     def weigh(i, above, below, turn_above, turn_below):
         def field(k, row, j):
@@ -227,20 +256,22 @@
             along_x, along_y = east + west, north + south
             friction, kept = field(2, i, j), field(4, i, j)
 
-            def step(is_first):
-                ax = jnp.where(is_first, WEIGHTS[0][0], WEIGHTS[1][0])
-                ay = jnp.where(is_first, WEIGHTS[0][1], WEIGHTS[1][1])
-                diagonal = ax * along_x + ay * along_y + friction
-                return ax, ay, jnp.where(kept != 0.0, damping / diagonal, 0.0)
-
-            ax, ay, gain = step(row_of < 4)
-            kind = row_of % 4
-            face = jnp.where(kind < 2, jnp.where(kind == 0, east, west), jnp.where(kind == 2, north, south))
-            coeffs[i, j] = gain * jnp.where(kind < 2, ax, ay) * face
-            _, _, gain = step(row_of % 2 == 0)
-            pull = -jnp.where(row_of % 2 == 0, field(0, i, j), field(1, i, j))
+            diagonal = ax * along_x + ay * along_y + friction
+            gain = jnp.where(kept != 0.0, damping / diagonal, 0.0)
+            face = jnp.where(
+                kind < 2,
+                jnp.where(kind == 0, east, west),
+                jnp.where(kind == 2, north, south),
+            )
+            weight = gain * along * face
+            coeffs[0, i, j] = weight * (1.0 / GROWN)
+            coeffs[1, i, j] = weight * (1.0 / KEEP_BACK)
+            coeffs[2, i, j] = weight * (-1.0 / SHRUNK)
+            pull = jnp.where(row_of < 4, field(0, i, j), field(1, i, j))
             extras[i, j] = jnp.where(
-                row_of < 4, gain * jnp.where(row_of < 2, pull, kept), pull
+                kind == 1,
+                GROWN * gain * kept,
+                jnp.where(kind == 0, gain, GROWN) * -pull,
             )
 
     weigh(0, high - 1, 1, True, False)
@@ -264,83 +295,89 @@
         body(0)
         body(high - 1)
 
-        def two(i, _):
-            body(2 * i + 1)
-            body(2 * i + 2)
+        def some(i, _):
+            for d in range(UNROLL):
+                body(UNROLL * i + d + 1)
             return 0
 
-        lax.fori_loop(0, (high - 2) // 2, two, 0)
+        full = (high - 2) // UNROLL
+        lax.fori_loop(0, full, some, 0)
+        for i in range(1 + UNROLL * full, high - 1):
+            body(i)
+
+    def extra(kind, m, i, j):
+        return extras[i, j, 4 * m + kind : 4 * m + kind + 1, :]
 
     def start(i):
         for j in range(wide):
             for m in range(2):
-                put(base, m, i, j, extras[i, j, m : m + 1, :] * planes[0, i, j])
+                put(base, m, i, j, extra(0, m, i, j) * planes[0, i, j])
 
     over_rows(start)
 
-    def sweep(source, store):
+    def sweep(source, scale, store):
         def body(i):
             for m in range(2):
                 mids = [source[m, i + 1, j] for j in range(wide)]
                 before = [roll(mids[-1], 1)] + mids[:-1]
                 after = mids[1:] + [roll(mids[0], -1)]
                 for j in range(wide):
-                    e, w, n, s = (coeffs[i, j, 4 * m + d : 4 * m + d + 1, :] for d in range(4))
-                    store(
-                        m,
-                        i,
-                        j,
-                        (base[m, i + 1, j] + KEEP_BACK * mids[j])
-                        + (e * source[m, i + 2, j] + w * source[m, i, j])
-                        + (n * after[j] + s * before[j]),
+                    e, w, n, s = (
+                        coeffs[scale, i, j, 4 * m + d : 4 * m + d + 1, :] for d in range(4)
                     )
+                    along_x = e * source[m, i + 2, j] + w * source[m, i, j]
+                    along_y = n * after[j] + s * before[j]
+                    store(m, i, j, mids[j] + (along_x + along_y))
 
         over_rows(body)
 
     def to(ref):
         return lambda m, i, j, value: put(ref, m, i, j, value)
 
+    def solve_from(one, two, three, store):
+        sweep(one, 0, to(two))
+        sweep(two, 1, to(three))
+
+        def add(m, i, j, value):
+            put(one, m, i, j, two[m, i + 1, j] + (KEEP_BACK * GROWN) * value)
+
+        sweep(three, 0, add)
+        sweep(one, 1, to(three))
+
+        def last(m, i, j, value):
+            store(m, i, j, one[m, i + 1, j] - (KEEP_BACK * SHRUNK) * value)
+
+        sweep(three, 2, last)
+
     def to_adjoint(m, i, j, value):
-        pong[m, i + 1, j] = extras[i, j, 2 + m : 3 + m, :] * value
+        put(ping, m, i, j, extra(1, m, i, j) * value)
 
     def to_sketch(m, i, j, value):
-        value = extras[i, j, 4 + m : 5 + m, :] * value
+        value = extra(2, m, i, j) * value
         planes[0, i, j] = value if m == 0 else planes[0, i, j] + value
 
-    for part in range(2):
-        source = base
-        for step in range(SWEEPS - 2):
-            target = ping if source is not ping else pong
-            sweep(source, to(target))
-            source = target
-        if part == 0:
-            target = ping if source is not ping else pong
-
-            def adjoint(m, i, j, value, target=target):
-                put(target, m, i, j, extras[i, j, 2 + m : 3 + m, :] * value)
-
-            sweep(source, adjoint)
-            base, ping, pong = target, base, source
-        else:
-            sweep(source, to_sketch)
-
-    def unband(i, _):
+    solve_from(base, ping, pong, to_adjoint)
+    solve_from(ping, base, pong, to_sketch)
+
+    def unband(i):
         for t in range(lanes_out // LANES):
-            tiles = [
-                planes[0, i, BANDS * t + a] if BANDS * t + a < wide else jnp.zeros((8, LANES), F32)
-                for a in range(BANDS)
-            ]
-            tiles = exchange_blocks(tiles)
-            for b in range(BANDS):
-                turned[high * b + i, :, LANES * t : LANES * t + LANES] = tiles[b]
+            tiles = [planes[0, i, j] for j in range(BANDS * t, min(BANDS * t + BANDS, wide))]
+            tiles += [jnp.zeros((8, LANES), F32)] * (BANDS - len(tiles))
+            for b, tile in enumerate(to_bands(tiles)):
+                turned[high * b + i, :, LANES * t : LANES * t + LANES] = tile
+
+    over_pairs(unband)
+
+    def unturn(b, _):
+        value = turned[pl.ds(high * b, high)].reshape(high * 8, lanes_out)
+        value = split_dot(value, places[b, :cols, :], transposed=True)
+        lined[pl.ds(high * b, high), :, :cols] = value.reshape(high, 8, cols)
         return 0
 
-    lax.fori_loop(0, high, unband, 0)
-    places = spread((lanes_out, cols), 1, 0)
+    lax.fori_loop(0, BANDS, unturn, 0)
     part = rows // len(outs)
     for k, out in enumerate(outs):
-        value = turned[pl.ds(over + part * (place[2] ^ k), part)].reshape(part * 8, lanes_out)
-        out[...] = split_dot(value, places).reshape(part, 8, cols)
+        out[...] = lined[pl.ds(over + part * (place[2] ^ k), part), :, :cols]
 
 
 def gram_of(place, *refs):
@@ -492,13 +529,14 @@
         *got,
         directions,
         fields,
+        band_places(cols, wide),
         scratch=[
             (2, PLANES + FIELDS, PAD, cols),
             (2, 2, groups, 8, LANES),
             (tall, 8, cols + 2 * LANES),
             (tall, 8, lanes_out),
             (2, high, wide, 8, LANES),
-            (high, wide, 8, LANES),
+            (3, high, wide, 8, LANES),
             (high, wide, 8, LANES),
             state,
             state,

time: 141 us -> 127 us (0.901)
  Pallas kernels: 61.5 us -> 47.4 us
    pallas_call x5, Pallas kernels: 61.5 us -> 47.4 us  [call(): pl.pallas_call(kernel, out_shape=shapes, in_specs=[smem] + [pl.BlockSpec(...]
where the time goes in v1:
time: 127 us; the launch traced here: 126 us
  waiting for transfers between devices  58.2 us (46%)
  Pallas kernels  47.4 us (37%)
  starting transfers between devices  16 us (13%)
  local copies, waits for them, and re-layouts  2.12 us (2%)
  other arithmetic  1.9 us (1%)
    ppermute x11, waiting for transfers between devices, swap_bit(): return lax.ppermute(value, axis, [(i, i ^ bit) for i in range(count)])  56.7 us
    pallas_call x5, Pallas kernels, call(): pl.pallas_call(kernel, out_shape=shapes, in_specs=[smem] + [pl.BlockSpec(...  47.4 us
    ppermute x11, starting transfers between devices, swap_bit(): return lax.ppermute(value, axis, [(i, i ^ bit) for i in range(count)])  10.1 us
    ppermute x5, starting transfers between devices, on_device(): lax.ppermute(m, axis, pairs)  5.92 us
  transfers between devices with their start and end apart: 16, of which 13 were waited for; matrix products, arithmetic and copies ran while one was open for 0% of the time, Pallas kernels for 0%

profile of v1, /device:TPU:20, one launch (start us, length us, event | category | flops | bytes accessed | tf_op | source)
XLA Modules:
  0.0 126.3 jit_solution(15371327808766258104)
XLA Ops:
  0.6 0.6 pad_add_fusion.place
  1.2 3.4 %shard_map.95 = (f32[5,128,256]{2,1,0:T(8,128)}, f32[13,16,256]{2,1,0:T(8,128)}, f32[2,16,8,128]{3,2,1,0:T(8,128)}, f32[2,16,8,128]{3,2,1,0:T(8,128)}, f32[2,2,8...) custom-call(s32[3]{0:T(128)} %pad_add_fusion.place, f32[8,128,256]{2,1,0:T(8,128)} %refs_5_.3, f32[2,128,256]{2,1,0:T(8,128)} %refs_1_.1, ...), custom_call_target="tpu_custom_call" | custom-call | tf_op jit(solution)/shard_map/pallas_call | solution.py:455
  4.6 0.6 collective-permute-start
  5.2 0.0 collective-permute-start.1
  5.2 0.7 collective-permute-start.2
  5.9 4.0 %collective-permute-start.3 = (f32[2,2,8,128]{3,2,1,0:T(8,128)}, f32[2,2,8,128]{3,2,1,0:T(8,128)S(1)}, u32[]{:S(2)}, u32[]{:S(2)}) collective-permute-start(f32[2,2,8,128]{3,2,1,0:T(8,128)} %get-tuple-element.22), channel_id=1, source_target_pairs={{0,20},{8,28},{4,16},{12,24},{16,4},{24,12},{20,0},{28,8},{1,21},{... | collective-permute-start | bytes 49160 | tf_op jit(solution)/shard_map/ppermute | solution.py:515
  9.9 0.7 collective-permute-start.4
  10.6 1.2 collective-permute-done.3.refs_3_
  11.8 0.0 copy-start.9
  11.8 0.0 collective-permute-done.4.refs_4_
  11.8 0.0 copy-start.10
  11.8 0.0 collective-permute-done.1.refs_1_
  11.8 0.0 copy-start.7
  11.8 0.0 collective-permute-done.2.refs_2_
  11.8 0.0 copy-start.8
  11.8 0.3 collective-permute-done.refs_0_
  12.1 0.0 copy-start.6
  12.1 0.3 copy-done.9
  12.4 0.0 copy-done.10
  12.4 0.1 copy-done.7
  12.5 0.0 copy-done.8
  12.5 0.3 copy-done.6
  12.8 32.7 %shard_map.96 = (f32[32,8,256]{2,1,0:T(8,128)}, f32[32,8,256]{2,1,0:T(8,128)}, f32[32,8,256]{2,1,0:T(8,128)}, f32[32,8,256]{2,1,0:T(8,128)}) custom-call(s32[3]{0:T(128)} %pad_add_fusion.place, f32[13,16,256]{2,1,0:T(8,128)} %copy-done.6, f32[2,16,8,128]{3,2,1,0:T(8,128)} %copy-done.7, f32[2,16,8,128]{3,2,1,0:T(8,128)} %copy-done.8, ...), custom_call_target="tpu_custom_call" | custom-call | tf_op jit(solution)/shard_map/pallas_call | solution.py:455
  45.5 1.6 %collective-permute-start.5 = (f32[32,8,256]{2,1,0:T(8,128)}, f32[32,8,256]{2,1,0:T(8,128)S(1)}, u32[]{:S(2)}, u32[]{:S(2)}) collective-permute-start(f32[32,8,256]{2,1,0:T(8,128)} %get-tuple-element.26), channel_id=1, source_target_pairs={{0,1},{1,0},{2,3},{3,2},{4,5},{5,4},{6,7},{7,6},{8,9},{9,8},{10,11... | collective-permute-start | bytes 786440 | tf_op jit(solution)/shard_map/ppermute | solution.py:478
  47.1 0.3 collective-permute-start.6
  47.4 1.6 %collective-permute-start.7 = (f32[32,8,256]{2,1,0:T(8,128)}, f32[32,8,256]{2,1,0:T(8,128)S(1)}, u32[]{:S(2)}, u32[]{:S(2)}) collective-permute-start(f32[32,8,256]{2,1,0:T(8,128)} %get-tuple-element.28), channel_id=1, source_target_pairs={{0,3},{1,2},{2,1},{3,0},{4,7},{5,6},{6,5},{7,4},{8,11},{9,10},{10,... | collective-permute-start | bytes 786440 | tf_op jit(solution)/shard_map/ppermute | solution.py:478
  49.0 7.4 %collective-permute-done.5.refs_1_ = f32[32,8,256]{2,1,0:T(8,128)S(1)} collective-permute-done((f32[32,8,256]{2,1,0:T(8,128)}, f32[32,8,256]{2,1,0:T(8,128)S(1)}, u32[]{:S(2)}, u32[]{:S(2)}) %collective-permute-start.5) | collective-permute-done | bytes 262176 | tf_op jit(solution)/shard_map/ppermute | solution.py:478
  56.4 0.0 copy-start.3
  56.4 2.0 %collective-permute-done.6.refs_2_ = f32[32,8,256]{2,1,0:T(8,128)S(1)} collective-permute-done((f32[32,8,256]{2,1,0:T(8,128)}, f32[32,8,256]{2,1,0:T(8,128)S(1)}, u32[]{:S(2)}, u32[]{:S(2)}) %collective-permute-start.6) | collective-permute-done | bytes 262176 | tf_op jit(solution)/shard_map/ppermute | solution.py:478
  58.4 0.0 copy-start.4
  58.4 13.1 %collective-permute-done.7.refs_3_ = f32[32,8,256]{2,1,0:T(8,128)S(1)} collective-permute-done((f32[32,8,256]{2,1,0:T(8,128)}, f32[32,8,256]{2,1,0:T(8,128)S(1)}, u32[]{:S(2)}, u32[]{:S(2)}) %collective-permute-start.7) | collective-permute-done | bytes 262176 | tf_op jit(solution)/shard_map/ppermute | solution.py:478
  71.5 0.0 copy-start.5
  71.5 0.0 copy-done.3
  71.5 0.0 copy-done.4
  71.5 0.7 copy-done.5
  72.2 2.8 %shard_map.97 = (f32[32,32,256]{2,1,0:T(8,128)}, f32[32,32]{1,0:T(8,128)}) custom-call(s32[3]{0:T(128)} %pad_add_fusion.place, f32[32,8,256]{2,1,0:T(8,128)} %get-tuple-element.25.refs_0_, f32[32,8,256]{2,1,0:T(8,128)} %copy-done.3, f32[32,8,256]{2,1,0:T(8,128)} %copy-done.4, f32[32,8,256]{2,1,0:T(8,128)} %copy-done.5), custom_call_target="tpu_custom_call" | custom-call | tf_op jit(solution)/shard_map/pallas_call | solution.py:455
  75.0 1.6 %collective-permute-start.8 = (f32[32,32]{1,0:T(8,128)}, f32[32,32]{1,0:T(8,128)S(1)}, u32[]{:S(2)}, u32[]{:S(2)}) collective-permute-start(f32[32,32]{1,0:T(8,128)} %get-tuple-element.29), channel_id=1, source_target_pairs={{0,4},{4,0},{8,12},{12,8},{1,5},{5,1},{9,13},{13,9},{2,6},{6,2},{1... | collective-permute-start | bytes 12296 | tf_op jit(solution)/shard_map/ppermute | solution.py:478
  76.6 1.0 collective-permute-done.8
  77.7 0.7 add.15
  78.4 1.0 collective-permute-start.9
  79.4 2.8 %collective-permute-done.9 = f32[32,32]{1,0:T(8,128)S(1)} collective-permute-done((f32[32,32]{1,0:T(8,128)S(1)}, f32[32,32]{1,0:T(8,128)S(1)}, u32[]{:S(2)}, u32[]{:S(2)}) %collective-permute-start.9) | collective-permute-done | bytes 4128 | tf_op jit(solution)/shard_map/ppermute | solution.py:478
  82.2 0.5 collective-permute-start.10
  82.7 3.2 %collective-permute-done.10 = f32[32,32]{1,0:T(8,128)S(1)} collective-permute-done((f32[32,32]{1,0:T(8,128)S(1)}, f32[32,32]{1,0:T(8,128)S(1)}, u32[]{:S(2)}, u32[]{:S(2)}) %collective-permute-start.10) | collective-permute-done | bytes 4128 | tf_op jit(solution)/shard_map/ppermute | solution.py:478
  85.9 0.0 collective-permute-start.11
  85.9 3.7 %collective-permute-done.11 = f32[32,32]{1,0:T(8,128)S(1)} collective-permute-done((f32[32,32]{1,0:T(8,128)S(1)}, f32[32,32]{1,0:T(8,128)S(1)}, u32[]{:S(2)}, u32[]{:S(2)}) %collective-permute-start.11) | collective-permute-done | bytes 4128 | tf_op jit(solution)/shard_map/ppermute | solution.py:478
  89.7 0.0 collective-permute-start.12
  89.7 4.6 %collective-permute-done.12 = f32[32,32]{1,0:T(8,128)S(1)} collective-permute-done((f32[32,32]{1,0:T(8,128)S(1)}, f32[32,32]{1,0:T(8,128)S(1)}, u32[]{:S(2)}, u32[]{:S(2)}) %collective-permute-start.12) | collective-permute-done | bytes 4128 | tf_op jit(solution)/shard_map/ppermute | solution.py:478
  94.3 0.6 add.19.gram_ref
  94.9 6.0 %shard_map.98 = (f32[32,8,256]{2,1,0:T(8,128)}, f32[32,8,256]{2,1,0:T(8,128)}, f32[32,8,256]{2,1,0:T(8,128)}, f32[32,8,256]{2,1,0:T(8,128)}, f32[32,32]{1,0:T(8,128)}) custom-call(s32[3]{0:T(128)} %pad_add_fusion.place, f32[32,32]{1,0:T(8,128)} %add.19.gram_ref, f32[32,32,256]{2,1,0:T(8,128)} %get-tuple-element.30.whole), custom_call_target="tpu_custom_call" | custom-call | tf_op jit(solution)/shard_map/pallas_call | solution.py:455
  100.9 0.0 collective-permute-start.13
  100.9 1.9 %collective-permute-start.14 = (f32[32,8,256]{2,1,0:T(8,128)}, f32[32,8,256]{2,1,0:T(8,128)S(1)}, u32[]{:S(2)}, u32[]{:S(2)}) collective-permute-start(f32[32,8,256]{2,1,0:T(8,128)} %get-tuple-element.33), channel_id=1, source_target_pairs={{0,2},{1,3},{2,0},{3,1},{4,6},{5,7},{6,4},{7,5},{8,10},{9,11},{10,... | collective-permute-start | bytes 786440 | tf_op jit(solution)/shard_map/ppermute | solution.py:478
  102.8 1.6 %collective-permute-start.15 = (f32[32,8,256]{2,1,0:T(8,128)}, f32[32,8,256]{2,1,0:T(8,128)S(1)}, u32[]{:S(2)}, u32[]{:S(2)}) collective-permute-start(f32[32,8,256]{2,1,0:T(8,128)} %get-tuple-element.34), channel_id=1, source_target_pairs={{0,3},{1,2},{2,1},{3,0},{4,7},{5,6},{6,5},{7,4},{8,11},{9,10},{10,... | collective-permute-start | bytes 786440 | tf_op jit(solution)/shard_map/ppermute | solution.py:478
  104.4 6.0 %collective-permute-done.13.refs_1_ = f32[32,8,256]{2,1,0:T(8,128)S(1)} collective-permute-done((f32[32,8,256]{2,1,0:T(8,128)}, f32[32,8,256]{2,1,0:T(8,128)S(1)}, u32[]{:S(2)}, u32[]{:S(2)}) %collective-permute-start.13) | collective-permute-done | bytes 262176 | tf_op jit(solution)/shard_map/ppermute | solution.py:478
  110.4 0.0 copy-start
  110.4 8.0 %collective-permute-done.14.refs_2_ = f32[32,8,256]{2,1,0:T(8,128)S(1)} collective-permute-done((f32[32,8,256]{2,1,0:T(8,128)}, f32[32,8,256]{2,1,0:T(8,128)S(1)}, u32[]{:S(2)}, u32[]{:S(2)}) %collective-permute-start.14) | collective-permute-done | bytes 262176 | tf_op jit(solution)/shard_map/ppermute | solution.py:478
  118.4 0.0 copy-start.1
  118.4 4.8 %collective-permute-done.15.refs_3_ = f32[32,8,256]{2,1,0:T(8,128)S(1)} collective-permute-done((f32[32,8,256]{2,1,0:T(8,128)}, f32[32,8,256]{2,1,0:T(8,128)S(1)}, u32[]{:S(2)}, u32[]{:S(2)}) %collective-permute-start.15) | collective-permute-done | bytes 262176 | tf_op jit(solution)/shard_map/ppermute | solution.py:478
  123.2 0.0 copy-start.2
  123.2 0.0 copy-done
  123.2 0.0 copy-done.1
  123.2 0.7 copy-done.2
  123.9 2.4 %shard_map.99 = f32[8,128,256]{2,1,0:T(8,128)} custom-call(s32[3]{0:T(128)} %pad_add_fusion.place, f32[32,8,256]{2,1,0:T(8,128)} %get-tuple-element.31.refs_0_, f32[32,8,256]{2,1,0:T(8,128)} %copy-done, f32[32,8,256]{2,1,0:T(8,128)} %copy-done.1, f32[32,8,256]{2,1,0:T(8,128)} %copy-done.2), custom_call_target="tpu_custom_call" | custom-call | tf_op jit(solution)/shard_map/pallas_call | solution.py:455
  (3 shorter events, 0.0 us)
Async XLA Ops:
  4.6 7.4 %collective-permute-start = (f32[13,16,256]{2,1,0:T(8,128)}, f32[13,16,256]{2,1,0:T(8,128)S(1)}, u32[]{:S(2)}, u32[]{:S(2)}) collective-permute-start(f32[13,16,256]{2,1,0:T(8,128)} %get-tuple-element.19), channel_id=1, source_target_pairs={{0,16},{16,0},{1,17},{17,1},{2,18},{18,2},{3,19},{19,3},{4,20},{20... | collective-permute-start | bytes 638984 | tf_op jit(solution)/shard_map/ppermute | solution.py:515
  5.2 6.6 %collective-permute-start.1 = (f32[2,16,8,128]{3,2,1,0:T(8,128)}, f32[2,16,8,128]{3,2,1,0:T(8,128)S(1)}, u32[]{:S(2)}, u32[]{:S(2)}) collective-permute-start(f32[2,16,8,128]{3,2,1,0:T(8,128)} %get-tuple-element.20), channel_id=1, source_target_pairs={{0,4},{8,12},{4,0},{12,8},{1,5},{9,13},{5,1},{13,9},{2,6},{10,14},... | collective-permute-start | bytes 393224 | tf_op jit(solution)/shard_map/ppermute | solution.py:515
  5.2 6.6 %collective-permute-start.2 = (f32[2,16,8,128]{3,2,1,0:T(8,128)}, f32[2,16,8,128]{3,2,1,0:T(8,128)S(1)}, u32[]{:S(2)}, u32[]{:S(2)}) collective-permute-start(f32[2,16,8,128]{3,2,1,0:T(8,128)} %get-tuple-element.21), channel_id=1, source_target_pairs={{4,8},{8,4},{5,9},{9,5},{6,10},{10,6},{7,11},{11,7},{20,24},{24,20... | collective-permute-start | bytes 393224 | tf_op jit(solution)/shard_map/ppermute | solution.py:515
  5.9 5.9 %collective-permute-start.3 = (f32[2,2,8,128]{3,2,1,0:T(8,128)}, f32[2,2,8,128]{3,2,1,0:T(8,128)S(1)}, u32[]{:S(2)}, u32[]{:S(2)}) collective-permute-start(f32[2,2,8,128]{3,2,1,0:T(8,128)} %get-tuple-element.22), channel_id=1, source_target_pairs={{0,20},{8,28},{4,16},{12,24},{16,4},{24,12},{20,0},{28,8},{1,21},{... | collective-permute-start | bytes 49160 | tf_op jit(solution)/shard_map/ppermute | solution.py:515
  9.9 1.9 %collective-permute-start.4 = (f32[2,2,8,128]{3,2,1,0:T(8,128)}, f32[2,2,8,128]{3,2,1,0:T(8,128)S(1)}, u32[]{:S(2)}, u32[]{:S(2)}) collective-permute-start(f32[2,2,8,128]{3,2,1,0:T(8,128)} %get-tuple-element.23), channel_id=1, source_target_pairs={{4,24},{8,20},{20,8},{24,4},{5,25},{9,21},{21,9},{25,5},{6,26},{10... | collective-permute-start | bytes 49160 | tf_op jit(solution)/shard_map/ppermute | solution.py:515
  11.8 0.6 copy-start.9
  11.8 0.6 copy-start.10
  11.8 0.7 copy-start.7
  11.8 0.7 copy-start.8
  12.1 0.7 copy-start.6
  45.5 10.9 %collective-permute-start.5 = (f32[32,8,256]{2,1,0:T(8,128)}, f32[32,8,256]{2,1,0:T(8,128)S(1)}, u32[]{:S(2)}, u32[]{:S(2)}) collective-permute-start(f32[32,8,256]{2,1,0:T(8,128)} %get-tuple-element.26), channel_id=1, source_target_pairs={{0,1},{1,0},{2,3},{3,2},{4,5},{5,4},{6,7},{7,6},{8,9},{9,8},{10,11... | collective-permute-start | bytes 786440 | tf_op jit(solution)/shard_map/ppermute | solution.py:478
  47.1 11.3 %collective-permute-start.6 = (f32[32,8,256]{2,1,0:T(8,128)}, f32[32,8,256]{2,1,0:T(8,128)S(1)}, u32[]{:S(2)}, u32[]{:S(2)}) collective-permute-start(f32[32,8,256]{2,1,0:T(8,128)} %get-tuple-element.27), channel_id=1, source_target_pairs={{0,2},{1,3},{2,0},{3,1},{4,6},{5,7},{6,4},{7,5},{8,10},{9,11},{10,... | collective-permute-start | bytes 786440 | tf_op jit(solution)/shard_map/ppermute | solution.py:478
  47.4 24.1 %collective-permute-start.7 = (f32[32,8,256]{2,1,0:T(8,128)}, f32[32,8,256]{2,1,0:T(8,128)S(1)}, u32[]{:S(2)}, u32[]{:S(2)}) collective-permute-start(f32[32,8,256]{2,1,0:T(8,128)} %get-tuple-element.28), channel_id=1, source_target_pairs={{0,3},{1,2},{2,1},{3,0},{4,7},{5,6},{6,5},{7,4},{8,11},{9,10},{10,... | collective-permute-start | bytes 786440 | tf_op jit(solution)/shard_map/ppermute | solution.py:478
  56.4 15.1 %copy-start.3 = (f32[32,8,256]{2,1,0:T(8,128)}, f32[32,8,256]{2,1,0:T(8,128)S(1)}, u32[]{:S(2)}) copy-start(f32[32,8,256]{2,1,0:T(8,128)S(1)} %collective-permute-done.5.refs_1_) | copy-start | bytes 786436
  58.4 13.1 %copy-start.4 = (f32[32,8,256]{2,1,0:T(8,128)}, f32[32,8,256]{2,1,0:T(8,128)S(1)}, u32[]{:S(2)}) copy-start(f32[32,8,256]{2,1,0:T(8,128)S(1)} %collective-permute-done.6.refs_2_) | copy-start | bytes 786436
  71.5 0.7 copy-start.5
  75.0 2.7 %collective-permute-start.8 = (f32[32,32]{1,0:T(8,128)}, f32[32,32]{1,0:T(8,128)S(1)}, u32[]{:S(2)}, u32[]{:S(2)}) collective-permute-start(f32[32,32]{1,0:T(8,128)} %get-tuple-element.29), channel_id=1, source_target_pairs={{0,4},{4,0},{8,12},{12,8},{1,5},{5,1},{9,13},{13,9},{2,6},{6,2},{1... | collective-permute-start | bytes 12296 | tf_op jit(solution)/shard_map/ppermute | solution.py:478
  78.4 3.7 %collective-permute-start.9 = (f32[32,32]{1,0:T(8,128)S(1)}, f32[32,32]{1,0:T(8,128)S(1)}, u32[]{:S(2)}, u32[]{:S(2)}) collective-permute-start(f32[32,32]{1,0:T(8,128)S(1)} %add.15), channel_id=1, source_target_pairs={{0,8},{4,12},{8,0},{12,4},{1,9},{5,13},{9,1},{13,5},{2,10},{6,14},... | collective-permute-start | bytes 12296 | tf_op jit(solution)/shard_map/ppermute | solution.py:478
  82.2 3.7 %collective-permute-start.10 = (f32[32,32]{1,0:T(8,128)S(1)}, f32[32,32]{1,0:T(8,128)S(1)}, u32[]{:S(2)}, u32[]{:S(2)}) collective-permute-start(f32[32,32]{1,0:T(8,128)S(1)} %add.16), channel_id=1, source_target_pairs={{0,16},{16,0},{1,17},{17,1},{2,18},{18,2},{3,19},{19,3},{4,20},{20... | collective-permute-start | bytes 12296 | tf_op jit(solution)/shard_map/ppermute | solution.py:478
  85.9 3.7 %collective-permute-start.11 = (f32[32,32]{1,0:T(8,128)S(1)}, f32[32,32]{1,0:T(8,128)S(1)}, u32[]{:S(2)}, u32[]{:S(2)}) collective-permute-start(f32[32,32]{1,0:T(8,128)S(1)} %add.17), channel_id=1, source_target_pairs={{0,1},{1,0},{2,3},{3,2},{4,5},{5,4},{6,7},{7,6},{8,9},{9,8},{10,11... | collective-permute-start | bytes 12296 | tf_op jit(solution)/shard_map/ppermute | solution.py:478
  89.7 4.6 %collective-permute-start.12 = (f32[32,32]{1,0:T(8,128)S(1)}, f32[32,32]{1,0:T(8,128)S(1)}, u32[]{:S(2)}, u32[]{:S(2)}) collective-permute-start(f32[32,32]{1,0:T(8,128)S(1)} %add.18), channel_id=1, source_target_pairs={{0,2},{1,3},{2,0},{3,1},{4,6},{5,7},{6,4},{7,5},{8,10},{9,11},{10,... | collective-permute-start | bytes 12296 | tf_op jit(solution)/shard_map/ppermute | solution.py:478
  100.9 9.5 %collective-permute-start.13 = (f32[32,8,256]{2,1,0:T(8,128)}, f32[32,8,256]{2,1,0:T(8,128)S(1)}, u32[]{:S(2)}, u32[]{:S(2)}) collective-permute-start(f32[32,8,256]{2,1,0:T(8,128)} %get-tuple-element.32), channel_id=1, source_target_pairs={{0,1},{1,0},{2,3},{3,2},{4,5},{5,4},{6,7},{7,6},{8,9},{9,8},{10,11... | collective-permute-start | bytes 786440 | tf_op jit(solution)/shard_map/ppermute | solution.py:478
  100.9 17.5 %collective-permute-start.14 = (f32[32,8,256]{2,1,0:T(8,128)}, f32[32,8,256]{2,1,0:T(8,128)S(1)}, u32[]{:S(2)}, u32[]{:S(2)}) collective-permute-start(f32[32,8,256]{2,1,0:T(8,128)} %get-tuple-element.33), channel_id=1, source_target_pairs={{0,2},{1,3},{2,0},{3,1},{4,6},{5,7},{6,4},{7,5},{8,10},{9,11},{10,... | collective-permute-start | bytes 786440 | tf_op jit(solution)/shard_map/ppermute | solution.py:478
  102.8 20.4 %collective-permute-start.15 = (f32[32,8,256]{2,1,0:T(8,128)}, f32[32,8,256]{2,1,0:T(8,128)S(1)}, u32[]{:S(2)}, u32[]{:S(2)}) collective-permute-start(f32[32,8,256]{2,1,0:T(8,128)} %get-tuple-element.34), channel_id=1, source_target_pairs={{0,3},{1,2},{2,1},{3,0},{4,7},{5,6},{6,5},{7,4},{8,11},{9,10},{10,... | collective-permute-start | bytes 786440 | tf_op jit(solution)/shard_map/ppermute | solution.py:478
  110.4 12.9 %copy-start = (f32[32,8,256]{2,1,0:T(8,128)}, f32[32,8,256]{2,1,0:T(8,128)S(1)}, u32[]{:S(2)}) copy-start(f32[32,8,256]{2,1,0:T(8,128)S(1)} %collective-permute-done.13.refs_1_) | copy-start | bytes 786436
  118.4 4.8 %copy-start.1 = (f32[32,8,256]{2,1,0:T(8,128)}, f32[32,8,256]{2,1,0:T(8,128)S(1)}, u32[]{:S(2)}) copy-start(f32[32,8,256]{2,1,0:T(8,128)S(1)} %collective-permute-done.14.refs_2_) | copy-start | bytes 786436
  123.2 0.7 copy-start.2

commit v2 on v1

--- a/solution.py
+++ b/solution.py
@@ -21,10 +21,9 @@
 FIELDS = 5
 F32 = jnp.float32
 BF16 = jnp.bfloat16
-AXES = ("gx", "gy", "dir")
 WEIGHTS = ((4.0, 1.0), (1.0, 4.0))
 PARTS = 2
-UNROLL = 3
+FIRST_ROWS = 80
 
 
 def iota(shape, dim):
@@ -35,7 +34,7 @@
     return pltpu.roll(value, shift % LANES, 1)
 
 
-def pack(counts, place, *refs):
+def pack(counts, *refs):
     count_x, count_y = counts
     sources, refs = refs[:7], refs[7:]
     fields, refs = refs[0], refs[1:]
@@ -62,7 +61,7 @@
     copies[0].wait()
 
     for pairing, out in enumerate(row_out):
-        send_last = place[0] % 2 == pairing
+        send_last = lax.axis_index("gx") % 2 == pairing
         base = pl.ds(pl.multiple_of(jnp.where(send_last, rows - PAD, 0), PAD), PAD)
         out[:PLANES] = dirs[:, base, :]
         out[PLANES:] = fields[:, base, :]
@@ -80,10 +79,10 @@
                     here, roll(planes[p, span, cols - LANES :], PAD * (p + 1)), last
                 )
             for pairing, out in enumerate(col_out):
-                send_last = place[1] % 2 == pairing
+                send_last = lax.axis_index("gy") % 2 == pairing
                 out[q, g] = jnp.where(send_last, last, first)
     for i in range(count_x):
-        send_last = place[0] % 2 == i
+        send_last = lax.axis_index("gx") % 2 == i
         base = pl.ds(jnp.where(send_last, (rows - PAD) // 8, 0), PAD // 8)
         for j in range(count_y):
             corner_out[i * count_y + j][...] = col_out[j][:, base]
@@ -139,8 +138,9 @@
     return total
 
 
-def solve(counts, place, *refs):
+def solve(counts, span, *refs):
     count_x, count_y = counts
+    row_first, row_count = span
     got_rows, refs = refs[:count_x], refs[count_x:]
     got_cols, refs = refs[:count_y], refs[count_y:]
     got_corners, refs = refs[: count_x * count_y], refs[count_x * count_y :]
@@ -148,12 +148,12 @@
     *outs, halo_rows, halo_cols, lined, turned, planes, coeffs, extras, base, ping, pong = refs
     rows, cols = dirs.shape[1:]
     tall = lined.shape[0]
-    over = (tall - rows) // 2
+    over = (tall - row_count) // 2
     high = tall // BANDS
     wide = planes.shape[2]
     groups = (rows + 2 * PAD) // 8
     edge = PAD // 8
-    even = [place[0] % 2 == 0, place[1] % 2 == 0]
+    even = [lax.axis_index("gx") % 2 == 0, lax.axis_index("gy") % 2 == 0]
 
     def sides(axis, one, two):
         return jnp.where(even[axis], two, one), jnp.where(even[axis], one, two)
@@ -183,16 +183,15 @@
     lane = iota((8, LANES), 1)
     own_slot = lane // PAD == iota((8, LANES), 0)
 
-    def over_pairs(body):
-        def two(i, _):
-            body(2 * i)
-            body(2 * i + 1)
-            return 0
-
-        lax.fori_loop(0, high // 2, two, 0)
+    def over_rows(body):
+        for i in range(high):
+            body(i)
 
     for q, (source, first, count) in enumerate(((dirs, 0, PLANES), (fields, PLANES, FIELDS))):
         for g in range(groups):
+            lines_of = [8 * g + d - PAD - (row_first - over) for d in range(8)]
+            if lines_of[-1] < 0 or lines_of[0] >= tall:
+                continue
             inner = edge <= g < groups - edge
             side, at = (0, g) if g < edge else (1, g - groups + edge)
             stack = []
@@ -204,24 +203,20 @@
                 else:
                     stack.append(halo_rows[side, first + p, 8 * at : 8 * at + 8, :])
             lines = jnp.swapaxes(jnp.stack(stack), 0, 1)
-            for s in range(8):
-                line = 8 * g + s - (PAD - over)
+            for d, line in enumerate(lines_of):
                 if 0 <= line < tall:
-                    lined[line, :, :cols] = lines[s]
+                    lined[line, :, :cols] = lines[d]
                     for side_y in range(2):
                         begin = cols + LANES * side_y
                         lined[line, :, begin : begin + LANES] = jnp.where(
-                            own_slot, halo_cols[side_y, q, g, s : s + 1, :], 0.0
+                            own_slot, halo_cols[side_y, q, g, d : d + 1, :], 0.0
                         )
 
-        def turn(b, _):
+        for b in range(BANDS):
             value = lined[pl.ds(high * b, high)].reshape(high * 8, cols + 2 * LANES)
             turned[pl.ds(high * b, high)] = split_dot(value, places[b]).reshape(
                 high, 8, lanes_out
             )
-            return 0
-
-        lax.fori_loop(0, BANDS, turn, 0)
 
         def band(i):
             for t in range(lanes_out // LANES):
@@ -231,7 +226,7 @@
                 for j, tile in enumerate(from_bands(tiles)[: wide - BANDS * t], BANDS * t):
                     planes[q, i, j] = tile
 
-        over_pairs(band)
+        over_rows(band)
 
     row_of = iota((8, LANES), 0)
     kind = row_of % 4
@@ -281,7 +276,7 @@
         weigh(i, i - 1, i + 1, False, False)
         return 0
 
-    lax.fori_loop(1, high - 1, weigh_inner, 0)
+    lax.fori_loop(1, high - 1, weigh_inner, 0, unroll=4)
 
     def put(ref, m, i, j, value, edges=True):
         ref[m, i + 1, j] = value
@@ -291,22 +286,8 @@
             if i == high - 1:
                 ref[m, 0, j] = roll(value, SPANS)
 
-    def over_rows(body):
-        body(0)
-        body(high - 1)
-
-        def some(i, _):
-            for d in range(UNROLL):
-                body(UNROLL * i + d + 1)
-            return 0
-
-        full = (high - 2) // UNROLL
-        lax.fori_loop(0, full, some, 0)
-        for i in range(1 + UNROLL * full, high - 1):
-            body(i)
-
     def extra(kind, m, i, j):
-        return extras[i, j, 4 * m + kind : 4 * m + kind + 1, :]
+        return extras[i, j, pl.ds(4 * m + kind, 1), :]
 
     def start(i):
         for j in range(wide):
@@ -334,68 +315,77 @@
     def to(ref):
         return lambda m, i, j, value: put(ref, m, i, j, value)
 
-    def solve_from(one, two, three, store):
-        sweep(one, 0, to(two))
-        sweep(two, 1, to(three))
+    def solve_from_base(kind, _):
+        sweep(base, 0, to(ping))
+        sweep(ping, 1, to(pong))
 
         def add(m, i, j, value):
-            put(one, m, i, j, two[m, i + 1, j] + (KEEP_BACK * GROWN) * value)
-
-        sweep(three, 0, add)
-        sweep(one, 1, to(three))
+            put(base, m, i, j, ping[m, i + 1, j] + (KEEP_BACK * GROWN) * value)
+
+        sweep(pong, 0, add)
+        sweep(base, 1, to(pong))
 
         def last(m, i, j, value):
-            store(m, i, j, one[m, i + 1, j] - (KEEP_BACK * SHRUNK) * value)
-
-        sweep(three, 2, last)
-
-    def to_adjoint(m, i, j, value):
-        put(ping, m, i, j, extra(1, m, i, j) * value)
-
-    def to_sketch(m, i, j, value):
-        value = extra(2, m, i, j) * value
-        planes[0, i, j] = value if m == 0 else planes[0, i, j] + value
-
-    solve_from(base, ping, pong, to_adjoint)
-    solve_from(ping, base, pong, to_sketch)
+            value = base[m, i + 1, j] - (KEEP_BACK * SHRUNK) * value
+            put(base, m, i, j, extra(kind, m, i, j) * value)
+
+        sweep(pong, 2, last)
+        return 0
+
+    lax.fori_loop(1, 3, solve_from_base, 0)
 
     def unband(i):
         for t in range(lanes_out // LANES):
-            tiles = [planes[0, i, j] for j in range(BANDS * t, min(BANDS * t + BANDS, wide))]
+            columns = range(BANDS * t, min(BANDS * t + BANDS, wide))
+            tiles = [base[0, i + 1, j] + base[1, i + 1, j] for j in columns]
             tiles += [jnp.zeros((8, LANES), F32)] * (BANDS - len(tiles))
             for b, tile in enumerate(to_bands(tiles)):
                 turned[high * b + i, :, LANES * t : LANES * t + LANES] = tile
 
-    over_pairs(unband)
-
-    def unturn(b, _):
+    over_rows(unband)
+
+    for b in range(BANDS):
         value = turned[pl.ds(high * b, high)].reshape(high * 8, lanes_out)
         value = split_dot(value, places[b, :cols, :], transposed=True)
         lined[pl.ds(high * b, high), :, :cols] = value.reshape(high, 8, cols)
-        return 0
-
-    lax.fori_loop(0, BANDS, unturn, 0)
-    part = rows // len(outs)
+
+    part = row_count // len(outs)
     for k, out in enumerate(outs):
-        out[...] = lined[pl.ds(over + part * (place[2] ^ k), part), :, :cols]
-
-
-def gram_of(place, *refs):
-    parts, (whole, gram) = refs[:-2], refs[-2:]
-    count = len(parts)
-    for k, part in enumerate(parts):
-        block = pl.multiple_of(8 * (place[2] ^ k), 8)
-        for r in range(part.shape[0]):
-            whole[r, pl.ds(block, 8), :] = part[r]
-    total = jnp.zeros((8 * count, 8 * count), F32)
-    for r in range(whole.shape[0]):
-        total = total + lax.dot_general(
-            whole[r],
-            whole[r],
-            (((1,), (1,)), ((), ())),
-            precision=lax.Precision.HIGHEST,
-            preferred_element_type=F32,
-        )
+        out[...] = lined[pl.ds(over + part * (lax.axis_index("dir") ^ k), part), :, :cols]
+
+
+def halves(value):
+    high = value.astype(BF16)
+    return high, (value - high.astype(F32)).astype(BF16)
+
+
+def gram_sum(parts):
+    total = cross = None
+    dims = (((1,), (1,)), ((), ()))
+    for r in range(parts[0].shape[0]):
+        high, low = halves(jnp.concatenate([part[r] for part in parts], axis=0))
+        one = lax.dot_general(high, high, dims, preferred_element_type=F32)
+        two = lax.dot_general(high, low, dims, preferred_element_type=F32)
+        total = one if total is None else total + one
+        cross = two if cross is None else cross + two
+    return total + (cross + cross.T)
+
+
+def gram_first(*refs):
+    refs[-1][...] = gram_sum(refs[:-1])
+
+
+def by_device(value, me, held):
+    for k in range(value.shape[0] // 8):
+        held[pl.ds(pl.multiple_of(8 * (me ^ k), 8), 8), :] = value[8 * k : 8 * k + 8]
+    return held[...]
+
+
+def gram_rest(before, *refs):
+    parts, (gram, held) = refs[:-2], refs[-2:]
+    total = before[...] + gram_sum(parts)
+    for _ in range(2):
+        total = by_device(total, lax.axis_index("dir"), held).T
     gram[...] = total
 
 
@@ -415,47 +405,55 @@
     return work / jnp.sqrt(pivots), lane, row_of
 
 
-def basis_of(cells, place, gram_ref, whole, *refs):
-    outs, upper, scratch = refs[:-2], refs[-2], refs[-1]
-    size = gram_ref.shape[0]
+def basis_of(cells, pieces, terms, *refs):
+    sums, refs = refs[:terms], refs[terms:]
+    own, refs = refs[: 4 * pieces], refs[4 * pieces :]
+    *outs, upper, held = refs
     count = len(outs)
-    work, lane, row_of = factor(gram_ref[...] / cells, size)
+    size = sums[0].shape[0]
+    gram = functools.reduce(lambda a, b: a + b, [term[...] for term in sums])
+    work, lane, row_of = factor(gram / cells, size)
     upper[...] = jnp.where(lane >= row_of, work, 0.0)[:, :size]
-    scratch[...] = work
-    inverse = jnp.concatenate(
-        [
-            scratch[pl.ds(pl.multiple_of(8 * (place[2] ^ k), 8), 8), :]
-            for k in range(count)
-        ],
-        axis=0,
-    )[:, size : 2 * size]
-    for r in range(whole.shape[0]):
-        value = jnp.dot(
-            inverse, whole[r], precision=lax.Precision.HIGHEST, preferred_element_type=F32
-        )
-        for k, out in enumerate(outs):
-            out[r] = value[8 * k : 8 * k + 8]
-
-
-def assemble(place, *refs):
-    parts, out = refs[:-1], refs[-1]
-    for k, part in enumerate(parts):
-        rows = part.shape[0]
-        base = rows * (place[2] ^ k)
-        for c in range(rows // 8):
-            out[:, pl.ds(pl.multiple_of(base + 8 * c, 8), 8), :] = jnp.swapaxes(
-                part[8 * c : 8 * c + 8], 0, 1
-            )
-
-
-def call(kernel, outs, *args, scratch=(), limit=56, space=pltpu.VMEM):
-    smem = pl.BlockSpec(memory_space=pltpu.SMEM)
+    inverse = work[:, size : 2 * size]
+    for _ in range(2):
+        inverse = by_device(inverse, lax.axis_index("dir"), held).T
+    high, low = halves(inverse)
+    both = jnp.concatenate([high, low], axis=0)
+    base = 0
+    for piece in range(pieces):
+        parts = own[count * piece : count * piece + count]
+        for r in range(parts[0].shape[0]):
+            value = jnp.concatenate([part[r] for part in parts], axis=0)
+            value_high, value_low = halves(value)
+            first = jnp.dot(both, value_high, preferred_element_type=F32)
+            second = jnp.dot(high, value_low, preferred_element_type=F32)
+            total = first[:size] + (first[size:] + second)
+            for k, out in enumerate(outs):
+                out[base + r] = total[8 * k : 8 * k + 8]
+        base += parts[0].shape[0]
+
+
+def assemble(spans, *refs):
+    parts, (out, held) = refs[:-2], refs[-2:]
+    count = len(parts)
+    base = 0
+    for first, rows in spans:
+        share = rows // count
+        for k, part in enumerate(parts):
+            at = first + share * (lax.axis_index("dir") ^ k)
+            held[pl.ds(at, share)] = part[base : base + share]
+        base += share
+    for g in range(out.shape[1] // 8):
+        out[:, 8 * g : 8 * g + 8, :] = jnp.swapaxes(held[8 * g : 8 * g + 8], 0, 1)
+
+
+def call(kernel, outs, *args, scratch=(), limit=8, space=pltpu.VMEM):
     vmem = pl.BlockSpec(memory_space=pltpu.VMEM)
     shapes = [jax.ShapeDtypeStruct(shape, F32) for shape in outs]
     return pl.pallas_call(
         kernel,
         out_shape=shapes,
-        in_specs=[smem] + [pl.BlockSpec(memory_space=space)] * (len(args) - 1),
+        in_specs=[pl.BlockSpec(memory_space=space)] * len(args),
         out_specs=[vmem] * len(shapes),
         scratch_shapes=[
             pltpu.VMEM(shape, F32) if isinstance(shape, tuple) else shape for shape in scratch
@@ -478,19 +476,31 @@
     return lax.ppermute(value, axis, [(i, i ^ bit) for i in range(count)])
 
 
-def sum_all(value):
-    for axis in ("gy", "gx", "dir"):
-        bit = 1
-        while bit < lax.axis_size(axis):
-            value = value + swap_bit(value, axis, bit)
-            bit *= 2
-    return value
+def partial_sums(value):
+    axes = ("gx", "gy", "dir")
+    sizes = [lax.axis_size(axis) for axis in axes]
+    strides = [sizes[1] * sizes[2], sizes[2], 1]
+    bits = [
+        [stride << b for b in range(size.bit_length() - 1)] for size, stride in zip(sizes, strides)
+    ]
+    rest = bits[1][1:] + bits[0]
+    stages = [bits[2], bits[1][:1]] + [rest[i : i + 2] for i in range(0, len(rest), 2)]
+    count = sizes[0] * strides[0]
+    terms = [value]
+    for stage in stages:
+        value = functools.reduce(lambda a, b: a + b, terms)
+        masks = [0]
+        for bit in stage:
+            masks += [mask | bit for mask in masks]
+        terms = [value] + [
+            lax.ppermute(value, axes, [(i, i ^ mask) for i in range(count)]) for mask in masks[1:]
+        ]
+    return terms
 
 
 def on_device(directions, velocity, viscosity, basal_drag, misfit_weight, ice_mask, grounded):
     own, rows, cols = directions.shape
     across = lax.axis_size("dir")
-    place = jnp.stack([lax.axis_index(axis) for axis in AXES]).astype(jnp.int32)
     args = (directions, velocity, viscosity, basal_drag, misfit_weight, ice_mask, grounded)
 
     count_y = lax.axis_size("gy")
@@ -502,10 +512,10 @@
         + [(PLANES + FIELDS, PAD, cols)] * counts[0]
         + [(2, rows // 8, 8, LANES)] * counts[1]
         + [(2, PAD // 8, 8, LANES)] * (counts[0] * counts[1]),
-        place,
         *args,
         scratch=[pltpu.VMEM(a.shape, a.dtype) for a in args] + [pltpu.SemaphoreType.DMA((7,))],
         space=pl.ANY,
+        limit=60,
     )
     moves = [("gx", s) for s in sets_x] + [("gy", s) for s in sets_y]
     for set_x in sets_x:
@@ -515,51 +525,62 @@
     got = [lax.ppermute(m, axis, pairs) for m, (axis, pairs) in zip(messages, moves)]
 
     over = REACH + 2
-    tall = rows + 2 * over
     wide = pl.cdiv(cols + 2 * PAD, SPANS)
     groups = (rows + 2 * PAD) // 8
-    high = tall // BANDS
     lanes_out = pl.cdiv(wide, BANDS) * LANES
-    state = (2, high + 2, wide, 8, LANES)
-    part = (rows // across, own, cols)
-    parts = call(
-        functools.partial(solve, counts),
-        [part] * across,
-        place,
-        *got,
-        directions,
-        fields,
-        band_places(cols, wide),
-        scratch=[
-            (2, PLANES + FIELDS, PAD, cols),
-            (2, 2, groups, 8, LANES),
-            (tall, 8, cols + 2 * LANES),
-            (tall, 8, lanes_out),
-            (2, high, wide, 8, LANES),
-            (3, high, wide, 8, LANES),
-            (high, wide, 8, LANES),
-            state,
-            state,
-            state,
-        ],
+    places = band_places(cols, wide)
+    spans = [(0, FIRST_ROWS * rows // 128), (FIRST_ROWS * rows // 128, rows - FIRST_ROWS * rows // 128)]
+    pieces = []
+    for span in spans:
+        tall = span[1] + 2 * over
+        high = tall // BANDS
+        state = (2, high + 2, wide, 8, LANES)
+        own_parts = call(
+            functools.partial(solve, counts, span),
+            [(span[1] // across, own, cols)] * across,
+            *got,
+            directions,
+            fields,
+            places,
+            scratch=[
+                (2, PLANES + FIELDS, PAD, cols),
+                (2, 2, groups, 8, LANES),
+                (tall, 8, cols + 2 * LANES),
+                (tall, 8, lanes_out),
+                (2, high, wide, 8, LANES),
+                (3, high, wide, 8, LANES),
+                (high, wide, 8, LANES),
+                state,
+                state,
+                state,
+            ],
+            limit=32,
+        )
+        pieces.append(
+            [own_parts[0]] + [swap_bit(own_parts[k], "dir", k) for k in range(1, across)]
+        )
+    total = own * across
+    (gram,) = call(gram_first, [(total, total)], *pieces[0])
+    (gram,) = call(
+        gram_rest, [(total, total)], gram, *pieces[1], scratch=[(total, total)]
+    )
+    grams = partial_sums(gram)
+    count = rows * cols * lax.axis_size("gx") * lax.axis_size("gy")
+    *parts, upper = call(
+        functools.partial(basis_of, float(count), len(pieces), len(grams)),
+        [(rows // across, own, cols)] * across + [(total, total)],
+        *grams,
+        *pieces[0],
+        *pieces[1],
+        scratch=[(total, total)],
     )
     parts = [parts[0]] + [swap_bit(parts[k], "dir", k) for k in range(1, across)]
-    total = own * across
-    whole, gram = call(
-        gram_of, [(rows // across, total, cols), (total, total)], place, *parts
+    (basis,) = call(
+        functools.partial(assemble, spans),
+        [(own, rows, cols)],
+        *parts,
+        scratch=[(rows, own, cols)],
     )
-    gram = sum_all(gram)
-    count = rows * cols * lax.axis_size("gx") * lax.axis_size("gy")
-    *parts, upper = call(
-        functools.partial(basis_of, float(count)),
-        [part] * across + [(total, total)],
-        place,
-        gram,
-        whole,
-        scratch=[(total, LANES)],
-    )
-    parts = [parts[0]] + [swap_bit(parts[k], "dir", k) for k in range(1, across)]
-    (basis,) = call(assemble, [(own, rows, cols)], place, *parts)
     return (basis, upper)
 
 

time: 127 us -> 99 us (0.78)
  waiting for transfers between devices: 58.2 us -> 39.4 us
  Pallas kernels: 47.4 us -> 31 us
  starting transfers between devices: 16 us -> 24.1 us
  other arithmetic: 1.9 us -> 0.01 us
    ppermute x11 -> x9, waiting for transfers between devices: 56.7 us -> 31 us  [swap_bit(): return lax.ppermute(value, axis, [(i, i ^ bit) for i in range(count)])]
    pallas_call x5 -> x7, Pallas kernels: 47.4 us -> 31 us  [call(): pl.pallas_call(kernel, out_shape=shapes, in_specs=[pl.BlockSpec(memory_sp...]
    ppermute x0 -> x7, starting transfers between devices: none -> 7.04 us  [partial_sums(): lax.ppermute(value, axes, [(i, i ^ mask) for i in range(count)])]
    ppermute x0 -> x7, waiting for transfers between devices: none -> 6.88 us  [partial_sums(): lax.ppermute(value, axes, [(i, i ^ mask) for i in range(count)])]
    add x5 -> x2, other arithmetic: 1.34 us -> 0.01 us  [partial_sums(): value = functools.reduce(lambda a, b: a + b, terms)]
    ppermute x11 -> x9, starting transfers between devices: 10.1 us -> 11.2 us  [swap_bit(): return lax.ppermute(value, axis, [(i, i ^ bit) for i in range(count)])]
  transfers between devices with their start and end apart: 16 -> 21, of which waited for: 13 -> 15; matrix products, arithmetic and copies ran while one was open for 0% -> 0% of each run, Pallas kernels for 0% -> 10%
where the time goes in v2:
time: 99 us; the launch traced here: 97.8 us
  waiting for transfers between devices  39.4 us (40%)
  Pallas kernels  31 us (31%)
  starting transfers between devices  24.1 us (24%)
  local copies, waits for them, and re-layouts  2.5 us (3%)
    ppermute x9, waiting for transfers between devices, swap_bit(): return lax.ppermute(value, axis, [(i, i ^ bit) for i in range(count)])  31 us
    pallas_call x7, Pallas kernels, call(): pl.pallas_call(kernel, out_shape=shapes, in_specs=[pl.BlockSpec(memory_sp...  31 us
    ppermute x9, starting transfers between devices, swap_bit(): return lax.ppermute(value, axis, [(i, i ^ bit) for i in range(count)])  11.2 us
    ppermute x7, starting transfers between devices, partial_sums(): lax.ppermute(value, axes, [(i, i ^ mask) for i in range(count)])  7.04 us
    ppermute x7, waiting for transfers between devices, partial_sums(): lax.ppermute(value, axes, [(i, i ^ mask) for i in range(count)])  6.88 us
    ppermute x5, starting transfers between devices, on_device(): lax.ppermute(m, axis, pairs)  5.92 us
    unnamed x6, local copies, waits for them, and re-layouts  2.5 us
  transfers between devices with their start and end apart: 21, of which 15 were waited for; matrix products, arithmetic and copies ran while one was open for 0% of the time, Pallas kernels for 10%

profile of v2, /device:TPU:20, one launch (start us, length us, event | category | flops | bytes accessed | tf_op | source)
XLA Modules:
  0.0 97.8 jit_solution(14762888138825131925)
XLA Ops:
  0.6 0.0 copy-start
  0.6 3.1 %shard_map.95 = (f32[5,128,256]{2,1,0:T(8,128)}, f32[13,16,256]{2,1,0:T(8,128)}, f32[2,16,8,128]{3,2,1,0:T(8,128)}, f32[2,16,8,128]{3,2,1,0:T(8,128)}, f32[2,2,8...) custom-call(f32[8,128,256]{2,1,0:T(8,128)} %refs_5_.5, f32[2,128,256]{2,1,0:T(8,128)} %refs_1_.1, f32[128,256]{1,0:T(8,128)} %refs_2_.1, ...), custom_call_target="tpu_custom_call" | custom-call | tf_op jit(solution)/shard_map/pallas_call | solution.py:453
  3.7 0.6 collective-permute-start
  4.3 0.0 collective-permute-start.1
  4.3 0.7 collective-permute-start.2
  4.9 4.0 %collective-permute-start.3 = (f32[2,2,8,128]{3,2,1,0:T(8,128)}, f32[2,2,8,128]{3,2,1,0:T(8,128)S(1)}, u32[]{:S(2)}, u32[]{:S(2)}) collective-permute-start(f32[2,2,8,128]{3,2,1,0:T(8,128)} %get-tuple-element.24), channel_id=1, source_target_pairs={{0,20},{8,28},{4,16},{12,24},{16,4},{24,12},{20,0},{28,8},{1,21},{... | collective-permute-start | bytes 49160 | tf_op jit(solution)/shard_map/ppermute | solution.py:525
  9.0 0.7 collective-permute-start.4
  9.6 1.2 %collective-permute-done.3.refs_3_ = f32[2,2,8,128]{3,2,1,0:T(8,128)S(1)} collective-permute-done((f32[2,2,8,128]{3,2,1,0:T(8,128)}, f32[2,2,8,128]{3,2,1,0:T(8,128)S(1)}, u32[]{:S(2)}, u32[]{:S(2)}) %collective-permute-start.3) | collective-permute-done | bytes 16416 | tf_op jit(solution)/shard_map/ppermute | solution.py:525
  10.9 0.0 collective-permute-done.4.refs_4_
  10.9 0.0 collective-permute-done.1.refs_1_
  10.9 0.0 collective-permute-done.2.refs_2_
  10.9 0.3 collective-permute-done.refs_0_
  11.1 0.0 copy-done
  11.2 0.0 copy-start.1
  11.2 1.4 %copy-done.1 = bf16[4,512,384]{2,1,0:T(8,128)(2,1)S(1)} copy-done((bf16[4,512,384]{2,1,0:T(8,128)(2,1)S(1)}, bf16[4,512,384]{2,1,0:T(8,128)(2,1)}, u32[]{:S(2)}) %copy-start.1) | copy-done | bytes 1572888
  12.6 0.0 copy-start.2
  12.6 1.1 %copy-done.2 = f32[5,128,256]{2,1,0:T(8,128)S(1)} copy-done((f32[5,128,256]{2,1,0:T(8,128)S(1)}, f32[5,128,256]{2,1,0:T(8,128)}, u32[]{:S(2)}) %copy-start.2) | copy-done | bytes 655384
  13.6 12.8 %shard_map.96 = (f32[20,8,256]{2,1,0:T(8,128)S(1)}, f32[20,8,256]{2,1,0:T(8,128)S(1)}, f32[20,8,256]{2,1,0:T(8,128)S(1)}, f32[20,8,256]{2,1,0:T(8,128)S(1)}) custom-call(f32[13,16,256]{2,1,0:T(8,128)S(1)} %collective-permute-done.refs_0_, f32[2,16,8,128]{3,2,1,0:T(8,128)S(1)} %collective-permute-done.1.refs_1_, ...), custom_call_target="tpu_custom_call" | custom-call | tf_op jit(solution)/shard_map/pallas_call | solution.py:453
  26.5 1.7 %collective-permute-start.5 = (f32[20,8,256]{2,1,0:T(8,128)S(1)}, f32[20,8,256]{2,1,0:T(8,128)S(1)}, u32[]{:S(2)}, u32[]{:S(2)}) collective-permute-start(f32[20,8,256]{2,1,0:T(8,128)S(1)} %get-tuple-element.28), channel_id=1, source_target_pairs={{0,1},{1,0},{2,3},{3,2},{4,5},{5,4},{6,7},{7,6},{8,9},{9,8},{10,11... | collective-permute-start | bytes 491528 | tf_op jit(solution)/shard_map/ppermute | solution.py:476
  28.1 0.3 collective-permute-start.6
  28.4 1.6 %collective-permute-start.7 = (f32[20,8,256]{2,1,0:T(8,128)S(1)}, f32[20,8,256]{2,1,0:T(8,128)S(1)}, u32[]{:S(2)}, u32[]{:S(2)}) collective-permute-start(f32[20,8,256]{2,1,0:T(8,128)S(1)} %get-tuple-element.30), channel_id=1, source_target_pairs={{0,3},{1,2},{2,1},{3,0},{4,7},{5,6},{6,5},{7,4},{8,11},{9,10},{10,... | collective-permute-start | bytes 491528 | tf_op jit(solution)/shard_map/ppermute | solution.py:476
  30.0 9.3 %shard_map.98 = (f32[12,8,256]{2,1,0:T(8,128)S(1)}, f32[12,8,256]{2,1,0:T(8,128)S(1)}, f32[12,8,256]{2,1,0:T(8,128)S(1)}, f32[12,8,256]{2,1,0:T(8,128)S(1)}) custom-call(f32[13,16,256]{2,1,0:T(8,128)S(1)} %collective-permute-done.refs_0_, f32[2,16,8,128]{3,2,1,0:T(8,128)S(1)} %collective-permute-done.1.refs_1_, ...), custom_call_target="tpu_custom_call" | custom-call | tf_op jit(solution)/shard_map/pallas_call | solution.py:453
  39.3 2.6 %collective-permute-start.8 = (f32[12,8,256]{2,1,0:T(8,128)S(1)}, f32[12,8,256]{2,1,0:T(8,128)S(1)}, u32[]{:S(2)}, u32[]{:S(2)}) collective-permute-start(f32[12,8,256]{2,1,0:T(8,128)S(1)} %get-tuple-element.32), channel_id=1, source_target_pairs={{0,1},{1,0},{2,3},{3,2},{4,5},{5,4},{6,7},{7,6},{8,9},{9,8},{10,11... | collective-permute-start | bytes 294920 | tf_op jit(solution)/shard_map/ppermute | solution.py:476
  41.9 0.0 collective-permute-start.9
  41.9 0.0 collective-permute-done.5.refs_1_.refs_5_
  41.9 1.5 %collective-permute-start.10 = (f32[12,8,256]{2,1,0:T(8,128)S(1)}, f32[12,8,256]{2,1,0:T(8,128)S(1)}, u32[]{:S(2)}, u32[]{:S(2)}) collective-permute-start(f32[12,8,256]{2,1,0:T(8,128)S(1)} %get-tuple-element.34), channel_id=1, source_target_pairs={{0,3},{1,2},{2,1},{3,0},{4,7},{5,6},{6,5},{7,4},{8,11},{9,10},{10,... | collective-permute-start | bytes 294920 | tf_op jit(solution)/shard_map/ppermute | solution.py:476
  43.4 0.0 collective-permute-done.6.refs_2_.refs_6_
  43.4 0.9 collective-permute-done.7.refs_3_.refs_7_
  44.3 0.4 shard_map.97.before
  44.7 0.0 collective-permute-done.8.refs_1_.refs_9_
  44.7 4.5 %collective-permute-done.9.refs_2_.refs_10_ = f32[12,8,256]{2,1,0:T(8,128)S(1)} collective-permute-done((f32[12,8,256]{2,1,0:T(8,128)S(1)}, f32[12,8,256]{2,1,0:T(8,128)S(1)}, u32[]{:S(2)}, u32[]{:S(2)}) %collective-permute-start.9) | collective-permute-done | bytes 98336 | tf_op jit(solution)/shard_map/ppermute | solution.py:476
  49.2 4.2 %collective-permute-done.10.refs_3_.refs_11_ = f32[12,8,256]{2,1,0:T(8,128)S(1)} collective-permute-done((f32[12,8,256]{2,1,0:T(8,128)S(1)}, f32[12,8,256]{2,1,0:T(8,128)S(1)}, u32[]{:S(2)}, u32[]{:S(2)}) %collective-permute-start.10) | collective-permute-done | bytes 98336 | tf_op jit(solution)/shard_map/ppermute | solution.py:476
  53.4 0.5 shard_map.99
  53.9 0.5 collective-permute-start.13
  54.4 1.2 %collective-permute-start.12 = (f32[32,32]{1,0:T(8,128)S(1)}, f32[32,32]{1,0:T(8,128)S(1)}, u32[]{:S(2)}, u32[]{:S(2)}) collective-permute-start(f32[32,32]{1,0:T(8,128)S(1)} %shard_map.99), channel_id=1, source_target_pairs={{0,2},{1,3},{2,0},{3,1},{4,6},{5,7},{6,4},{7,5},{8,10},{9,11},{10,... | collective-permute-start | bytes 12296 | tf_op jit(solution)/shard_map/ppermute | solution.py:496
  55.6 1.8 %collective-permute-start.11 = (f32[32,32]{1,0:T(8,128)S(1)}, f32[32,32]{1,0:T(8,128)S(1)}, u32[]{:S(2)}, u32[]{:S(2)}) collective-permute-start(f32[32,32]{1,0:T(8,128)S(1)} %shard_map.99), channel_id=1, source_target_pairs={{0,1},{1,0},{2,3},{3,2},{4,5},{5,4},{6,7},{7,6},{8,9},{9,8},{10,11... | collective-permute-start | bytes 12296 | tf_op jit(solution)/shard_map/ppermute | solution.py:496
  57.4 0.5 collective-permute-done.13
  57.9 1.2 %collective-permute-done.12 = f32[32,32]{1,0:T(8,128)S(1)} collective-permute-done((f32[32,32]{1,0:T(8,128)S(1)}, f32[32,32]{1,0:T(8,128)S(1)}, u32[]{:S(2)}, u32[]{:S(2)}) %collective-permute-start.12) | collective-permute-done | bytes 4128 | tf_op jit(solution)/shard_map/ppermute | solution.py:496
  59.0 0.3 collective-permute-done.11
  59.4 0.0 collective-permute-start.14
  59.4 1.2 %collective-permute-done.14 = f32[32,32]{1,0:T(8,128)S(1)} collective-permute-done((f32[32,32]{1,0:T(8,128)S(1)}, f32[32,32]{1,0:T(8,128)S(1)}, u32[]{:S(2)}, u32[]{:S(2)}) %collective-permute-start.14) | collective-permute-done | bytes 4128 | tf_op jit(solution)/shard_map/ppermute | solution.py:496
  60.6 2.0 %collective-permute-start.17 = (f32[32,32]{1,0:T(8,128)S(1)}, f32[32,32]{1,0:T(8,128)S(1)}, u32[]{:S(2)}, u32[]{:S(2)}) collective-permute-start(f32[32,32]{1,0:T(8,128)S(1)} %add.15.refs_0_), channel_id=1, source_target_pairs={{0,24},{1,25},{2,26},{3,27},{4,28},{5,29},{6,30},{7,31},{8,16},{9,... | collective-permute-start | bytes 12296 | tf_op jit(solution)/shard_map/ppermute | solution.py:496
  62.6 1.5 %collective-permute-start.16 = (f32[32,32]{1,0:T(8,128)S(1)}, f32[32,32]{1,0:T(8,128)S(1)}, u32[]{:S(2)}, u32[]{:S(2)}) collective-permute-start(f32[32,32]{1,0:T(8,128)S(1)} %add.15.refs_0_), channel_id=1, source_target_pairs={{0,16},{1,17},{2,18},{3,19},{4,20},{5,21},{6,22},{7,23},{8,24},{9,... | collective-permute-start | bytes 12296 | tf_op jit(solution)/shard_map/ppermute | solution.py:496
  64.1 0.0 collective-permute-start.15
  64.1 1.1 %collective-permute-done.17.refs_3_ = f32[32,32]{1,0:T(8,128)S(1)} collective-permute-done((f32[32,32]{1,0:T(8,128)S(1)}, f32[32,32]{1,0:T(8,128)S(1)}, u32[]{:S(2)}, u32[]{:S(2)}) %collective-permute-start.17) | collective-permute-done | bytes 4128 | tf_op jit(solution)/shard_map/ppermute | solution.py:496
  65.2 1.1 %collective-permute-done.16.refs_2_ = f32[32,32]{1,0:T(8,128)S(1)} collective-permute-done((f32[32,32]{1,0:T(8,128)S(1)}, f32[32,32]{1,0:T(8,128)S(1)}, u32[]{:S(2)}, u32[]{:S(2)}) %collective-permute-start.16) | collective-permute-done | bytes 4128 | tf_op jit(solution)/shard_map/ppermute | solution.py:496
  66.3 1.5 %collective-permute-done.15.refs_1_ = f32[32,32]{1,0:T(8,128)S(1)} collective-permute-done((f32[32,32]{1,0:T(8,128)S(1)}, f32[32,32]{1,0:T(8,128)S(1)}, u32[]{:S(2)}, u32[]{:S(2)}) %collective-permute-start.15) | collective-permute-done | bytes 4128 | tf_op jit(solution)/shard_map/ppermute | solution.py:496
  67.8 3.8 %shard_map.100 = (f32[32,8,256]{2,1,0:T(8,128)S(1)}, f32[32,8,256]{2,1,0:T(8,128)S(1)}, f32[32,8,256]{2,1,0:T(8,128)S(1)}, f32[32,8,256]{2,1,0:T(8,128)S(1)}, f32[32,32]{1,0:T(8,128)}) custom-call(f32[32,32]{1,0:T(8,128)S(1)} %add.15.refs_0_, f32[32,32]{1,0:T(8,128)S(1)} %collective-permute-done.15.refs_1_, f32[32,32]{1,0:T(8,128)S(1)} %collective-permute-done.16.refs_2_, ...), custom_call_target="tpu_custom_call" | custom-call | tf_op jit(solution)/shard_map/pallas_call | solution.py:453
  71.6 0.9 collective-permute-start.18
  72.5 1.0 %collective-permute-start.19 = (f32[32,8,256]{2,1,0:T(8,128)S(1)}, f32[32,8,256]{2,1,0:T(8,128)S(1)}, u32[]{:S(2)}, u32[]{:S(2)}) collective-permute-start(f32[32,8,256]{2,1,0:T(8,128)S(1)} %get-tuple-element.37), channel_id=1, source_target_pairs={{0,2},{1,3},{2,0},{3,1},{4,6},{5,7},{6,4},{7,5},{8,10},{9,11},{10,... | collective-permute-start | bytes 786440 | tf_op jit(solution)/shard_map/ppermute | solution.py:476
  73.5 1.6 %collective-permute-start.20 = (f32[32,8,256]{2,1,0:T(8,128)S(1)}, f32[32,8,256]{2,1,0:T(8,128)S(1)}, u32[]{:S(2)}, u32[]{:S(2)}) collective-permute-start(f32[32,8,256]{2,1,0:T(8,128)S(1)} %get-tuple-element.38), channel_id=1, source_target_pairs={{0,3},{1,2},{2,1},{3,0},{4,7},{5,6},{6,5},{7,4},{8,11},{9,10},{10,... | collective-permute-start | bytes 786440 | tf_op jit(solution)/shard_map/ppermute | solution.py:476
  75.1 6.1 %collective-permute-done.18.refs_1_ = f32[32,8,256]{2,1,0:T(8,128)S(1)} collective-permute-done((f32[32,8,256]{2,1,0:T(8,128)S(1)}, f32[32,8,256]{2,1,0:T(8,128)S(1)}, u32[]{:S(2)}, u32[]{:S(2)}) %collective-permute-start.18) | collective-permute-done | bytes 262176 | tf_op jit(solution)/shard_map/ppermute | solution.py:476
  81.2 10.3 %collective-permute-done.19.refs_2_ = f32[32,8,256]{2,1,0:T(8,128)S(1)} collective-permute-done((f32[32,8,256]{2,1,0:T(8,128)S(1)}, f32[32,8,256]{2,1,0:T(8,128)S(1)}, u32[]{:S(2)}, u32[]{:S(2)}) %collective-permute-start.19) | collective-permute-done | bytes 262176 | tf_op jit(solution)/shard_map/ppermute | solution.py:476
  91.5 5.0 %collective-permute-done.20.refs_3_ = f32[32,8,256]{2,1,0:T(8,128)S(1)} collective-permute-done((f32[32,8,256]{2,1,0:T(8,128)S(1)}, f32[32,8,256]{2,1,0:T(8,128)S(1)}, u32[]{:S(2)}, u32[]{:S(2)}) %collective-permute-start.20) | collective-permute-done | bytes 262176 | tf_op jit(solution)/shard_map/ppermute | solution.py:476
  96.5 1.2 %shard_map.101 = f32[8,128,256]{2,1,0:T(8,128)} custom-call(f32[32,8,256]{2,1,0:T(8,128)S(1)} %get-tuple-element.35.refs_0_, f32[32,8,256]{2,1,0:T(8,128)S(1)} %collective-permute-done.18.refs_1_, f32[32,8,256]{2,1,0:T(8,128)S(1)} %collective-permute-done.19.refs_2_, f32[32,8,256]{2,1,0:T(8,128)S(1)} %collective-permute-done.20.refs_3_), custom_call_target="tpu_custom_call" | custom-call | tf_op jit(solution)/shard_map/pallas_call | solution.py:453
  (2 shorter events, 0.0 us)
Async XLA Ops:
  0.6 10.5 %copy-start = (f32[8,128,256]{2,1,0:T(8,128)S(1)}, f32[8,128,256]{2,1,0:T(8,128)}, u32[]{:S(2)}) copy-start(f32[8,128,256]{2,1,0:T(8,128)} %refs_5_.5) | copy-start | bytes 3145732
  3.7 7.4 %collective-permute-start = (f32[13,16,256]{2,1,0:T(8,128)}, f32[13,16,256]{2,1,0:T(8,128)S(1)}, u32[]{:S(2)}, u32[]{:S(2)}) collective-permute-start(f32[13,16,256]{2,1,0:T(8,128)} %get-tuple-element.21), channel_id=1, source_target_pairs={{0,16},{16,0},{1,17},{17,1},{2,18},{18,2},{3,19},{19,3},{4,20},{20... | collective-permute-start | bytes 638984 | tf_op jit(solution)/shard_map/ppermute | solution.py:525
  4.3 6.6 %collective-permute-start.1 = (f32[2,16,8,128]{3,2,1,0:T(8,128)}, f32[2,16,8,128]{3,2,1,0:T(8,128)S(1)}, u32[]{:S(2)}, u32[]{:S(2)}) collective-permute-start(f32[2,16,8,128]{3,2,1,0:T(8,128)} %get-tuple-element.22), channel_id=1, source_target_pairs={{0,4},{8,12},{4,0},{12,8},{1,5},{9,13},{5,1},{13,9},{2,6},{10,14},... | collective-permute-start | bytes 393224 | tf_op jit(solution)/shard_map/ppermute | solution.py:525
  4.3 6.6 %collective-permute-start.2 = (f32[2,16,8,128]{3,2,1,0:T(8,128)}, f32[2,16,8,128]{3,2,1,0:T(8,128)S(1)}, u32[]{:S(2)}, u32[]{:S(2)}) collective-permute-start(f32[2,16,8,128]{3,2,1,0:T(8,128)} %get-tuple-element.23), channel_id=1, source_target_pairs={{4,8},{8,4},{5,9},{9,5},{6,10},{10,6},{7,11},{11,7},{20,24},{24,20... | collective-permute-start | bytes 393224 | tf_op jit(solution)/shard_map/ppermute | solution.py:525
  4.9 5.9 %collective-permute-start.3 = (f32[2,2,8,128]{3,2,1,0:T(8,128)}, f32[2,2,8,128]{3,2,1,0:T(8,128)S(1)}, u32[]{:S(2)}, u32[]{:S(2)}) collective-permute-start(f32[2,2,8,128]{3,2,1,0:T(8,128)} %get-tuple-element.24), channel_id=1, source_target_pairs={{0,20},{8,28},{4,16},{12,24},{16,4},{24,12},{20,0},{28,8},{1,21},{... | collective-permute-start | bytes 49160 | tf_op jit(solution)/shard_map/ppermute | solution.py:525
  9.0 1.9 %collective-permute-start.4 = (f32[2,2,8,128]{3,2,1,0:T(8,128)}, f32[2,2,8,128]{3,2,1,0:T(8,128)S(1)}, u32[]{:S(2)}, u32[]{:S(2)}) collective-permute-start(f32[2,2,8,128]{3,2,1,0:T(8,128)} %get-tuple-element.25), channel_id=1, source_target_pairs={{4,24},{8,20},{20,8},{24,4},{5,25},{9,21},{21,9},{25,5},{6,26},{10... | collective-permute-start | bytes 49160 | tf_op jit(solution)/shard_map/ppermute | solution.py:525
  11.2 1.4 %copy-start.1 = (bf16[4,512,384]{2,1,0:T(8,128)(2,1)S(1)}, bf16[4,512,384]{2,1,0:T(8,128)(2,1)}, u32[]{:S(2)}) copy-start(bf16[4,512,384]{2,1,0:T(8,128)(2,1)} %constant.2.clone.refs_7_) | copy-start | bytes 4718596
  12.6 1.1 %copy-start.2 = (f32[5,128,256]{2,1,0:T(8,128)S(1)}, f32[5,128,256]{2,1,0:T(8,128)}, u32[]{:S(2)}) copy-start(f32[5,128,256]{2,1,0:T(8,128)} %get-tuple-element.26.refs_6_) | copy-start | bytes 1966084
  26.5 15.4 %collective-permute-start.5 = (f32[20,8,256]{2,1,0:T(8,128)S(1)}, f32[20,8,256]{2,1,0:T(8,128)S(1)}, u32[]{:S(2)}, u32[]{:S(2)}) collective-permute-start(f32[20,8,256]{2,1,0:T(8,128)S(1)} %get-tuple-element.28), channel_id=1, source_target_pairs={{0,1},{1,0},{2,3},{3,2},{4,5},{5,4},{6,7},{7,6},{8,9},{9,8},{10,11... | collective-permute-start | bytes 491528 | tf_op jit(solution)/shard_map/ppermute | solution.py:476
  28.1 15.3 %collective-permute-start.6 = (f32[20,8,256]{2,1,0:T(8,128)S(1)}, f32[20,8,256]{2,1,0:T(8,128)S(1)}, u32[]{:S(2)}, u32[]{:S(2)}) collective-permute-start(f32[20,8,256]{2,1,0:T(8,128)S(1)} %get-tuple-element.29), channel_id=1, source_target_pairs={{0,2},{1,3},{2,0},{3,1},{4,6},{5,7},{6,4},{7,5},{8,10},{9,11},{10,... | collective-permute-start | bytes 491528 | tf_op jit(solution)/shard_map/ppermute | solution.py:476
  28.4 15.9 %collective-permute-start.7 = (f32[20,8,256]{2,1,0:T(8,128)S(1)}, f32[20,8,256]{2,1,0:T(8,128)S(1)}, u32[]{:S(2)}, u32[]{:S(2)}) collective-permute-start(f32[20,8,256]{2,1,0:T(8,128)S(1)} %get-tuple-element.30), channel_id=1, source_target_pairs={{0,3},{1,2},{2,1},{3,0},{4,7},{5,6},{6,5},{7,4},{8,11},{9,10},{10,... | collective-permute-start | bytes 491528 | tf_op jit(solution)/shard_map/ppermute | solution.py:476
  39.3 5.4 %collective-permute-start.8 = (f32[12,8,256]{2,1,0:T(8,128)S(1)}, f32[12,8,256]{2,1,0:T(8,128)S(1)}, u32[]{:S(2)}, u32[]{:S(2)}) collective-permute-start(f32[12,8,256]{2,1,0:T(8,128)S(1)} %get-tuple-element.32), channel_id=1, source_target_pairs={{0,1},{1,0},{2,3},{3,2},{4,5},{5,4},{6,7},{7,6},{8,9},{9,8},{10,11... | collective-permute-start | bytes 294920 | tf_op jit(solution)/shard_map/ppermute | solution.py:476
  41.9 7.3 %collective-permute-start.9 = (f32[12,8,256]{2,1,0:T(8,128)S(1)}, f32[12,8,256]{2,1,0:T(8,128)S(1)}, u32[]{:S(2)}, u32[]{:S(2)}) collective-permute-start(f32[12,8,256]{2,1,0:T(8,128)S(1)} %get-tuple-element.33), channel_id=1, source_target_pairs={{0,2},{1,3},{2,0},{3,1},{4,6},{5,7},{6,4},{7,5},{8,10},{9,11},{10,... | collective-permute-start | bytes 294920 | tf_op jit(solution)/shard_map/ppermute | solution.py:476
  41.9 11.6 %collective-permute-start.10 = (f32[12,8,256]{2,1,0:T(8,128)S(1)}, f32[12,8,256]{2,1,0:T(8,128)S(1)}, u32[]{:S(2)}, u32[]{:S(2)}) collective-permute-start(f32[12,8,256]{2,1,0:T(8,128)S(1)} %get-tuple-element.34), channel_id=1, source_target_pairs={{0,3},{1,2},{2,1},{3,0},{4,7},{5,6},{6,5},{7,4},{8,11},{9,10},{10,... | collective-permute-start | bytes 294920 | tf_op jit(solution)/shard_map/ppermute | solution.py:476
  53.9 4.0 %collective-permute-start.13 = (f32[32,32]{1,0:T(8,128)S(1)}, f32[32,32]{1,0:T(8,128)S(1)}, u32[]{:S(2)}, u32[]{:S(2)}) collective-permute-start(f32[32,32]{1,0:T(8,128)S(1)} %shard_map.99), channel_id=1, source_target_pairs={{0,3},{1,2},{2,1},{3,0},{4,7},{5,6},{6,5},{7,4},{8,11},{9,10},{10,... | collective-permute-start | bytes 12296 | tf_op jit(solution)/shard_map/ppermute | solution.py:496
  54.4 4.6 %collective-permute-start.12 = (f32[32,32]{1,0:T(8,128)S(1)}, f32[32,32]{1,0:T(8,128)S(1)}, u32[]{:S(2)}, u32[]{:S(2)}) collective-permute-start(f32[32,32]{1,0:T(8,128)S(1)} %shard_map.99), channel_id=1, source_target_pairs={{0,2},{1,3},{2,0},{3,1},{4,6},{5,7},{6,4},{7,5},{8,10},{9,11},{10,... | collective-permute-start | bytes 12296 | tf_op jit(solution)/shard_map/ppermute | solution.py:496
  55.6 3.7 %collective-permute-start.11 = (f32[32,32]{1,0:T(8,128)S(1)}, f32[32,32]{1,0:T(8,128)S(1)}, u32[]{:S(2)}, u32[]{:S(2)}) collective-permute-start(f32[32,32]{1,0:T(8,128)S(1)} %shard_map.99), channel_id=1, source_target_pairs={{0,1},{1,0},{2,3},{3,2},{4,5},{5,4},{6,7},{7,6},{8,9},{9,8},{10,11... | collective-permute-start | bytes 12296 | tf_op jit(solution)/shard_map/ppermute | solution.py:496
  59.4 1.2 %collective-permute-start.14 = (f32[32,32]{1,0:T(8,128)S(1)}, f32[32,32]{1,0:T(8,128)S(1)}, u32[]{:S(2)}, u32[]{:S(2)}) collective-permute-start(f32[32,32]{1,0:T(8,128)S(1)} %add_add_fusion), channel_id=1, source_target_pairs={{0,4},{1,5},{2,6},{3,7},{4,0},{5,1},{6,2},{7,3},{8,12},{9,13},{10,... | collective-permute-start | bytes 12296 | tf_op jit(solution)/shard_map/ppermute | solution.py:496
  60.6 4.6 %collective-permute-start.17 = (f32[32,32]{1,0:T(8,128)S(1)}, f32[32,32]{1,0:T(8,128)S(1)}, u32[]{:S(2)}, u32[]{:S(2)}) collective-permute-start(f32[32,32]{1,0:T(8,128)S(1)} %add.15.refs_0_), channel_id=1, source_target_pairs={{0,24},{1,25},{2,26},{3,27},{4,28},{5,29},{6,30},{7,31},{8,16},{9,... | collective-permute-start | bytes 12296 | tf_op jit(solution)/shard_map/ppermute | solution.py:496
  62.6 3.7 %collective-permute-start.16 = (f32[32,32]{1,0:T(8,128)S(1)}, f32[32,32]{1,0:T(8,128)S(1)}, u32[]{:S(2)}, u32[]{:S(2)}) collective-permute-start(f32[32,32]{1,0:T(8,128)S(1)} %add.15.refs_0_), channel_id=1, source_target_pairs={{0,16},{1,17},{2,18},{3,19},{4,20},{5,21},{6,22},{7,23},{8,24},{9,... | collective-permute-start | bytes 12296 | tf_op jit(solution)/shard_map/ppermute | solution.py:496
  64.1 3.7 %collective-permute-start.15 = (f32[32,32]{1,0:T(8,128)S(1)}, f32[32,32]{1,0:T(8,128)S(1)}, u32[]{:S(2)}, u32[]{:S(2)}) collective-permute-start(f32[32,32]{1,0:T(8,128)S(1)} %add.15.refs_0_), channel_id=1, source_target_pairs={{0,8},{1,9},{2,10},{3,11},{4,12},{5,13},{6,14},{7,15},{8,0},{9,1},... | collective-permute-start | bytes 12296 | tf_op jit(solution)/shard_map/ppermute | solution.py:496
  71.6 9.6 %collective-permute-start.18 = (f32[32,8,256]{2,1,0:T(8,128)S(1)}, f32[32,8,256]{2,1,0:T(8,128)S(1)}, u32[]{:S(2)}, u32[]{:S(2)}) collective-permute-start(f32[32,8,256]{2,1,0:T(8,128)S(1)} %get-tuple-element.36), channel_id=1, source_target_pairs={{0,1},{1,0},{2,3},{3,2},{4,5},{5,4},{6,7},{7,6},{8,9},{9,8},{10,11... | collective-permute-start | bytes 786440 | tf_op jit(solution)/shard_map/ppermute | solution.py:476
  72.5 19.0 %collective-permute-start.19 = (f32[32,8,256]{2,1,0:T(8,128)S(1)}, f32[32,8,256]{2,1,0:T(8,128)S(1)}, u32[]{:S(2)}, u32[]{:S(2)}) collective-permute-start(f32[32,8,256]{2,1,0:T(8,128)S(1)} %get-tuple-element.37), channel_id=1, source_target_pairs={{0,2},{1,3},{2,0},{3,1},{4,6},{5,7},{6,4},{7,5},{8,10},{9,11},{10,... | collective-permute-start | bytes 786440 | tf_op jit(solution)/shard_map/ppermute | solution.py:476
  73.5 23.0 %collective-permute-start.20 = (f32[32,8,256]{2,1,0:T(8,128)S(1)}, f32[32,8,256]{2,1,0:T(8,128)S(1)}, u32[]{:S(2)}, u32[]{:S(2)}) collective-permute-start(f32[32,8,256]{2,1,0:T(8,128)S(1)} %get-tuple-element.38), channel_id=1, source_target_pairs={{0,3},{1,2},{2,1},{3,0},{4,7},{5,6},{6,5},{7,4},{8,11},{9,10},{10,... | collective-permute-start | bytes 786440 | tf_op jit(solution)/shard_map/ppermute | solution.py:476

commit v3 on v2

--- a/solution.py
+++ b/solution.py
@@ -2,7 +2,6 @@
 
 import jax
 import jax.numpy as jnp
-import numpy as np
 from jax import lax
 from jax.experimental import pallas as pl
 from jax.experimental.pallas import tpu as pltpu
@@ -18,12 +17,13 @@
 BANDS = 4
 SPANS = LANES // BANDS
 PLANES = 8
+SWAPS = (0, 2, 3, 1)
 FIELDS = 5
 F32 = jnp.float32
 BF16 = jnp.bfloat16
 WEIGHTS = ((4.0, 1.0), (1.0, 4.0))
 PARTS = 2
-FIRST_ROWS = 80
+FIRST_ROWS = 88
 
 
 def iota(shape, dim):
@@ -32,6 +32,15 @@
 
 def roll(value, shift):
     return pltpu.roll(value, shift % LANES, 1)
+
+
+def put_fields(out, velocity, viscosity, drag, weight, mask, grounded):
+    friction = drag[...] * grounded[...].astype(F32)
+    out[0] = friction * velocity[0]
+    out[1] = friction * velocity[1]
+    out[2] = friction
+    out[3] = viscosity[...]
+    out[4] = weight[...] * mask[...].astype(F32)
 
 
 def pack(counts, *refs):
@@ -41,24 +50,23 @@
     row_out, refs = refs[:count_x], refs[count_x:]
     col_out, refs = refs[:count_y], refs[count_y:]
     corner_out, refs = refs[: count_x * count_y], refs[count_x * count_y :]
-    held, sems = refs[:7], refs[7]
+    held, dirs, sems = refs[:6], *refs[6:]
     copies = [
         pltpu.make_async_copy(source, target, sems.at[i])
-        for i, (source, target) in enumerate(zip(sources, held))
+        for i, (source, target) in enumerate(zip(sources[1:], held))
     ]
+    late = [
+        pltpu.make_async_copy(sources[0].at[p], dirs.at[p], sems.at[len(copies) + p])
+        for p in range(PLANES)
+    ]
+    for copy in copies + late:
+        copy.start()
     for copy in copies:
-        copy.start()
-    for copy in copies[1:]:
         copy.wait()
-    dirs, velocity, viscosity, drag, weight, mask, grounded = held
-    rows, cols = viscosity.shape
-    friction = drag[...] * grounded[...].astype(F32)
-    fields[0] = friction * velocity[0]
-    fields[1] = friction * velocity[1]
-    fields[2] = friction
-    fields[3] = viscosity[...]
-    fields[4] = weight[...] * mask[...].astype(F32)
-    copies[0].wait()
+    rows, cols = dirs.shape[1:]
+    put_fields(fields, *held)
+    for copy in late:
+        copy.wait()
 
     for pairing, out in enumerate(row_out):
         send_last = lax.axis_index("gx") % 2 == pairing
@@ -111,15 +119,23 @@
     return out
 
 
-def band_places(cols, wide):
-    slot = np.arange(LANES) % PAD
-    column = np.concatenate([np.arange(cols) + PAD, slot, slot + cols + PAD])
-    span, j = column // wide, column % wide
-    out = np.zeros((BANDS, column.size, pl.cdiv(wide, BANDS) * LANES), np.float32)
+def line_up(dirs, fields, lines, places):
+    rows, cols = dirs.shape[1:]
+    for g in range(rows // 8):
+        at = slice(8 * g, 8 * g + 8)
+        lines[at, :PLANES, :] = jnp.swapaxes(dirs[:, at, :], 0, 1)
+        stack = [fields[k, at, :] for k in range(FIELDS)]
+        stack += [jnp.zeros((8, cols), F32)] * (PLANES - FIELDS)
+        lines[at, PLANES:, :] = jnp.swapaxes(jnp.stack(stack), 0, 1)
+    wide = pl.cdiv(cols + 2 * PAD, SPANS)
+    k, lane = (iota(places.shape[1:], dim) for dim in (0, 1))
+    slot = k % PAD + jnp.where(k < cols + LANES, 0, cols + PAD)
+    column = jnp.where(k < cols, k + PAD, slot)
+    tile, block, span = lane // LANES, (lane // SPANS) % BANDS, lane % SPANS
     for band in range(BANDS):
-        lane = LANES * (j // BANDS) + SPANS * ((j + band) % BANDS) + span
-        out[band, np.arange(column.size), lane] = 1.0
-    return out.astype(BF16)
+        j = BANDS * tile + (block + BANDS - band) % BANDS
+        here = (column == wide * span + j) & (j < wide)
+        places[band] = jnp.where(here, 1.0, 0.0).astype(BF16)
 
 
 def split_dot(value, places, transposed=False):
@@ -144,9 +160,9 @@
     got_rows, refs = refs[:count_x], refs[count_x:]
     got_cols, refs = refs[:count_y], refs[count_y:]
     got_corners, refs = refs[: count_x * count_y], refs[count_x * count_y :]
-    dirs, fields, places, *refs = refs
+    own_lines, places, *refs = refs
     *outs, halo_rows, halo_cols, lined, turned, planes, coeffs, extras, base, ping, pong = refs
-    rows, cols = dirs.shape[1:]
+    rows, _, cols = own_lines.shape
     tall = lined.shape[0]
     over = (tall - row_count) // 2
     high = tall // BANDS
@@ -187,25 +203,26 @@
         for i in range(high):
             body(i)
 
-    for q, (source, first, count) in enumerate(((dirs, 0, PLANES), (fields, PLANES, FIELDS))):
+    for q, (first, count) in enumerate(((0, PLANES), (PLANES, FIELDS))):
         for g in range(groups):
             lines_of = [8 * g + d - PAD - (row_first - over) for d in range(8)]
             if lines_of[-1] < 0 or lines_of[0] >= tall:
                 continue
             inner = edge <= g < groups - edge
-            side, at = (0, g) if g < edge else (1, g - groups + edge)
-            stack = []
-            for p in range(PLANES):
-                if p >= count:
-                    stack.append(jnp.zeros((8, cols), F32))
-                elif inner:
-                    stack.append(source[p, 8 * (g - edge) : 8 * (g - edge) + 8, :])
-                else:
-                    stack.append(halo_rows[side, first + p, 8 * at : 8 * at + 8, :])
-            lines = jnp.swapaxes(jnp.stack(stack), 0, 1)
+            if not inner:
+                side, at = (0, g) if g < edge else (1, g - groups + edge)
+                stack = [
+                    halo_rows[side, first + p, 8 * at : 8 * at + 8, :] for p in range(count)
+                ]
+                stack += [jnp.zeros((8, cols), F32)] * (PLANES - count)
+                lines = jnp.swapaxes(jnp.stack(stack), 0, 1)
             for d, line in enumerate(lines_of):
                 if 0 <= line < tall:
-                    lined[line, :, :cols] = lines[d]
+                    lined[line, :, :cols] = (
+                        own_lines[8 * (g - edge) + d, PLANES * q : PLANES * q + PLANES, :]
+                        if inner
+                        else lines[d]
+                    )
                     for side_y in range(2):
                         begin = cols + LANES * side_y
                         lined[line, :, begin : begin + LANES] = jnp.where(
@@ -276,7 +293,7 @@
         weigh(i, i - 1, i + 1, False, False)
         return 0
 
-    lax.fori_loop(1, high - 1, weigh_inner, 0, unroll=4)
+    lax.fori_loop(1, high - 1, weigh_inner, 0, unroll=2)
 
     def put(ref, m, i, j, value, edges=True):
         ref[m, i + 1, j] = value
@@ -297,20 +314,20 @@
     over_rows(start)
 
     def sweep(source, scale, store):
-        def body(i):
-            for m in range(2):
-                mids = [source[m, i + 1, j] for j in range(wide)]
+        for m in range(2):
+            above, mids = ([source[m, i, j] for j in range(wide)] for i in range(2))
+            for i in range(high):
+                below = [source[m, i + 2, j] for j in range(wide)]
                 before = [roll(mids[-1], 1)] + mids[:-1]
                 after = mids[1:] + [roll(mids[0], -1)]
                 for j in range(wide):
                     e, w, n, s = (
                         coeffs[scale, i, j, 4 * m + d : 4 * m + d + 1, :] for d in range(4)
                     )
-                    along_x = e * source[m, i + 2, j] + w * source[m, i, j]
+                    along_x = e * below[j] + w * above[j]
                     along_y = n * after[j] + s * before[j]
                     store(m, i, j, mids[j] + (along_x + along_y))
-
-        over_rows(body)
+                above, mids = mids, below
 
     def to(ref):
         return lambda m, i, j, value: put(ref, m, i, j, value)
@@ -350,7 +367,7 @@
         lined[pl.ds(high * b, high), :, :cols] = value.reshape(high, 8, cols)
 
     part = row_count // len(outs)
-    for k, out in enumerate(outs):
+    for k, out in zip(SWAPS, outs):
         out[...] = lined[pl.ds(over + part * (lax.axis_index("dir") ^ k), part), :, :cols]
 
 
@@ -376,9 +393,15 @@
 
 
 def by_device(value, me, held):
-    for k in range(value.shape[0] // 8):
-        held[pl.ds(pl.multiple_of(8 * (me ^ k), 8), 8), :] = value[8 * k : 8 * k + 8]
+    for n, k in enumerate(SWAPS):
+        held[pl.ds(pl.multiple_of(8 * (me ^ k), 8), 8), :] = value[8 * n : 8 * n + 8]
     return held[...]
+
+
+def to_device(value, me, held):
+    held[...] = value
+    blocks = [held[pl.ds(pl.multiple_of(8 * (me ^ k), 8), 8), :] for k in SWAPS]
+    return jnp.concatenate(blocks, axis=0)
 
 
 def gram_rest(before, *refs):
@@ -405,32 +428,36 @@
     return work / jnp.sqrt(pivots), lane, row_of
 
 
-def basis_of(cells, pieces, terms, *refs):
+def form_basis(inverse, pieces, outs):
+    count = len(SWAPS)
+    high, low = halves(inverse)
+    both = jnp.concatenate([high, low], axis=0)
+    size = inverse.shape[0]
+    base = 0
+    for piece in range(len(pieces) // count):
+        parts = pieces[count * piece : count * piece + count]
+        for r in range(parts[0].shape[0]):
+            value_high, value_low = halves(jnp.concatenate([part[r] for part in parts], axis=0))
+            first = jnp.dot(both, value_high, preferred_element_type=F32)
+            second = jnp.dot(high, value_low, preferred_element_type=F32)
+            total = first[:size] + (first[size:] + second)
+            for n, out in enumerate(outs):
+                out[base + r] = total[8 * n : 8 * n + 8]
+        base += parts[0].shape[0]
+
+
+def basis_of(cells, terms, *refs):
     sums, refs = refs[:terms], refs[terms:]
-    own, refs = refs[: 4 * pieces], refs[4 * pieces :]
-    *outs, upper, held = refs
-    count = len(outs)
+    count = len(SWAPS)
+    pieces, outs, (upper, held) = refs[: -count - 2], refs[-count - 2 : -2], refs[-2:]
     size = sums[0].shape[0]
     gram = functools.reduce(lambda a, b: a + b, [term[...] for term in sums])
     work, lane, row_of = factor(gram / cells, size)
     upper[...] = jnp.where(lane >= row_of, work, 0.0)[:, :size]
-    inverse = work[:, size : 2 * size]
+    value = work[:, size : 2 * size]
     for _ in range(2):
-        inverse = by_device(inverse, lax.axis_index("dir"), held).T
-    high, low = halves(inverse)
-    both = jnp.concatenate([high, low], axis=0)
-    base = 0
-    for piece in range(pieces):
-        parts = own[count * piece : count * piece + count]
-        for r in range(parts[0].shape[0]):
-            value = jnp.concatenate([part[r] for part in parts], axis=0)
-            value_high, value_low = halves(value)
-            first = jnp.dot(both, value_high, preferred_element_type=F32)
-            second = jnp.dot(high, value_low, preferred_element_type=F32)
-            total = first[:size] + (first[size:] + second)
-            for k, out in enumerate(outs):
-                out[base + r] = total[8 * k : 8 * k + 8]
-        base += parts[0].shape[0]
+        value = to_device(value, lax.axis_index("dir"), held).T
+    form_basis(value, pieces, outs)
 
 
 def assemble(spans, *refs):
@@ -439,7 +466,7 @@
     base = 0
     for first, rows in spans:
         share = rows // count
-        for k, part in enumerate(parts):
+        for k, part in zip(SWAPS, parts):
             at = first + share * (lax.axis_index("dir") ^ k)
             held[pl.ds(at, share)] = part[base : base + share]
         base += share
@@ -449,7 +476,9 @@
 
 def call(kernel, outs, *args, scratch=(), limit=8, space=pltpu.VMEM):
     vmem = pl.BlockSpec(memory_space=pltpu.VMEM)
-    shapes = [jax.ShapeDtypeStruct(shape, F32) for shape in outs]
+    shapes = [
+        jax.ShapeDtypeStruct(shape, F32) if isinstance(shape, tuple) else shape for shape in outs
+    ]
     return pl.pallas_call(
         kernel,
         out_shape=shapes,
@@ -513,7 +542,9 @@
         + [(2, rows // 8, 8, LANES)] * counts[1]
         + [(2, PAD // 8, 8, LANES)] * (counts[0] * counts[1]),
         *args,
-        scratch=[pltpu.VMEM(a.shape, a.dtype) for a in args] + [pltpu.SemaphoreType.DMA((7,))],
+        scratch=[pltpu.VMEM(a.shape, a.dtype) for a in args[1:]]
+        + [directions.shape]
+        + [pltpu.SemaphoreType.DMA((len(args) - 1 + PLANES,))],
         space=pl.ANY,
         limit=60,
     )
@@ -528,7 +559,16 @@
     wide = pl.cdiv(cols + 2 * PAD, SPANS)
     groups = (rows + 2 * PAD) // 8
     lanes_out = pl.cdiv(wide, BANDS) * LANES
-    places = band_places(cols, wide)
+    own_lines, places = call(
+        line_up,
+        [
+            (rows, 2 * PLANES, cols),
+            jax.ShapeDtypeStruct((BANDS, cols + 2 * LANES, lanes_out), BF16),
+        ],
+        directions,
+        fields,
+        limit=24,
+    )
     spans = [(0, FIRST_ROWS * rows // 128), (FIRST_ROWS * rows // 128, rows - FIRST_ROWS * rows // 128)]
     pieces = []
     for span in spans:
@@ -539,8 +579,7 @@
             functools.partial(solve, counts, span),
             [(span[1] // across, own, cols)] * across,
             *got,
-            directions,
-            fields,
+            own_lines,
             places,
             scratch=[
                 (2, PLANES + FIELDS, PAD, cols),
@@ -557,7 +596,7 @@
             limit=32,
         )
         pieces.append(
-            [own_parts[0]] + [swap_bit(own_parts[k], "dir", k) for k in range(1, across)]
+            [own_parts[0]] + [swap_bit(p, "dir", k) for p, k in zip(own_parts[1:], SWAPS[1:])]
         )
     total = own * across
     (gram,) = call(gram_first, [(total, total)], *pieces[0])
@@ -566,15 +605,16 @@
     )
     grams = partial_sums(gram)
     count = rows * cols * lax.axis_size("gx") * lax.axis_size("gy")
+    part = (rows // across, own, cols)
     *parts, upper = call(
-        functools.partial(basis_of, float(count), len(pieces), len(grams)),
-        [(rows // across, own, cols)] * across + [(total, total)],
+        functools.partial(basis_of, float(count), len(grams)),
+        [part] * across + [(total, total)],
         *grams,
         *pieces[0],
         *pieces[1],
         scratch=[(total, total)],
     )
-    parts = [parts[0]] + [swap_bit(parts[k], "dir", k) for k in range(1, across)]
+    parts = [parts[0]] + [swap_bit(p, "dir", k) for p, k in zip(parts[1:], SWAPS[1:])]
     (basis,) = call(
         functools.partial(assemble, spans),
         [(own, rows, cols)],

time: 99 us -> 94.5 us (0.955)
  waiting for transfers between devices: 39.4 us -> 34.9 us
  starting transfers between devices: 24.1 us -> 27 us
  local copies, waits for them, and re-layouts: 2.5 us -> 1.09 us
    ppermute x9, starting transfers between devices: 11.2 us -> 14.1 us  [swap_bit(): return lax.ppermute(value, axis, [(i, i ^ bit) for i in range(count)])]
    ppermute x9, waiting for transfers between devices: 31 us -> 29.2 us  [swap_bit(): return lax.ppermute(value, axis, [(i, i ^ bit) for i in range(count)])]
    ppermute x5, waiting for transfers between devices: 1.5 us -> 0.01 us  [on_device(): lax.ppermute(m, axis, pairs)]
    unnamed x6 -> x4, local copies, waits for them, and re-layouts: 2.5 us -> 1.09 us
    ppermute x7, waiting for transfers between devices: 6.88 us -> 5.66 us  [partial_sums(): lax.ppermute(value, axes, [(i, i ^ mask) for i in range(count)])]
    pallas_call x7 -> x8, Pallas kernels: 31 us -> 30.5 us  [call(): pl.pallas_call(kernel, out_shape=shapes, in_specs=[pl.BlockSpec(memory_sp...]
  transfers between devices with their start and end apart: 21 -> 21, of which waited for: 15 -> 10; matrix products, arithmetic and copies ran while one was open for 0% -> 0% of each run, Pallas kernels for 10% -> 10%
where the time goes in v3:
time: 94.5 us; the launch traced here: 94.2 us
  waiting for transfers between devices  34.9 us (37%)
  Pallas kernels  30.5 us (32%)
  starting transfers between devices  27 us (29%)
  local copies, waits for them, and re-layouts  1.09 us (1%)
    pallas_call x8, Pallas kernels, call(): pl.pallas_call(kernel, out_shape=shapes, in_specs=[pl.BlockSpec(memory_sp...  30.5 us
    ppermute x9, waiting for transfers between devices, swap_bit(): return lax.ppermute(value, axis, [(i, i ^ bit) for i in range(count)])  29.2 us
    ppermute x9, starting transfers between devices, swap_bit(): return lax.ppermute(value, axis, [(i, i ^ bit) for i in range(count)])  14.1 us
    ppermute x7, starting transfers between devices, partial_sums(): lax.ppermute(value, axes, [(i, i ^ mask) for i in range(count)])  6.99 us
    ppermute x5, starting transfers between devices, on_device(): lax.ppermute(m, axis, pairs)  5.92 us
    ppermute x7, waiting for transfers between devices, partial_sums(): lax.ppermute(value, axes, [(i, i ^ mask) for i in range(count)])  5.66 us
  transfers between devices with their start and end apart: 21, of which 10 were waited for; matrix products, arithmetic and copies ran while one was open for 0% of the time, Pallas kernels for 10%

profile of v3, /device:TPU:20, one launch (start us, length us, event | category | flops | bytes accessed | tf_op | source)
XLA Modules:
  0.0 94.2 jit_solution(16958700370154868001)
XLA Ops:
  0.6 0.0 copy-start
  0.6 3.1 %shard_map.86 = (f32[5,128,256]{2,1,0:T(8,128)}, f32[13,16,256]{2,1,0:T(8,128)}, f32[2,16,8,128]{3,2,1,0:T(8,128)}, f32[2,16,8,128]{3,2,1,0:T(8,128)}, f32[2,2,8...) custom-call(f32[8,128,256]{2,1,0:T(8,128)} %dirs.1, f32[2,128,256]{2,1,0:T(8,128)} %refs_1_.1, f32[128,256]{1,0:T(8,128)} %refs_2_.1, ...), custom_call_target="tpu_custom_call" | custom-call | tf_op jit(solution)/shard_map/pallas_call | solution.py:482
  3.8 0.6 collective-permute-start
  4.3 0.0 collective-permute-start.1
  4.3 0.7 collective-permute-start.2
  5.0 4.0 %collective-permute-start.3 = (f32[2,2,8,128]{3,2,1,0:T(8,128)}, f32[2,2,8,128]{3,2,1,0:T(8,128)S(1)}, u32[]{:S(2)}, u32[]{:S(2)}) collective-permute-start(f32[2,2,8,128]{3,2,1,0:T(8,128)} %get-tuple-element.26), channel_id=1, source_target_pairs={{0,20},{8,28},{4,16},{12,24},{16,4},{24,12},{20,0},{28,8},{1,21},{... | collective-permute-start | bytes 49160 | tf_op jit(solution)/shard_map/ppermute | solution.py:556
  9.0 0.7 collective-permute-start.4
  9.7 0.0 copy-done
  9.7 0.0 copy-start.1
  9.7 1.1 %copy-done.1 = f32[5,128,256]{2,1,0:T(8,128)S(1)} copy-done((f32[5,128,256]{2,1,0:T(8,128)S(1)}, f32[5,128,256]{2,1,0:T(8,128)}, u32[]{:S(2)}) %copy-start.1) | copy-done | bytes 655384
  10.8 0.7 shard_map.87
  11.5 0.0 collective-permute-done.3.refs_3_
  11.5 0.0 collective-permute-done.4.refs_4_
  11.5 0.0 collective-permute-done.1.refs_1_
  11.5 0.0 collective-permute-done.2.refs_2_
  11.5 0.0 collective-permute-done.refs_0_
  11.6 13.1 %shard_map.88 = (f32[22,8,256]{2,1,0:T(8,128)S(1)}, f32[22,8,256]{2,1,0:T(8,128)S(1)}, f32[22,8,256]{2,1,0:T(8,128)S(1)}, f32[22,8,256]{2,1,0:T(8,128)S(1)}) custom-call(f32[13,16,256]{2,1,0:T(8,128)S(1)} %collective-permute-done.refs_0_, f32[2,16,8,128]{3,2,1,0:T(8,128)S(1)} %collective-permute-done.1.refs_1_, ...), custom_call_target="tpu_custom_call" | custom-call | tf_op jit(solution)/shard_map/pallas_call | solution.py:482
  24.7 0.4 collective-permute-start.5
  25.1 2.7 %collective-permute-start.6 = (f32[22,8,256]{2,1,0:T(8,128)S(1)}, f32[22,8,256]{2,1,0:T(8,128)S(1)}, u32[]{:S(2)}, u32[]{:S(2)}) collective-permute-start(f32[22,8,256]{2,1,0:T(8,128)S(1)} %get-tuple-element.33), channel_id=1, source_target_pairs={{0,3},{1,2},{2,1},{3,0},{4,7},{5,6},{6,5},{7,4},{8,11},{9,10},{10,... | collective-permute-start | bytes 540680 | tf_op jit(solution)/shard_map/ppermute | solution.py:505
  27.8 1.3 %collective-permute-start.7 = (f32[22,8,256]{2,1,0:T(8,128)S(1)}, f32[22,8,256]{2,1,0:T(8,128)S(1)}, u32[]{:S(2)}, u32[]{:S(2)}) collective-permute-start(f32[22,8,256]{2,1,0:T(8,128)S(1)} %get-tuple-element.34), channel_id=1, source_target_pairs={{0,1},{1,0},{2,3},{3,2},{4,5},{5,4},{6,7},{7,6},{8,9},{9,8},{10,11... | collective-permute-start | bytes 540680 | tf_op jit(solution)/shard_map/ppermute | solution.py:505
  29.1 7.9 %shard_map.90 = (f32[10,8,256]{2,1,0:T(8,128)S(1)}, f32[10,8,256]{2,1,0:T(8,128)S(1)}, f32[10,8,256]{2,1,0:T(8,128)S(1)}, f32[10,8,256]{2,1,0:T(8,128)S(1)}) custom-call(f32[13,16,256]{2,1,0:T(8,128)S(1)} %collective-permute-done.refs_0_, f32[2,16,8,128]{3,2,1,0:T(8,128)S(1)} %collective-permute-done.1.refs_1_, ...), custom_call_target="tpu_custom_call" | custom-call | tf_op jit(solution)/shard_map/pallas_call | solution.py:482
  37.1 0.2 collective-permute-start.8
  37.2 2.0 %collective-permute-start.9 = (f32[10,8,256]{2,1,0:T(8,128)S(1)}, f32[10,8,256]{2,1,0:T(8,128)S(1)}, u32[]{:S(2)}, u32[]{:S(2)}) collective-permute-start(f32[10,8,256]{2,1,0:T(8,128)S(1)} %get-tuple-element.37), channel_id=1, source_target_pairs={{0,3},{1,2},{2,1},{3,0},{4,7},{5,6},{6,5},{7,4},{8,11},{9,10},{10,... | collective-permute-start | bytes 245768 | tf_op jit(solution)/shard_map/ppermute | solution.py:505
  39.3 0.0 collective-permute-done.5.refs_1_.refs_5_
  39.3 3.0 %collective-permute-start.10 = (f32[10,8,256]{2,1,0:T(8,128)S(1)}, f32[10,8,256]{2,1,0:T(8,128)S(1)}, u32[]{:S(2)}, u32[]{:S(2)}) collective-permute-start(f32[10,8,256]{2,1,0:T(8,128)S(1)} %get-tuple-element.38), channel_id=1, source_target_pairs={{0,1},{1,0},{2,3},{3,2},{4,5},{5,4},{6,7},{7,6},{8,9},{9,8},{10,11... | collective-permute-start | bytes 245768 | tf_op jit(solution)/shard_map/ppermute | solution.py:505
  42.3 5.9 %collective-permute-done.6.refs_2_.refs_6_ = f32[22,8,256]{2,1,0:T(8,128)S(1)} collective-permute-done((f32[22,8,256]{2,1,0:T(8,128)S(1)}, f32[22,8,256]{2,1,0:T(8,128)S(1)}, u32[]{:S(2)}, u32[]{:S(2)}) %collective-permute-start.6) | collective-permute-done | bytes 180256 | tf_op jit(solution)/shard_map/ppermute | solution.py:505
  48.1 0.0 collective-permute-done.7.refs_3_.refs_7_
  48.1 0.4 shard_map.89.before
  48.5 0.0 collective-permute-done.8.refs_1_.refs_9_
  48.5 3.1 %collective-permute-done.9.refs_2_.refs_10_ = f32[10,8,256]{2,1,0:T(8,128)S(1)} collective-permute-done((f32[10,8,256]{2,1,0:T(8,128)S(1)}, f32[10,8,256]{2,1,0:T(8,128)S(1)}, u32[]{:S(2)}, u32[]{:S(2)}) %collective-permute-start.9) | collective-permute-done | bytes 81952 | tf_op jit(solution)/shard_map/ppermute | solution.py:505
  51.6 0.0 collective-permute-done.10.refs_3_.refs_11_
  51.6 0.4 shard_map.91
  52.1 0.0 collective-permute-start.13
  52.1 2.1 %collective-permute-start.12 = (f32[32,32]{1,0:T(8,128)S(1)}, f32[32,32]{1,0:T(8,128)S(1)}, u32[]{:S(2)}, u32[]{:S(2)}) collective-permute-start(f32[32,32]{1,0:T(8,128)S(1)} %shard_map.91), channel_id=1, source_target_pairs={{0,2},{1,3},{2,0},{3,1},{4,6},{5,7},{6,4},{7,5},{8,10},{9,11},{10,... | collective-permute-start | bytes 12296 | tf_op jit(solution)/shard_map/ppermute | solution.py:525
  54.2 1.4 %collective-permute-start.11 = (f32[32,32]{1,0:T(8,128)S(1)}, f32[32,32]{1,0:T(8,128)S(1)}, u32[]{:S(2)}, u32[]{:S(2)}) collective-permute-start(f32[32,32]{1,0:T(8,128)S(1)} %shard_map.91), channel_id=1, source_target_pairs={{0,1},{1,0},{2,3},{3,2},{4,5},{5,4},{6,7},{7,6},{8,9},{9,8},{10,11... | collective-permute-start | bytes 12296 | tf_op jit(solution)/shard_map/ppermute | solution.py:525
  55.6 0.6 collective-permute-done.13
  56.2 0.6 collective-permute-done.12
  56.8 1.1 %collective-permute-done.11 = f32[32,32]{1,0:T(8,128)S(1)} collective-permute-done((f32[32,32]{1,0:T(8,128)S(1)}, f32[32,32]{1,0:T(8,128)S(1)}, u32[]{:S(2)}, u32[]{:S(2)}) %collective-permute-start.11) | collective-permute-done | bytes 4128 | tf_op jit(solution)/shard_map/ppermute | solution.py:525
  57.9 0.0 collective-permute-start.14
  57.9 1.2 %collective-permute-done.14 = f32[32,32]{1,0:T(8,128)S(1)} collective-permute-done((f32[32,32]{1,0:T(8,128)S(1)}, f32[32,32]{1,0:T(8,128)S(1)}, u32[]{:S(2)}, u32[]{:S(2)}) %collective-permute-start.14) | collective-permute-done | bytes 4128 | tf_op jit(solution)/shard_map/ppermute | solution.py:525
  59.1 0.7 collective-permute-start.17
  59.8 1.3 %collective-permute-start.16 = (f32[32,32]{1,0:T(8,128)S(1)}, f32[32,32]{1,0:T(8,128)S(1)}, u32[]{:S(2)}, u32[]{:S(2)}) collective-permute-start(f32[32,32]{1,0:T(8,128)S(1)} %add.15.refs_0_), channel_id=1, source_target_pairs={{0,16},{1,17},{2,18},{3,19},{4,20},{5,21},{6,22},{7,23},{8,24},{9,... | collective-permute-start | bytes 12296 | tf_op jit(solution)/shard_map/ppermute | solution.py:525
  61.0 1.6 %collective-permute-start.15 = (f32[32,32]{1,0:T(8,128)S(1)}, f32[32,32]{1,0:T(8,128)S(1)}, u32[]{:S(2)}, u32[]{:S(2)}) collective-permute-start(f32[32,32]{1,0:T(8,128)S(1)} %add.15.refs_0_), channel_id=1, source_target_pairs={{0,8},{1,9},{2,10},{3,11},{4,12},{5,13},{6,14},{7,15},{8,0},{9,1},... | collective-permute-start | bytes 12296 | tf_op jit(solution)/shard_map/ppermute | solution.py:525
  62.6 1.2 %collective-permute-done.17.refs_3_ = f32[32,32]{1,0:T(8,128)S(1)} collective-permute-done((f32[32,32]{1,0:T(8,128)S(1)}, f32[32,32]{1,0:T(8,128)S(1)}, u32[]{:S(2)}, u32[]{:S(2)}) %collective-permute-start.17) | collective-permute-done | bytes 4128 | tf_op jit(solution)/shard_map/ppermute | solution.py:525
  63.8 0.0 collective-permute-done.16.refs_2_
  63.8 1.0 %collective-permute-done.15.refs_1_ = f32[32,32]{1,0:T(8,128)S(1)} collective-permute-done((f32[32,32]{1,0:T(8,128)S(1)}, f32[32,32]{1,0:T(8,128)S(1)}, u32[]{:S(2)}, u32[]{:S(2)}) %collective-permute-start.15) | collective-permute-done | bytes 4128 | tf_op jit(solution)/shard_map/ppermute | solution.py:525
  64.7 3.5 %shard_map.92 = (f32[32,8,256]{2,1,0:T(8,128)S(1)}, f32[32,8,256]{2,1,0:T(8,128)S(1)}, f32[32,8,256]{2,1,0:T(8,128)S(1)}, f32[32,8,256]{2,1,0:T(8,128)S(1)}, f32[32,32]{1,0:T(8,128)}) custom-call(f32[32,32]{1,0:T(8,128)S(1)} %add.15.refs_0_, f32[32,32]{1,0:T(8,128)S(1)} %collective-permute-done.15.refs_1_, f32[32,32]{1,0:T(8,128)S(1)} %collective-permute-done.16.refs_2_, ...), custom_call_target="tpu_custom_call" | custom-call | tf_op jit(solution)/shard_map/pallas_call | solution.py:482
  68.3 1.1 %collective-permute-start.18 = (f32[32,8,256]{2,1,0:T(8,128)S(1)}, f32[32,8,256]{2,1,0:T(8,128)S(1)}, u32[]{:S(2)}, u32[]{:S(2)}) collective-permute-start(f32[32,8,256]{2,1,0:T(8,128)S(1)} %get-tuple-element.40), channel_id=1, source_target_pairs={{0,2},{1,3},{2,0},{3,1},{4,6},{5,7},{6,4},{7,5},{8,10},{9,11},{10,... | collective-permute-start | bytes 786440 | tf_op jit(solution)/shard_map/ppermute | solution.py:505
  69.4 1.7 %collective-permute-start.19 = (f32[32,8,256]{2,1,0:T(8,128)S(1)}, f32[32,8,256]{2,1,0:T(8,128)S(1)}, u32[]{:S(2)}, u32[]{:S(2)}) collective-permute-start(f32[32,8,256]{2,1,0:T(8,128)S(1)} %get-tuple-element.41), channel_id=1, source_target_pairs={{0,3},{1,2},{2,1},{3,0},{4,7},{5,6},{6,5},{7,4},{8,11},{9,10},{10,... | collective-permute-start | bytes 786440 | tf_op jit(solution)/shard_map/ppermute | solution.py:505
  71.1 1.6 %collective-permute-start.20 = (f32[32,8,256]{2,1,0:T(8,128)S(1)}, f32[32,8,256]{2,1,0:T(8,128)S(1)}, u32[]{:S(2)}, u32[]{:S(2)}) collective-permute-start(f32[32,8,256]{2,1,0:T(8,128)S(1)} %get-tuple-element.42), channel_id=1, source_target_pairs={{0,1},{1,0},{2,3},{3,2},{4,5},{5,4},{6,7},{7,6},{8,9},{9,8},{10,11... | collective-permute-start | bytes 786440 | tf_op jit(solution)/shard_map/ppermute | solution.py:505
  72.7 13.3 %collective-permute-done.18.refs_1_ = f32[32,8,256]{2,1,0:T(8,128)S(1)} collective-permute-done((f32[32,8,256]{2,1,0:T(8,128)S(1)}, f32[32,8,256]{2,1,0:T(8,128)S(1)}, u32[]{:S(2)}, u32[]{:S(2)}) %collective-permute-start.18) | collective-permute-done | bytes 262176 | tf_op jit(solution)/shard_map/ppermute | solution.py:505
  86.0 7.0 %collective-permute-done.19.refs_2_ = f32[32,8,256]{2,1,0:T(8,128)S(1)} collective-permute-done((f32[32,8,256]{2,1,0:T(8,128)S(1)}, f32[32,8,256]{2,1,0:T(8,128)S(1)}, u32[]{:S(2)}, u32[]{:S(2)}) %collective-permute-start.19) | collective-permute-done | bytes 262176 | tf_op jit(solution)/shard_map/ppermute | solution.py:505
  93.0 0.0 collective-permute-done.20.refs_3_
  93.0 1.2 %shard_map.93 = f32[8,128,256]{2,1,0:T(8,128)} custom-call(f32[32,8,256]{2,1,0:T(8,128)S(1)} %get-tuple-element.39.refs_0_, f32[32,8,256]{2,1,0:T(8,128)S(1)} %collective-permute-done.18.refs_1_, f32[32,8,256]{2,1,0:T(8,128)S(1)} %collective-permute-done.19.refs_2_, f32[32,8,256]{2,1,0:T(8,128)S(1)} %collective-permute-done.20.refs_3_), custom_call_target="tpu_custom_call" | custom-call | tf_op jit(solution)/shard_map/pallas_call | solution.py:482
  (2 shorter events, 0.0 us)
Async XLA Ops:
  0.6 9.1 %copy-start = (f32[8,128,256]{2,1,0:T(8,128)S(1)}, f32[8,128,256]{2,1,0:T(8,128)}, u32[]{:S(2)}) copy-start(f32[8,128,256]{2,1,0:T(8,128)} %dirs.1) | copy-start | bytes 3145732
  3.8 7.8 %collective-permute-start = (f32[13,16,256]{2,1,0:T(8,128)}, f32[13,16,256]{2,1,0:T(8,128)S(1)}, u32[]{:S(2)}, u32[]{:S(2)}) collective-permute-start(f32[13,16,256]{2,1,0:T(8,128)} %get-tuple-element.23), channel_id=1, source_target_pairs={{0,16},{16,0},{1,17},{17,1},{2,18},{18,2},{3,19},{19,3},{4,20},{20... | collective-permute-start | bytes 638984 | tf_op jit(solution)/shard_map/ppermute | solution.py:556
  4.3 7.2 %collective-permute-start.1 = (f32[2,16,8,128]{3,2,1,0:T(8,128)}, f32[2,16,8,128]{3,2,1,0:T(8,128)S(1)}, u32[]{:S(2)}, u32[]{:S(2)}) collective-permute-start(f32[2,16,8,128]{3,2,1,0:T(8,128)} %get-tuple-element.24), channel_id=1, source_target_pairs={{0,4},{8,12},{4,0},{12,8},{1,5},{9,13},{5,1},{13,9},{2,6},{10,14},... | collective-permute-start | bytes 393224 | tf_op jit(solution)/shard_map/ppermute | solution.py:556
  4.3 7.2 %collective-permute-start.2 = (f32[2,16,8,128]{3,2,1,0:T(8,128)}, f32[2,16,8,128]{3,2,1,0:T(8,128)S(1)}, u32[]{:S(2)}, u32[]{:S(2)}) collective-permute-start(f32[2,16,8,128]{3,2,1,0:T(8,128)} %get-tuple-element.25), channel_id=1, source_target_pairs={{4,8},{8,4},{5,9},{9,5},{6,10},{10,6},{7,11},{11,7},{20,24},{24,20... | collective-permute-start | bytes 393224 | tf_op jit(solution)/shard_map/ppermute | solution.py:556
  5.0 6.5 %collective-permute-start.3 = (f32[2,2,8,128]{3,2,1,0:T(8,128)}, f32[2,2,8,128]{3,2,1,0:T(8,128)S(1)}, u32[]{:S(2)}, u32[]{:S(2)}) collective-permute-start(f32[2,2,8,128]{3,2,1,0:T(8,128)} %get-tuple-element.26), channel_id=1, source_target_pairs={{0,20},{8,28},{4,16},{12,24},{16,4},{24,12},{20,0},{28,8},{1,21},{... | collective-permute-start | bytes 49160 | tf_op jit(solution)/shard_map/ppermute | solution.py:556
  9.0 2.5 %collective-permute-start.4 = (f32[2,2,8,128]{3,2,1,0:T(8,128)}, f32[2,2,8,128]{3,2,1,0:T(8,128)S(1)}, u32[]{:S(2)}, u32[]{:S(2)}) collective-permute-start(f32[2,2,8,128]{3,2,1,0:T(8,128)} %get-tuple-element.27), channel_id=1, source_target_pairs={{4,24},{8,20},{20,8},{24,4},{5,25},{9,21},{21,9},{25,5},{6,26},{10... | collective-permute-start | bytes 49160 | tf_op jit(solution)/shard_map/ppermute | solution.py:556
  9.7 1.1 %copy-start.1 = (f32[5,128,256]{2,1,0:T(8,128)S(1)}, f32[5,128,256]{2,1,0:T(8,128)}, u32[]{:S(2)}) copy-start(f32[5,128,256]{2,1,0:T(8,128)} %get-tuple-element.28.fields) | copy-start | bytes 1966084
  24.7 14.6 %collective-permute-start.5 = (f32[22,8,256]{2,1,0:T(8,128)S(1)}, f32[22,8,256]{2,1,0:T(8,128)S(1)}, u32[]{:S(2)}, u32[]{:S(2)}) collective-permute-start(f32[22,8,256]{2,1,0:T(8,128)S(1)} %get-tuple-element.32), channel_id=1, source_target_pairs={{0,2},{1,3},{2,0},{3,1},{4,6},{5,7},{6,4},{7,5},{8,10},{9,11},{10,... | collective-permute-start | bytes 540680 | tf_op jit(solution)/shard_map/ppermute | solution.py:505
  25.1 23.0 %collective-permute-start.6 = (f32[22,8,256]{2,1,0:T(8,128)S(1)}, f32[22,8,256]{2,1,0:T(8,128)S(1)}, u32[]{:S(2)}, u32[]{:S(2)}) collective-permute-start(f32[22,8,256]{2,1,0:T(8,128)S(1)} %get-tuple-element.33), channel_id=1, source_target_pairs={{0,3},{1,2},{2,1},{3,0},{4,7},{5,6},{6,5},{7,4},{8,11},{9,10},{10,... | collective-permute-start | bytes 540680 | tf_op jit(solution)/shard_map/ppermute | solution.py:505
  27.8 20.3 %collective-permute-start.7 = (f32[22,8,256]{2,1,0:T(8,128)S(1)}, f32[22,8,256]{2,1,0:T(8,128)S(1)}, u32[]{:S(2)}, u32[]{:S(2)}) collective-permute-start(f32[22,8,256]{2,1,0:T(8,128)S(1)} %get-tuple-element.34), channel_id=1, source_target_pairs={{0,1},{1,0},{2,3},{3,2},{4,5},{5,4},{6,7},{7,6},{8,9},{9,8},{10,11... | collective-permute-start | bytes 540680 | tf_op jit(solution)/shard_map/ppermute | solution.py:505
  37.1 11.5 %collective-permute-start.8 = (f32[10,8,256]{2,1,0:T(8,128)S(1)}, f32[10,8,256]{2,1,0:T(8,128)S(1)}, u32[]{:S(2)}, u32[]{:S(2)}) collective-permute-start(f32[10,8,256]{2,1,0:T(8,128)S(1)} %get-tuple-element.36), channel_id=1, source_target_pairs={{0,2},{1,3},{2,0},{3,1},{4,6},{5,7},{6,4},{7,5},{8,10},{9,11},{10,... | collective-permute-start | bytes 245768 | tf_op jit(solution)/shard_map/ppermute | solution.py:505
  37.2 14.4 %collective-permute-start.9 = (f32[10,8,256]{2,1,0:T(8,128)S(1)}, f32[10,8,256]{2,1,0:T(8,128)S(1)}, u32[]{:S(2)}, u32[]{:S(2)}) collective-permute-start(f32[10,8,256]{2,1,0:T(8,128)S(1)} %get-tuple-element.37), channel_id=1, source_target_pairs={{0,3},{1,2},{2,1},{3,0},{4,7},{5,6},{6,5},{7,4},{8,11},{9,10},{10,... | collective-permute-start | bytes 245768 | tf_op jit(solution)/shard_map/ppermute | solution.py:505
  39.3 12.3 %collective-permute-start.10 = (f32[10,8,256]{2,1,0:T(8,128)S(1)}, f32[10,8,256]{2,1,0:T(8,128)S(1)}, u32[]{:S(2)}, u32[]{:S(2)}) collective-permute-start(f32[10,8,256]{2,1,0:T(8,128)S(1)} %get-tuple-element.38), channel_id=1, source_target_pairs={{0,1},{1,0},{2,3},{3,2},{4,5},{5,4},{6,7},{7,6},{8,9},{9,8},{10,11... | collective-permute-start | bytes 245768 | tf_op jit(solution)/shard_map/ppermute | solution.py:505
  52.1 4.1 %collective-permute-start.13 = (f32[32,32]{1,0:T(8,128)S(1)}, f32[32,32]{1,0:T(8,128)S(1)}, u32[]{:S(2)}, u32[]{:S(2)}) collective-permute-start(f32[32,32]{1,0:T(8,128)S(1)} %shard_map.91), channel_id=1, source_target_pairs={{0,3},{1,2},{2,1},{3,0},{4,7},{5,6},{6,5},{7,4},{8,11},{9,10},{10,... | collective-permute-start | bytes 12296 | tf_op jit(solution)/shard_map/ppermute | solution.py:525
  52.1 4.7 %collective-permute-start.12 = (f32[32,32]{1,0:T(8,128)S(1)}, f32[32,32]{1,0:T(8,128)S(1)}, u32[]{:S(2)}, u32[]{:S(2)}) collective-permute-start(f32[32,32]{1,0:T(8,128)S(1)} %shard_map.91), channel_id=1, source_target_pairs={{0,2},{1,3},{2,0},{3,1},{4,6},{5,7},{6,4},{7,5},{8,10},{9,11},{10,... | collective-permute-start | bytes 12296 | tf_op jit(solution)/shard_map/ppermute | solution.py:525
  54.2 3.7 %collective-permute-start.11 = (f32[32,32]{1,0:T(8,128)S(1)}, f32[32,32]{1,0:T(8,128)S(1)}, u32[]{:S(2)}, u32[]{:S(2)}) collective-permute-start(f32[32,32]{1,0:T(8,128)S(1)} %shard_map.91), channel_id=1, source_target_pairs={{0,1},{1,0},{2,3},{3,2},{4,5},{5,4},{6,7},{7,6},{8,9},{9,8},{10,11... | collective-permute-start | bytes 12296 | tf_op jit(solution)/shard_map/ppermute | solution.py:525
  57.9 1.2 %collective-permute-start.14 = (f32[32,32]{1,0:T(8,128)S(1)}, f32[32,32]{1,0:T(8,128)S(1)}, u32[]{:S(2)}, u32[]{:S(2)}) collective-permute-start(f32[32,32]{1,0:T(8,128)S(1)} %add_add_fusion), channel_id=1, source_target_pairs={{0,4},{1,5},{2,6},{3,7},{4,0},{5,1},{6,2},{7,3},{8,12},{9,13},{10,... | collective-permute-start | bytes 12296 | tf_op jit(solution)/shard_map/ppermute | solution.py:525
  59.1 4.7 %collective-permute-start.17 = (f32[32,32]{1,0:T(8,128)S(1)}, f32[32,32]{1,0:T(8,128)S(1)}, u32[]{:S(2)}, u32[]{:S(2)}) collective-permute-start(f32[32,32]{1,0:T(8,128)S(1)} %add.15.refs_0_), channel_id=1, source_target_pairs={{0,24},{1,25},{2,26},{3,27},{4,28},{5,29},{6,30},{7,31},{8,16},{9,... | collective-permute-start | bytes 12296 | tf_op jit(solution)/shard_map/ppermute | solution.py:525
  59.8 4.0 %collective-permute-start.16 = (f32[32,32]{1,0:T(8,128)S(1)}, f32[32,32]{1,0:T(8,128)S(1)}, u32[]{:S(2)}, u32[]{:S(2)}) collective-permute-start(f32[32,32]{1,0:T(8,128)S(1)} %add.15.refs_0_), channel_id=1, source_target_pairs={{0,16},{1,17},{2,18},{3,19},{4,20},{5,21},{6,22},{7,23},{8,24},{9,... | collective-permute-start | bytes 12296 | tf_op jit(solution)/shard_map/ppermute | solution.py:525
  61.0 3.7 %collective-permute-start.15 = (f32[32,32]{1,0:T(8,128)S(1)}, f32[32,32]{1,0:T(8,128)S(1)}, u32[]{:S(2)}, u32[]{:S(2)}) collective-permute-start(f32[32,32]{1,0:T(8,128)S(1)} %add.15.refs_0_), channel_id=1, source_target_pairs={{0,8},{1,9},{2,10},{3,11},{4,12},{5,13},{6,14},{7,15},{8,0},{9,1},... | collective-permute-start | bytes 12296 | tf_op jit(solution)/shard_map/ppermute | solution.py:525
  68.3 17.7 %collective-permute-start.18 = (f32[32,8,256]{2,1,0:T(8,128)S(1)}, f32[32,8,256]{2,1,0:T(8,128)S(1)}, u32[]{:S(2)}, u32[]{:S(2)}) collective-permute-start(f32[32,8,256]{2,1,0:T(8,128)S(1)} %get-tuple-element.40), channel_id=1, source_target_pairs={{0,2},{1,3},{2,0},{3,1},{4,6},{5,7},{6,4},{7,5},{8,10},{9,11},{10,... | collective-permute-start | bytes 786440 | tf_op jit(solution)/shard_map/ppermute | solution.py:505
  69.4 23.6 %collective-permute-start.19 = (f32[32,8,256]{2,1,0:T(8,128)S(1)}, f32[32,8,256]{2,1,0:T(8,128)S(1)}, u32[]{:S(2)}, u32[]{:S(2)}) collective-permute-start(f32[32,8,256]{2,1,0:T(8,128)S(1)} %get-tuple-element.41), channel_id=1, source_target_pairs={{0,3},{1,2},{2,1},{3,0},{4,7},{5,6},{6,5},{7,4},{8,11},{9,10},{10,... | collective-permute-start | bytes 786440 | tf_op jit(solution)/shard_map/ppermute | solution.py:505
  71.1 21.8 %collective-permute-start.20 = (f32[32,8,256]{2,1,0:T(8,128)S(1)}, f32[32,8,256]{2,1,0:T(8,128)S(1)}, u32[]{:S(2)}, u32[]{:S(2)}) collective-permute-start(f32[32,8,256]{2,1,0:T(8,128)S(1)} %get-tuple-element.42), channel_id=1, source_target_pairs={{0,1},{1,0},{2,3},{3,2},{4,5},{5,4},{6,7},{7,6},{8,9},{9,8},{10,11... | collective-permute-start | bytes 786440 | tf_op jit(solution)/shard_map/ppermute | solution.py:505

commit v4 on v3

--- a/solution.py
+++ b/solution.py
@@ -22,6 +22,7 @@
 F32 = jnp.float32
 BF16 = jnp.bfloat16
 WEIGHTS = ((4.0, 1.0), (1.0, 4.0))
+BLOCK = 8
 PARTS = 2
 FIRST_ROWS = 88
 
@@ -417,30 +418,32 @@
     row_of = iota((size, LANES), 0)
     wide = jnp.concatenate([gram, jnp.zeros((size, LANES - size), F32)], axis=1)
     work = jnp.where(lane < size, wide, jnp.where(lane == row_of + size, 1.0, 0.0))
-    pivots = jnp.ones((size, 1), F32)
-    index = iota((size, 1), 0)
-    for k in range(size):
-        top = work[k : k + 1, :]
-        pivot = top[:, k : k + 1]
-        ratio = jnp.where(index > k, work[:, k : k + 1] / pivot, 0.0)
-        pivots = jnp.where(index == k, pivot, pivots)
-        work = work - ratio * top
+    pivots = jnp.ones(work.shape, F32)
+    for k in range(0, size, BLOCK):
+        columns = [jnp.broadcast_to(work[:, c : c + 1], work.shape) for c in range(k, k + BLOCK)]
+        tops = [work[c : c + 1, :] for c in range(k, k + BLOCK)]
+        for a in range(BLOCK):
+            pivot = columns[a][k + a : k + a + 1, :]
+            pivots = jnp.where(row_of == k + a, pivot, pivots)
+            for c in range(a + 1, BLOCK):
+                ratio = columns[c][k + a : k + a + 1, :] / pivot
+                columns[c] = columns[c] - columns[a] * ratio
+                tops[c] = tops[c] - ratio * tops[a]
+            work = work - jnp.where(row_of > k + a, columns[a], 0.0) * (tops[a] / pivot)
     return work / jnp.sqrt(pivots), lane, row_of
 
 
 def form_basis(inverse, pieces, outs):
     count = len(SWAPS)
     high, low = halves(inverse)
-    both = jnp.concatenate([high, low], axis=0)
-    size = inverse.shape[0]
+    left = jnp.concatenate([high, low, high], axis=1)
     base = 0
     for piece in range(len(pieces) // count):
         parts = pieces[count * piece : count * piece + count]
         for r in range(parts[0].shape[0]):
-            value_high, value_low = halves(jnp.concatenate([part[r] for part in parts], axis=0))
-            first = jnp.dot(both, value_high, preferred_element_type=F32)
-            second = jnp.dot(high, value_low, preferred_element_type=F32)
-            total = first[:size] + (first[size:] + second)
+            high, low = halves(jnp.concatenate([part[r] for part in parts], axis=0))
+            right = jnp.concatenate([high, high, low], axis=0)
+            total = jnp.dot(left, right, preferred_element_type=F32)
             for n, out in enumerate(outs):
                 out[base + r] = total[8 * n : 8 * n + 8]
         base += parts[0].shape[0]

time: 94.5 us -> 92.5 us (0.979)
  Pallas kernels: 30.5 us -> 28.5 us
    pallas_call x8, Pallas kernels: 30.5 us -> 28.5 us  [call(): pl.pallas_call(kernel, out_shape=shapes, in_specs=[pl.BlockSpec(memory_sp...]
where the time goes in v4:
time: 92.5 us; the launch traced here: 92.2 us
  waiting for transfers between devices  34.9 us (38%)
  Pallas kernels  28.5 us (31%)
  starting transfers between devices  26.9 us (29%)
  local copies, waits for them, and re-layouts  1.09 us (1%)
    ppermute x9, waiting for transfers between devices, swap_bit(): return lax.ppermute(value, axis, [(i, i ^ bit) for i in range(count)])  29.2 us
    pallas_call x8, Pallas kernels, call(): pl.pallas_call(kernel, out_shape=shapes, in_specs=[pl.BlockSpec(memory_sp...  28.5 us
    ppermute x9, starting transfers between devices, swap_bit(): return lax.ppermute(value, axis, [(i, i ^ bit) for i in range(count)])  14 us
    ppermute x7, starting transfers between devices, partial_sums(): lax.ppermute(value, axes, [(i, i ^ mask) for i in range(count)])  6.99 us
    ppermute x5, starting transfers between devices, on_device(): lax.ppermute(m, axis, pairs)  5.92 us
    ppermute x7, waiting for transfers between devices, partial_sums(): lax.ppermute(value, axes, [(i, i ^ mask) for i in range(count)])  5.66 us
  transfers between devices with their start and end apart: 21, of which 10 were waited for; matrix products, arithmetic and copies ran while one was open for 0% of the time, Pallas kernels for 10%

profile of v4, /device:TPU:20, one launch (start us, length us, event | category | flops | bytes accessed | tf_op | source)
XLA Modules:
  0.0 92.2 jit_solution(16944392794910935505)
XLA Ops:
  0.6 0.0 copy-start
  0.6 3.1 %shard_map.86 = (f32[5,128,256]{2,1,0:T(8,128)}, f32[13,16,256]{2,1,0:T(8,128)}, f32[2,16,8,128]{3,2,1,0:T(8,128)}, f32[2,16,8,128]{3,2,1,0:T(8,128)}, f32[2,2,8...) custom-call(f32[8,128,256]{2,1,0:T(8,128)} %dirs.1, f32[2,128,256]{2,1,0:T(8,128)} %refs_1_.1, f32[128,256]{1,0:T(8,128)} %refs_2_.1, ...), custom_call_target="tpu_custom_call" | custom-call | tf_op jit(solution)/shard_map/pallas_call | solution.py:485
  3.8 0.6 collective-permute-start
  4.3 0.0 collective-permute-start.1
  4.3 0.7 collective-permute-start.2
  5.0 4.0 %collective-permute-start.3 = (f32[2,2,8,128]{3,2,1,0:T(8,128)}, f32[2,2,8,128]{3,2,1,0:T(8,128)S(1)}, u32[]{:S(2)}, u32[]{:S(2)}) collective-permute-start(f32[2,2,8,128]{3,2,1,0:T(8,128)} %get-tuple-element.26), channel_id=1, source_target_pairs={{0,20},{8,28},{4,16},{12,24},{16,4},{24,12},{20,0},{28,8},{1,21},{... | collective-permute-start | bytes 49160 | tf_op jit(solution)/shard_map/ppermute | solution.py:559
  9.0 0.7 collective-permute-start.4
  9.7 0.0 copy-done
  9.7 0.0 copy-start.1
  9.7 1.1 %copy-done.1 = f32[5,128,256]{2,1,0:T(8,128)S(1)} copy-done((f32[5,128,256]{2,1,0:T(8,128)S(1)}, f32[5,128,256]{2,1,0:T(8,128)}, u32[]{:S(2)}) %copy-start.1) | copy-done | bytes 655384
  10.8 0.7 shard_map.87
  11.5 0.0 collective-permute-done.3.refs_3_
  11.5 0.0 collective-permute-done.4.refs_4_
  11.5 0.0 collective-permute-done.1.refs_1_
  11.5 0.0 collective-permute-done.2.refs_2_
  11.5 0.0 collective-permute-done.refs_0_
  11.6 13.1 %shard_map.88 = (f32[22,8,256]{2,1,0:T(8,128)S(1)}, f32[22,8,256]{2,1,0:T(8,128)S(1)}, f32[22,8,256]{2,1,0:T(8,128)S(1)}, f32[22,8,256]{2,1,0:T(8,128)S(1)}) custom-call(f32[13,16,256]{2,1,0:T(8,128)S(1)} %collective-permute-done.refs_0_, f32[2,16,8,128]{3,2,1,0:T(8,128)S(1)} %collective-permute-done.1.refs_1_, ...), custom_call_target="tpu_custom_call" | custom-call | tf_op jit(solution)/shard_map/pallas_call | solution.py:485
  24.7 0.4 collective-permute-start.5
  25.1 2.7 %collective-permute-start.6 = (f32[22,8,256]{2,1,0:T(8,128)S(1)}, f32[22,8,256]{2,1,0:T(8,128)S(1)}, u32[]{:S(2)}, u32[]{:S(2)}) collective-permute-start(f32[22,8,256]{2,1,0:T(8,128)S(1)} %get-tuple-element.33), channel_id=1, source_target_pairs={{0,3},{1,2},{2,1},{3,0},{4,7},{5,6},{6,5},{7,4},{8,11},{9,10},{10,... | collective-permute-start | bytes 540680 | tf_op jit(solution)/shard_map/ppermute | solution.py:508
  27.8 1.3 %collective-permute-start.7 = (f32[22,8,256]{2,1,0:T(8,128)S(1)}, f32[22,8,256]{2,1,0:T(8,128)S(1)}, u32[]{:S(2)}, u32[]{:S(2)}) collective-permute-start(f32[22,8,256]{2,1,0:T(8,128)S(1)} %get-tuple-element.34), channel_id=1, source_target_pairs={{0,1},{1,0},{2,3},{3,2},{4,5},{5,4},{6,7},{7,6},{8,9},{9,8},{10,11... | collective-permute-start | bytes 540680 | tf_op jit(solution)/shard_map/ppermute | solution.py:508
  29.1 7.9 %shard_map.90 = (f32[10,8,256]{2,1,0:T(8,128)S(1)}, f32[10,8,256]{2,1,0:T(8,128)S(1)}, f32[10,8,256]{2,1,0:T(8,128)S(1)}, f32[10,8,256]{2,1,0:T(8,128)S(1)}) custom-call(f32[13,16,256]{2,1,0:T(8,128)S(1)} %collective-permute-done.refs_0_, f32[2,16,8,128]{3,2,1,0:T(8,128)S(1)} %collective-permute-done.1.refs_1_, ...), custom_call_target="tpu_custom_call" | custom-call | tf_op jit(solution)/shard_map/pallas_call | solution.py:485
  37.1 0.2 collective-permute-start.8
  37.2 2.0 %collective-permute-start.9 = (f32[10,8,256]{2,1,0:T(8,128)S(1)}, f32[10,8,256]{2,1,0:T(8,128)S(1)}, u32[]{:S(2)}, u32[]{:S(2)}) collective-permute-start(f32[10,8,256]{2,1,0:T(8,128)S(1)} %get-tuple-element.37), channel_id=1, source_target_pairs={{0,3},{1,2},{2,1},{3,0},{4,7},{5,6},{6,5},{7,4},{8,11},{9,10},{10,... | collective-permute-start | bytes 245768 | tf_op jit(solution)/shard_map/ppermute | solution.py:508
  39.3 0.0 collective-permute-done.5.refs_1_.refs_5_
  39.3 3.0 %collective-permute-start.10 = (f32[10,8,256]{2,1,0:T(8,128)S(1)}, f32[10,8,256]{2,1,0:T(8,128)S(1)}, u32[]{:S(2)}, u32[]{:S(2)}) collective-permute-start(f32[10,8,256]{2,1,0:T(8,128)S(1)} %get-tuple-element.38), channel_id=1, source_target_pairs={{0,1},{1,0},{2,3},{3,2},{4,5},{5,4},{6,7},{7,6},{8,9},{9,8},{10,11... | collective-permute-start | bytes 245768 | tf_op jit(solution)/shard_map/ppermute | solution.py:508
  42.3 5.9 %collective-permute-done.6.refs_2_.refs_6_ = f32[22,8,256]{2,1,0:T(8,128)S(1)} collective-permute-done((f32[22,8,256]{2,1,0:T(8,128)S(1)}, f32[22,8,256]{2,1,0:T(8,128)S(1)}, u32[]{:S(2)}, u32[]{:S(2)}) %collective-permute-start.6) | collective-permute-done | bytes 180256 | tf_op jit(solution)/shard_map/ppermute | solution.py:508
  48.1 0.0 collective-permute-done.7.refs_3_.refs_7_
  48.1 0.4 shard_map.89.before
  48.5 0.0 collective-permute-done.8.refs_1_.refs_9_
  48.5 3.1 %collective-permute-done.9.refs_2_.refs_10_ = f32[10,8,256]{2,1,0:T(8,128)S(1)} collective-permute-done((f32[10,8,256]{2,1,0:T(8,128)S(1)}, f32[10,8,256]{2,1,0:T(8,128)S(1)}, u32[]{:S(2)}, u32[]{:S(2)}) %collective-permute-start.9) | collective-permute-done | bytes 81952 | tf_op jit(solution)/shard_map/ppermute | solution.py:508
  51.6 0.0 collective-permute-done.10.refs_3_.refs_11_
  51.6 0.4 shard_map.91
  52.1 0.0 collective-permute-start.13
  52.1 2.1 %collective-permute-start.12 = (f32[32,32]{1,0:T(8,128)S(1)}, f32[32,32]{1,0:T(8,128)S(1)}, u32[]{:S(2)}, u32[]{:S(2)}) collective-permute-start(f32[32,32]{1,0:T(8,128)S(1)} %shard_map.91), channel_id=1, source_target_pairs={{0,2},{1,3},{2,0},{3,1},{4,6},{5,7},{6,4},{7,5},{8,10},{9,11},{10,... | collective-permute-start | bytes 12296 | tf_op jit(solution)/shard_map/ppermute | solution.py:528
  54.2 1.4 %collective-permute-start.11 = (f32[32,32]{1,0:T(8,128)S(1)}, f32[32,32]{1,0:T(8,128)S(1)}, u32[]{:S(2)}, u32[]{:S(2)}) collective-permute-start(f32[32,32]{1,0:T(8,128)S(1)} %shard_map.91), channel_id=1, source_target_pairs={{0,1},{1,0},{2,3},{3,2},{4,5},{5,4},{6,7},{7,6},{8,9},{9,8},{10,11... | collective-permute-start | bytes 12296 | tf_op jit(solution)/shard_map/ppermute | solution.py:528
  55.6 0.6 collective-permute-done.13
  56.2 0.6 collective-permute-done.12
  56.8 1.1 %collective-permute-done.11 = f32[32,32]{1,0:T(8,128)S(1)} collective-permute-done((f32[32,32]{1,0:T(8,128)S(1)}, f32[32,32]{1,0:T(8,128)S(1)}, u32[]{:S(2)}, u32[]{:S(2)}) %collective-permute-start.11) | collective-permute-done | bytes 4128 | tf_op jit(solution)/shard_map/ppermute | solution.py:528
  57.9 0.0 collective-permute-start.14
  57.9 1.2 %collective-permute-done.14 = f32[32,32]{1,0:T(8,128)S(1)} collective-permute-done((f32[32,32]{1,0:T(8,128)S(1)}, f32[32,32]{1,0:T(8,128)S(1)}, u32[]{:S(2)}, u32[]{:S(2)}) %collective-permute-start.14) | collective-permute-done | bytes 4128 | tf_op jit(solution)/shard_map/ppermute | solution.py:528
  59.1 0.7 collective-permute-start.17
  59.8 1.3 %collective-permute-start.16 = (f32[32,32]{1,0:T(8,128)S(1)}, f32[32,32]{1,0:T(8,128)S(1)}, u32[]{:S(2)}, u32[]{:S(2)}) collective-permute-start(f32[32,32]{1,0:T(8,128)S(1)} %add.15.refs_0_), channel_id=1, source_target_pairs={{0,16},{1,17},{2,18},{3,19},{4,20},{5,21},{6,22},{7,23},{8,24},{9,... | collective-permute-start | bytes 12296 | tf_op jit(solution)/shard_map/ppermute | solution.py:528
  61.0 1.6 %collective-permute-start.15 = (f32[32,32]{1,0:T(8,128)S(1)}, f32[32,32]{1,0:T(8,128)S(1)}, u32[]{:S(2)}, u32[]{:S(2)}) collective-permute-start(f32[32,32]{1,0:T(8,128)S(1)} %add.15.refs_0_), channel_id=1, source_target_pairs={{0,8},{1,9},{2,10},{3,11},{4,12},{5,13},{6,14},{7,15},{8,0},{9,1},... | collective-permute-start | bytes 12296 | tf_op jit(solution)/shard_map/ppermute | solution.py:528
  62.6 1.2 %collective-permute-done.17.refs_3_ = f32[32,32]{1,0:T(8,128)S(1)} collective-permute-done((f32[32,32]{1,0:T(8,128)S(1)}, f32[32,32]{1,0:T(8,128)S(1)}, u32[]{:S(2)}, u32[]{:S(2)}) %collective-permute-start.17) | collective-permute-done | bytes 4128 | tf_op jit(solution)/shard_map/ppermute | solution.py:528
  63.8 0.0 collective-permute-done.16.refs_2_
  63.8 1.0 %collective-permute-done.15.refs_1_ = f32[32,32]{1,0:T(8,128)S(1)} collective-permute-done((f32[32,32]{1,0:T(8,128)S(1)}, f32[32,32]{1,0:T(8,128)S(1)}, u32[]{:S(2)}, u32[]{:S(2)}) %collective-permute-start.15) | collective-permute-done | bytes 4128 | tf_op jit(solution)/shard_map/ppermute | solution.py:528
  64.7 1.5 %shard_map.92 = (f32[32,8,256]{2,1,0:T(8,128)S(1)}, f32[32,8,256]{2,1,0:T(8,128)S(1)}, f32[32,8,256]{2,1,0:T(8,128)S(1)}, f32[32,8,256]{2,1,0:T(8,128)S(1)}, f32[32,32]{1,0:T(8,128)}) custom-call(f32[32,32]{1,0:T(8,128)S(1)} %add.15.refs_0_, f32[32,32]{1,0:T(8,128)S(1)} %collective-permute-done.15.refs_1_, f32[32,32]{1,0:T(8,128)S(1)} %collective-permute-done.16.refs_2_, ...), custom_call_target="tpu_custom_call" | custom-call | tf_op jit(solution)/shard_map/pallas_call | solution.py:485
  66.3 1.1 %collective-permute-start.18 = (f32[32,8,256]{2,1,0:T(8,128)S(1)}, f32[32,8,256]{2,1,0:T(8,128)S(1)}, u32[]{:S(2)}, u32[]{:S(2)}) collective-permute-start(f32[32,8,256]{2,1,0:T(8,128)S(1)} %get-tuple-element.40), channel_id=1, source_target_pairs={{0,2},{1,3},{2,0},{3,1},{4,6},{5,7},{6,4},{7,5},{8,10},{9,11},{10,... | collective-permute-start | bytes 786440 | tf_op jit(solution)/shard_map/ppermute | solution.py:508
  67.4 1.7 %collective-permute-start.19 = (f32[32,8,256]{2,1,0:T(8,128)S(1)}, f32[32,8,256]{2,1,0:T(8,128)S(1)}, u32[]{:S(2)}, u32[]{:S(2)}) collective-permute-start(f32[32,8,256]{2,1,0:T(8,128)S(1)} %get-tuple-element.41), channel_id=1, source_target_pairs={{0,3},{1,2},{2,1},{3,0},{4,7},{5,6},{6,5},{7,4},{8,11},{9,10},{10,... | collective-permute-start | bytes 786440 | tf_op jit(solution)/shard_map/ppermute | solution.py:508
  69.1 1.6 %collective-permute-start.20 = (f32[32,8,256]{2,1,0:T(8,128)S(1)}, f32[32,8,256]{2,1,0:T(8,128)S(1)}, u32[]{:S(2)}, u32[]{:S(2)}) collective-permute-start(f32[32,8,256]{2,1,0:T(8,128)S(1)} %get-tuple-element.42), channel_id=1, source_target_pairs={{0,1},{1,0},{2,3},{3,2},{4,5},{5,4},{6,7},{7,6},{8,9},{9,8},{10,11... | collective-permute-start | bytes 786440 | tf_op jit(solution)/shard_map/ppermute | solution.py:508
  70.7 13.3 %collective-permute-done.18.refs_1_ = f32[32,8,256]{2,1,0:T(8,128)S(1)} collective-permute-done((f32[32,8,256]{2,1,0:T(8,128)S(1)}, f32[32,8,256]{2,1,0:T(8,128)S(1)}, u32[]{:S(2)}, u32[]{:S(2)}) %collective-permute-start.18) | collective-permute-done | bytes 262176 | tf_op jit(solution)/shard_map/ppermute | solution.py:508
  83.9 7.0 %collective-permute-done.19.refs_2_ = f32[32,8,256]{2,1,0:T(8,128)S(1)} collective-permute-done((f32[32,8,256]{2,1,0:T(8,128)S(1)}, f32[32,8,256]{2,1,0:T(8,128)S(1)}, u32[]{:S(2)}, u32[]{:S(2)}) %collective-permute-start.19) | collective-permute-done | bytes 262176 | tf_op jit(solution)/shard_map/ppermute | solution.py:508
  90.9 0.0 collective-permute-done.20.refs_3_
  90.9 1.2 %shard_map.93 = f32[8,128,256]{2,1,0:T(8,128)} custom-call(f32[32,8,256]{2,1,0:T(8,128)S(1)} %get-tuple-element.39.refs_0_, f32[32,8,256]{2,1,0:T(8,128)S(1)} %collective-permute-done.18.refs_1_, f32[32,8,256]{2,1,0:T(8,128)S(1)} %collective-permute-done.19.refs_2_, f32[32,8,256]{2,1,0:T(8,128)S(1)} %collective-permute-done.20.refs_3_), custom_call_target="tpu_custom_call" | custom-call | tf_op jit(solution)/shard_map/pallas_call | solution.py:485
  (2 shorter events, 0.0 us)
Async XLA Ops:
  0.6 9.1 %copy-start = (f32[8,128,256]{2,1,0:T(8,128)S(1)}, f32[8,128,256]{2,1,0:T(8,128)}, u32[]{:S(2)}) copy-start(f32[8,128,256]{2,1,0:T(8,128)} %dirs.1) | copy-start | bytes 3145732
  3.8 7.8 %collective-permute-start = (f32[13,16,256]{2,1,0:T(8,128)}, f32[13,16,256]{2,1,0:T(8,128)S(1)}, u32[]{:S(2)}, u32[]{:S(2)}) collective-permute-start(f32[13,16,256]{2,1,0:T(8,128)} %get-tuple-element.23), channel_id=1, source_target_pairs={{0,16},{16,0},{1,17},{17,1},{2,18},{18,2},{3,19},{19,3},{4,20},{20... | collective-permute-start | bytes 638984 | tf_op jit(solution)/shard_map/ppermute | solution.py:559
  4.3 7.2 %collective-permute-start.1 = (f32[2,16,8,128]{3,2,1,0:T(8,128)}, f32[2,16,8,128]{3,2,1,0:T(8,128)S(1)}, u32[]{:S(2)}, u32[]{:S(2)}) collective-permute-start(f32[2,16,8,128]{3,2,1,0:T(8,128)} %get-tuple-element.24), channel_id=1, source_target_pairs={{0,4},{8,12},{4,0},{12,8},{1,5},{9,13},{5,1},{13,9},{2,6},{10,14},... | collective-permute-start | bytes 393224 | tf_op jit(solution)/shard_map/ppermute | solution.py:559
  4.3 7.2 %collective-permute-start.2 = (f32[2,16,8,128]{3,2,1,0:T(8,128)}, f32[2,16,8,128]{3,2,1,0:T(8,128)S(1)}, u32[]{:S(2)}, u32[]{:S(2)}) collective-permute-start(f32[2,16,8,128]{3,2,1,0:T(8,128)} %get-tuple-element.25), channel_id=1, source_target_pairs={{4,8},{8,4},{5,9},{9,5},{6,10},{10,6},{7,11},{11,7},{20,24},{24,20... | collective-permute-start | bytes 393224 | tf_op jit(solution)/shard_map/ppermute | solution.py:559
  5.0 6.5 %collective-permute-start.3 = (f32[2,2,8,128]{3,2,1,0:T(8,128)}, f32[2,2,8,128]{3,2,1,0:T(8,128)S(1)}, u32[]{:S(2)}, u32[]{:S(2)}) collective-permute-start(f32[2,2,8,128]{3,2,1,0:T(8,128)} %get-tuple-element.26), channel_id=1, source_target_pairs={{0,20},{8,28},{4,16},{12,24},{16,4},{24,12},{20,0},{28,8},{1,21},{... | collective-permute-start | bytes 49160 | tf_op jit(solution)/shard_map/ppermute | solution.py:559
  9.0 2.5 %collective-permute-start.4 = (f32[2,2,8,128]{3,2,1,0:T(8,128)}, f32[2,2,8,128]{3,2,1,0:T(8,128)S(1)}, u32[]{:S(2)}, u32[]{:S(2)}) collective-permute-start(f32[2,2,8,128]{3,2,1,0:T(8,128)} %get-tuple-element.27), channel_id=1, source_target_pairs={{4,24},{8,20},{20,8},{24,4},{5,25},{9,21},{21,9},{25,5},{6,26},{10... | collective-permute-start | bytes 49160 | tf_op jit(solution)/shard_map/ppermute | solution.py:559
  9.7 1.1 %copy-start.1 = (f32[5,128,256]{2,1,0:T(8,128)S(1)}, f32[5,128,256]{2,1,0:T(8,128)}, u32[]{:S(2)}) copy-start(f32[5,128,256]{2,1,0:T(8,128)} %get-tuple-element.28.fields) | copy-start | bytes 1966084
  24.7 14.6 %collective-permute-start.5 = (f32[22,8,256]{2,1,0:T(8,128)S(1)}, f32[22,8,256]{2,1,0:T(8,128)S(1)}, u32[]{:S(2)}, u32[]{:S(2)}) collective-permute-start(f32[22,8,256]{2,1,0:T(8,128)S(1)} %get-tuple-element.32), channel_id=1, source_target_pairs={{0,2},{1,3},{2,0},{3,1},{4,6},{5,7},{6,4},{7,5},{8,10},{9,11},{10,... | collective-permute-start | bytes 540680 | tf_op jit(solution)/shard_map/ppermute | solution.py:508
  25.1 23.0 %collective-permute-start.6 = (f32[22,8,256]{2,1,0:T(8,128)S(1)}, f32[22,8,256]{2,1,0:T(8,128)S(1)}, u32[]{:S(2)}, u32[]{:S(2)}) collective-permute-start(f32[22,8,256]{2,1,0:T(8,128)S(1)} %get-tuple-element.33), channel_id=1, source_target_pairs={{0,3},{1,2},{2,1},{3,0},{4,7},{5,6},{6,5},{7,4},{8,11},{9,10},{10,... | collective-permute-start | bytes 540680 | tf_op jit(solution)/shard_map/ppermute | solution.py:508
  27.8 20.3 %collective-permute-start.7 = (f32[22,8,256]{2,1,0:T(8,128)S(1)}, f32[22,8,256]{2,1,0:T(8,128)S(1)}, u32[]{:S(2)}, u32[]{:S(2)}) collective-permute-start(f32[22,8,256]{2,1,0:T(8,128)S(1)} %get-tuple-element.34), channel_id=1, source_target_pairs={{0,1},{1,0},{2,3},{3,2},{4,5},{5,4},{6,7},{7,6},{8,9},{9,8},{10,11... | collective-permute-start | bytes 540680 | tf_op jit(solution)/shard_map/ppermute | solution.py:508
  37.1 11.5 %collective-permute-start.8 = (f32[10,8,256]{2,1,0:T(8,128)S(1)}, f32[10,8,256]{2,1,0:T(8,128)S(1)}, u32[]{:S(2)}, u32[]{:S(2)}) collective-permute-start(f32[10,8,256]{2,1,0:T(8,128)S(1)} %get-tuple-element.36), channel_id=1, source_target_pairs={{0,2},{1,3},{2,0},{3,1},{4,6},{5,7},{6,4},{7,5},{8,10},{9,11},{10,... | collective-permute-start | bytes 245768 | tf_op jit(solution)/shard_map/ppermute | solution.py:508
  37.2 14.4 %collective-permute-start.9 = (f32[10,8,256]{2,1,0:T(8,128)S(1)}, f32[10,8,256]{2,1,0:T(8,128)S(1)}, u32[]{:S(2)}, u32[]{:S(2)}) collective-permute-start(f32[10,8,256]{2,1,0:T(8,128)S(1)} %get-tuple-element.37), channel_id=1, source_target_pairs={{0,3},{1,2},{2,1},{3,0},{4,7},{5,6},{6,5},{7,4},{8,11},{9,10},{10,... | collective-permute-start | bytes 245768 | tf_op jit(solution)/shard_map/ppermute | solution.py:508
  39.3 12.3 %collective-permute-start.10 = (f32[10,8,256]{2,1,0:T(8,128)S(1)}, f32[10,8,256]{2,1,0:T(8,128)S(1)}, u32[]{:S(2)}, u32[]{:S(2)}) collective-permute-start(f32[10,8,256]{2,1,0:T(8,128)S(1)} %get-tuple-element.38), channel_id=1, source_target_pairs={{0,1},{1,0},{2,3},{3,2},{4,5},{5,4},{6,7},{7,6},{8,9},{9,8},{10,11... | collective-permute-start | bytes 245768 | tf_op jit(solution)/shard_map/ppermute | solution.py:508
  52.1 4.1 %collective-permute-start.13 = (f32[32,32]{1,0:T(8,128)S(1)}, f32[32,32]{1,0:T(8,128)S(1)}, u32[]{:S(2)}, u32[]{:S(2)}) collective-permute-start(f32[32,32]{1,0:T(8,128)S(1)} %shard_map.91), channel_id=1, source_target_pairs={{0,3},{1,2},{2,1},{3,0},{4,7},{5,6},{6,5},{7,4},{8,11},{9,10},{10,... | collective-permute-start | bytes 12296 | tf_op jit(solution)/shard_map/ppermute | solution.py:528
  52.1 4.7 %collective-permute-start.12 = (f32[32,32]{1,0:T(8,128)S(1)}, f32[32,32]{1,0:T(8,128)S(1)}, u32[]{:S(2)}, u32[]{:S(2)}) collective-permute-start(f32[32,32]{1,0:T(8,128)S(1)} %shard_map.91), channel_id=1, source_target_pairs={{0,2},{1,3},{2,0},{3,1},{4,6},{5,7},{6,4},{7,5},{8,10},{9,11},{10,... | collective-permute-start | bytes 12296 | tf_op jit(solution)/shard_map/ppermute | solution.py:528
  54.2 3.7 %collective-permute-start.11 = (f32[32,32]{1,0:T(8,128)S(1)}, f32[32,32]{1,0:T(8,128)S(1)}, u32[]{:S(2)}, u32[]{:S(2)}) collective-permute-start(f32[32,32]{1,0:T(8,128)S(1)} %shard_map.91), channel_id=1, source_target_pairs={{0,1},{1,0},{2,3},{3,2},{4,5},{5,4},{6,7},{7,6},{8,9},{9,8},{10,11... | collective-permute-start | bytes 12296 | tf_op jit(solution)/shard_map/ppermute | solution.py:528
  57.9 1.2 %collective-permute-start.14 = (f32[32,32]{1,0:T(8,128)S(1)}, f32[32,32]{1,0:T(8,128)S(1)}, u32[]{:S(2)}, u32[]{:S(2)}) collective-permute-start(f32[32,32]{1,0:T(8,128)S(1)} %add_add_fusion), channel_id=1, source_target_pairs={{0,4},{1,5},{2,6},{3,7},{4,0},{5,1},{6,2},{7,3},{8,12},{9,13},{10,... | collective-permute-start | bytes 12296 | tf_op jit(solution)/shard_map/ppermute | solution.py:528
  59.1 4.7 %collective-permute-start.17 = (f32[32,32]{1,0:T(8,128)S(1)}, f32[32,32]{1,0:T(8,128)S(1)}, u32[]{:S(2)}, u32[]{:S(2)}) collective-permute-start(f32[32,32]{1,0:T(8,128)S(1)} %add.15.refs_0_), channel_id=1, source_target_pairs={{0,24},{1,25},{2,26},{3,27},{4,28},{5,29},{6,30},{7,31},{8,16},{9,... | collective-permute-start | bytes 12296 | tf_op jit(solution)/shard_map/ppermute | solution.py:528
  59.8 4.0 %collective-permute-start.16 = (f32[32,32]{1,0:T(8,128)S(1)}, f32[32,32]{1,0:T(8,128)S(1)}, u32[]{:S(2)}, u32[]{:S(2)}) collective-permute-start(f32[32,32]{1,0:T(8,128)S(1)} %add.15.refs_0_), channel_id=1, source_target_pairs={{0,16},{1,17},{2,18},{3,19},{4,20},{5,21},{6,22},{7,23},{8,24},{9,... | collective-permute-start | bytes 12296 | tf_op jit(solution)/shard_map/ppermute | solution.py:528
  61.0 3.7 %collective-permute-start.15 = (f32[32,32]{1,0:T(8,128)S(1)}, f32[32,32]{1,0:T(8,128)S(1)}, u32[]{:S(2)}, u32[]{:S(2)}) collective-permute-start(f32[32,32]{1,0:T(8,128)S(1)} %add.15.refs_0_), channel_id=1, source_target_pairs={{0,8},{1,9},{2,10},{3,11},{4,12},{5,13},{6,14},{7,15},{8,0},{9,1},... | collective-permute-start | bytes 12296 | tf_op jit(solution)/shard_map/ppermute | solution.py:528
  66.3 17.7 %collective-permute-start.18 = (f32[32,8,256]{2,1,0:T(8,128)S(1)}, f32[32,8,256]{2,1,0:T(8,128)S(1)}, u32[]{:S(2)}, u32[]{:S(2)}) collective-permute-start(f32[32,8,256]{2,1,0:T(8,128)S(1)} %get-tuple-element.40), channel_id=1, source_target_pairs={{0,2},{1,3},{2,0},{3,1},{4,6},{5,7},{6,4},{7,5},{8,10},{9,11},{10,... | collective-permute-start | bytes 786440 | tf_op jit(solution)/shard_map/ppermute | solution.py:508
  67.4 23.6 %collective-permute-start.19 = (f32[32,8,256]{2,1,0:T(8,128)S(1)}, f32[32,8,256]{2,1,0:T(8,128)S(1)}, u32[]{:S(2)}, u32[]{:S(2)}) collective-permute-start(f32[32,8,256]{2,1,0:T(8,128)S(1)} %get-tuple-element.41), channel_id=1, source_target_pairs={{0,3},{1,2},{2,1},{3,0},{4,7},{5,6},{6,5},{7,4},{8,11},{9,10},{10,... | collective-permute-start | bytes 786440 | tf_op jit(solution)/shard_map/ppermute | solution.py:508
  69.1 21.8 %collective-permute-start.20 = (f32[32,8,256]{2,1,0:T(8,128)S(1)}, f32[32,8,256]{2,1,0:T(8,128)S(1)}, u32[]{:S(2)}, u32[]{:S(2)}) collective-permute-start(f32[32,8,256]{2,1,0:T(8,128)S(1)} %get-tuple-element.42), channel_id=1, source_target_pairs={{0,1},{1,0},{2,3},{3,2},{4,5},{5,4},{6,7},{7,6},{8,9},{9,8},{10,11... | collective-permute-start | bytes 786440 | tf_op jit(solution)/shard_map/ppermute | solution.py:508

commit v5 on v4

--- a/solution.py
+++ b/solution.py
@@ -464,7 +464,7 @@
 
 
 def assemble(spans, *refs):
-    parts, (out, held) = refs[:-2], refs[-2:]
+    parts, (out, held, turned, sems) = refs[:-4], refs[-4:]
     count = len(parts)
     base = 0
     for first, rows in spans:
@@ -473,12 +473,19 @@
             at = first + share * (lax.axis_index("dir") ^ k)
             held[pl.ds(at, share)] = part[base : base + share]
         base += share
-    for g in range(out.shape[1] // 8):
-        out[:, 8 * g : 8 * g + 8, :] = jnp.swapaxes(held[8 * g : 8 * g + 8], 0, 1)
-
-
-def call(kernel, outs, *args, scratch=(), limit=8, space=pltpu.VMEM):
-    vmem = pl.BlockSpec(memory_space=pltpu.VMEM)
+    copies = []
+    chunk = out.shape[1] // sems.shape[0]
+    for c in range(sems.shape[0]):
+        at = slice(chunk * c, chunk * c + chunk)
+        for g in range(chunk * c // 8, (chunk * c + chunk) // 8):
+            turned[:, 8 * g : 8 * g + 8, :] = jnp.swapaxes(held[8 * g : 8 * g + 8], 0, 1)
+        copies.append(pltpu.make_async_copy(turned.at[:, at, :], out.at[:, at, :], sems.at[c]))
+        copies[-1].start()
+    for copy in copies:
+        copy.wait()
+
+
+def call(kernel, outs, *args, scratch=(), limit=8, space=pltpu.VMEM, out_space=pltpu.VMEM):
     shapes = [
         jax.ShapeDtypeStruct(shape, F32) if isinstance(shape, tuple) else shape for shape in outs
     ]
@@ -486,7 +493,7 @@
         kernel,
         out_shape=shapes,
         in_specs=[pl.BlockSpec(memory_space=space)] * len(args),
-        out_specs=[vmem] * len(shapes),
+        out_specs=[pl.BlockSpec(memory_space=out_space)] * len(shapes),
         scratch_shapes=[
             pltpu.VMEM(shape, F32) if isinstance(shape, tuple) else shape for shape in scratch
         ],
@@ -622,7 +629,8 @@
         functools.partial(assemble, spans),
         [(own, rows, cols)],
         *parts,
-        scratch=[(rows, own, cols)],
+        scratch=[(rows, own, cols), (own, rows, cols), pltpu.SemaphoreType.DMA((4,))],
+        out_space=pltpu.HBM,
     )
     return (basis, upper)
 

time: 92.5 us -> 92.5 us (level)
  no operation moved by 1% of the time
where the time goes in v5:
time: 92.5 us; the launch traced here: 92.2 us
  waiting for transfers between devices  34.9 us (38%)
  Pallas kernels  28.3 us (31%)
  starting transfers between devices  26.9 us (29%)
  local copies, waits for them, and re-layouts  1.09 us (1%)
  between operations  0.96 us (1%)
    ppermute x9, waiting for transfers between devices, swap_bit(): return lax.ppermute(value, axis, [(i, i ^ bit) for i in range(count)])  29.2 us
    pallas_call x8, Pallas kernels, call(): pl.pallas_call(kernel, out_shape=shapes, in_specs=[pl.BlockSpec(memory_sp...  28.3 us
    ppermute x9, starting transfers between devices, swap_bit(): return lax.ppermute(value, axis, [(i, i ^ bit) for i in range(count)])  14 us
    ppermute x7, starting transfers between devices, partial_sums(): lax.ppermute(value, axes, [(i, i ^ mask) for i in range(count)])  6.99 us
    ppermute x5, starting transfers between devices, on_device(): lax.ppermute(m, axis, pairs)  5.92 us
    ppermute x7, waiting for transfers between devices, partial_sums(): lax.ppermute(value, axes, [(i, i ^ mask) for i in range(count)])  5.66 us
  transfers between devices with their start and end apart: 21, of which 10 were waited for; matrix products, arithmetic and copies ran while one was open for 0% of the time, Pallas kernels for 10%

profile of v5, /device:TPU:20, one launch (start us, length us, event | category | flops | bytes accessed | tf_op | source)
XLA Modules:
  0.0 92.2 jit_solution(3813443640272900004)
XLA Ops:
  0.6 0.0 copy-start
  0.6 3.1 %shard_map.86 = (f32[5,128,256]{2,1,0:T(8,128)}, f32[13,16,256]{2,1,0:T(8,128)}, f32[2,16,8,128]{3,2,1,0:T(8,128)}, f32[2,16,8,128]{3,2,1,0:T(8,128)}, f32[2,2,8...) custom-call(f32[8,128,256]{2,1,0:T(8,128)} %dirs.1, f32[2,128,256]{2,1,0:T(8,128)} %refs_1_.1, f32[128,256]{1,0:T(8,128)} %refs_2_.1, ...), custom_call_target="tpu_custom_call" | custom-call | tf_op jit(solution)/shard_map/pallas_call | solution.py:492
  3.8 0.6 collective-permute-start
  4.3 0.0 collective-permute-start.1
  4.3 0.7 collective-permute-start.2
  5.0 4.0 %collective-permute-start.3 = (f32[2,2,8,128]{3,2,1,0:T(8,128)}, f32[2,2,8,128]{3,2,1,0:T(8,128)S(1)}, u32[]{:S(2)}, u32[]{:S(2)}) collective-permute-start(f32[2,2,8,128]{3,2,1,0:T(8,128)} %get-tuple-element.26), channel_id=1, source_target_pairs={{0,20},{8,28},{4,16},{12,24},{16,4},{24,12},{20,0},{28,8},{1,21},{... | collective-permute-start | bytes 49160 | tf_op jit(solution)/shard_map/ppermute | solution.py:566
  9.0 0.7 collective-permute-start.4
  9.7 0.0 copy-done
  9.7 0.0 copy-start.1
  9.7 1.1 %copy-done.1 = f32[5,128,256]{2,1,0:T(8,128)S(1)} copy-done((f32[5,128,256]{2,1,0:T(8,128)S(1)}, f32[5,128,256]{2,1,0:T(8,128)}, u32[]{:S(2)}) %copy-start.1) | copy-done | bytes 655384
  10.8 0.7 shard_map.87
  11.5 0.0 collective-permute-done.3.refs_3_
  11.5 0.0 collective-permute-done.4.refs_4_
  11.5 0.0 collective-permute-done.1.refs_1_
  11.5 0.0 collective-permute-done.2.refs_2_
  11.5 0.0 collective-permute-done.refs_0_
  11.6 13.1 %shard_map.88 = (f32[22,8,256]{2,1,0:T(8,128)S(1)}, f32[22,8,256]{2,1,0:T(8,128)S(1)}, f32[22,8,256]{2,1,0:T(8,128)S(1)}, f32[22,8,256]{2,1,0:T(8,128)S(1)}) custom-call(f32[13,16,256]{2,1,0:T(8,128)S(1)} %collective-permute-done.refs_0_, f32[2,16,8,128]{3,2,1,0:T(8,128)S(1)} %collective-permute-done.1.refs_1_, ...), custom_call_target="tpu_custom_call" | custom-call | tf_op jit(solution)/shard_map/pallas_call | solution.py:492
  24.7 0.4 collective-permute-start.5
  25.1 2.7 %collective-permute-start.6 = (f32[22,8,256]{2,1,0:T(8,128)S(1)}, f32[22,8,256]{2,1,0:T(8,128)S(1)}, u32[]{:S(2)}, u32[]{:S(2)}) collective-permute-start(f32[22,8,256]{2,1,0:T(8,128)S(1)} %get-tuple-element.33), channel_id=1, source_target_pairs={{0,3},{1,2},{2,1},{3,0},{4,7},{5,6},{6,5},{7,4},{8,11},{9,10},{10,... | collective-permute-start | bytes 540680 | tf_op jit(solution)/shard_map/ppermute | solution.py:515
  27.8 1.3 %collective-permute-start.7 = (f32[22,8,256]{2,1,0:T(8,128)S(1)}, f32[22,8,256]{2,1,0:T(8,128)S(1)}, u32[]{:S(2)}, u32[]{:S(2)}) collective-permute-start(f32[22,8,256]{2,1,0:T(8,128)S(1)} %get-tuple-element.34), channel_id=1, source_target_pairs={{0,1},{1,0},{2,3},{3,2},{4,5},{5,4},{6,7},{7,6},{8,9},{9,8},{10,11... | collective-permute-start | bytes 540680 | tf_op jit(solution)/shard_map/ppermute | solution.py:515
  29.1 7.9 %shard_map.90 = (f32[10,8,256]{2,1,0:T(8,128)S(1)}, f32[10,8,256]{2,1,0:T(8,128)S(1)}, f32[10,8,256]{2,1,0:T(8,128)S(1)}, f32[10,8,256]{2,1,0:T(8,128)S(1)}) custom-call(f32[13,16,256]{2,1,0:T(8,128)S(1)} %collective-permute-done.refs_0_, f32[2,16,8,128]{3,2,1,0:T(8,128)S(1)} %collective-permute-done.1.refs_1_, ...), custom_call_target="tpu_custom_call" | custom-call | tf_op jit(solution)/shard_map/pallas_call | solution.py:492
  37.1 0.2 collective-permute-start.8
  37.2 2.0 %collective-permute-start.9 = (f32[10,8,256]{2,1,0:T(8,128)S(1)}, f32[10,8,256]{2,1,0:T(8,128)S(1)}, u32[]{:S(2)}, u32[]{:S(2)}) collective-permute-start(f32[10,8,256]{2,1,0:T(8,128)S(1)} %get-tuple-element.37), channel_id=1, source_target_pairs={{0,3},{1,2},{2,1},{3,0},{4,7},{5,6},{6,5},{7,4},{8,11},{9,10},{10,... | collective-permute-start | bytes 245768 | tf_op jit(solution)/shard_map/ppermute | solution.py:515
  39.3 0.0 collective-permute-done.5.refs_1_.refs_5_
  39.3 3.0 %collective-permute-start.10 = (f32[10,8,256]{2,1,0:T(8,128)S(1)}, f32[10,8,256]{2,1,0:T(8,128)S(1)}, u32[]{:S(2)}, u32[]{:S(2)}) collective-permute-start(f32[10,8,256]{2,1,0:T(8,128)S(1)} %get-tuple-element.38), channel_id=1, source_target_pairs={{0,1},{1,0},{2,3},{3,2},{4,5},{5,4},{6,7},{7,6},{8,9},{9,8},{10,11... | collective-permute-start | bytes 245768 | tf_op jit(solution)/shard_map/ppermute | solution.py:515
  42.3 5.9 %collective-permute-done.6.refs_2_.refs_6_ = f32[22,8,256]{2,1,0:T(8,128)S(1)} collective-permute-done((f32[22,8,256]{2,1,0:T(8,128)S(1)}, f32[22,8,256]{2,1,0:T(8,128)S(1)}, u32[]{:S(2)}, u32[]{:S(2)}) %collective-permute-start.6) | collective-permute-done | bytes 180256 | tf_op jit(solution)/shard_map/ppermute | solution.py:515
  48.1 0.0 collective-permute-done.7.refs_3_.refs_7_
  48.1 0.4 shard_map.89.before
  48.5 0.0 collective-permute-done.8.refs_1_.refs_9_
  48.5 3.1 %collective-permute-done.9.refs_2_.refs_10_ = f32[10,8,256]{2,1,0:T(8,128)S(1)} collective-permute-done((f32[10,8,256]{2,1,0:T(8,128)S(1)}, f32[10,8,256]{2,1,0:T(8,128)S(1)}, u32[]{:S(2)}, u32[]{:S(2)}) %collective-permute-start.9) | collective-permute-done | bytes 81952 | tf_op jit(solution)/shard_map/ppermute | solution.py:515
  51.6 0.0 collective-permute-done.10.refs_3_.refs_11_
  51.6 0.4 shard_map.91
  52.1 0.0 collective-permute-start.13
  52.1 2.1 %collective-permute-start.12 = (f32[32,32]{1,0:T(8,128)S(1)}, f32[32,32]{1,0:T(8,128)S(1)}, u32[]{:S(2)}, u32[]{:S(2)}) collective-permute-start(f32[32,32]{1,0:T(8,128)S(1)} %shard_map.91), channel_id=1, source_target_pairs={{0,2},{1,3},{2,0},{3,1},{4,6},{5,7},{6,4},{7,5},{8,10},{9,11},{10,... | collective-permute-start | bytes 12296 | tf_op jit(solution)/shard_map/ppermute | solution.py:535
  54.2 1.4 %collective-permute-start.11 = (f32[32,32]{1,0:T(8,128)S(1)}, f32[32,32]{1,0:T(8,128)S(1)}, u32[]{:S(2)}, u32[]{:S(2)}) collective-permute-start(f32[32,32]{1,0:T(8,128)S(1)} %shard_map.91), channel_id=1, source_target_pairs={{0,1},{1,0},{2,3},{3,2},{4,5},{5,4},{6,7},{7,6},{8,9},{9,8},{10,11... | collective-permute-start | bytes 12296 | tf_op jit(solution)/shard_map/ppermute | solution.py:535
  55.6 0.6 collective-permute-done.13
  56.2 0.6 collective-permute-done.12
  56.8 1.1 %collective-permute-done.11 = f32[32,32]{1,0:T(8,128)S(1)} collective-permute-done((f32[32,32]{1,0:T(8,128)S(1)}, f32[32,32]{1,0:T(8,128)S(1)}, u32[]{:S(2)}, u32[]{:S(2)}) %collective-permute-start.11) | collective-permute-done | bytes 4128 | tf_op jit(solution)/shard_map/ppermute | solution.py:535
  57.9 0.0 collective-permute-start.14
  57.9 1.2 %collective-permute-done.14 = f32[32,32]{1,0:T(8,128)S(1)} collective-permute-done((f32[32,32]{1,0:T(8,128)S(1)}, f32[32,32]{1,0:T(8,128)S(1)}, u32[]{:S(2)}, u32[]{:S(2)}) %collective-permute-start.14) | collective-permute-done | bytes 4128 | tf_op jit(solution)/shard_map/ppermute | solution.py:535
  59.1 0.7 collective-permute-start.17
  59.8 1.3 %collective-permute-start.16 = (f32[32,32]{1,0:T(8,128)S(1)}, f32[32,32]{1,0:T(8,128)S(1)}, u32[]{:S(2)}, u32[]{:S(2)}) collective-permute-start(f32[32,32]{1,0:T(8,128)S(1)} %add.15.refs_0_), channel_id=1, source_target_pairs={{0,16},{1,17},{2,18},{3,19},{4,20},{5,21},{6,22},{7,23},{8,24},{9,... | collective-permute-start | bytes 12296 | tf_op jit(solution)/shard_map/ppermute | solution.py:535
  61.0 1.6 %collective-permute-start.15 = (f32[32,32]{1,0:T(8,128)S(1)}, f32[32,32]{1,0:T(8,128)S(1)}, u32[]{:S(2)}, u32[]{:S(2)}) collective-permute-start(f32[32,32]{1,0:T(8,128)S(1)} %add.15.refs_0_), channel_id=1, source_target_pairs={{0,8},{1,9},{2,10},{3,11},{4,12},{5,13},{6,14},{7,15},{8,0},{9,1},... | collective-permute-start | bytes 12296 | tf_op jit(solution)/shard_map/ppermute | solution.py:535
  62.6 1.2 %collective-permute-done.17.refs_3_ = f32[32,32]{1,0:T(8,128)S(1)} collective-permute-done((f32[32,32]{1,0:T(8,128)S(1)}, f32[32,32]{1,0:T(8,128)S(1)}, u32[]{:S(2)}, u32[]{:S(2)}) %collective-permute-start.17) | collective-permute-done | bytes 4128 | tf_op jit(solution)/shard_map/ppermute | solution.py:535
  63.8 0.0 collective-permute-done.16.refs_2_
  63.8 1.0 %collective-permute-done.15.refs_1_ = f32[32,32]{1,0:T(8,128)S(1)} collective-permute-done((f32[32,32]{1,0:T(8,128)S(1)}, f32[32,32]{1,0:T(8,128)S(1)}, u32[]{:S(2)}, u32[]{:S(2)}) %collective-permute-start.15) | collective-permute-done | bytes 4128 | tf_op jit(solution)/shard_map/ppermute | solution.py:535
  64.7 1.5 %shard_map.92 = (f32[32,8,256]{2,1,0:T(8,128)S(1)}, f32[32,8,256]{2,1,0:T(8,128)S(1)}, f32[32,8,256]{2,1,0:T(8,128)S(1)}, f32[32,8,256]{2,1,0:T(8,128)S(1)}, f32[32,32]{1,0:T(8,128)}) custom-call(f32[32,32]{1,0:T(8,128)S(1)} %add.15.refs_0_, f32[32,32]{1,0:T(8,128)S(1)} %collective-permute-done.15.refs_1_, f32[32,32]{1,0:T(8,128)S(1)} %collective-permute-done.16.refs_2_, ...), custom_call_target="tpu_custom_call" | custom-call | tf_op jit(solution)/shard_map/pallas_call | solution.py:492
  66.3 1.1 %collective-permute-start.18 = (f32[32,8,256]{2,1,0:T(8,128)S(1)}, f32[32,8,256]{2,1,0:T(8,128)S(1)}, u32[]{:S(2)}, u32[]{:S(2)}) collective-permute-start(f32[32,8,256]{2,1,0:T(8,128)S(1)} %get-tuple-element.40), channel_id=1, source_target_pairs={{0,2},{1,3},{2,0},{3,1},{4,6},{5,7},{6,4},{7,5},{8,10},{9,11},{10,... | collective-permute-start | bytes 786440 | tf_op jit(solution)/shard_map/ppermute | solution.py:515
  67.4 1.7 %collective-permute-start.19 = (f32[32,8,256]{2,1,0:T(8,128)S(1)}, f32[32,8,256]{2,1,0:T(8,128)S(1)}, u32[]{:S(2)}, u32[]{:S(2)}) collective-permute-start(f32[32,8,256]{2,1,0:T(8,128)S(1)} %get-tuple-element.41), channel_id=1, source_target_pairs={{0,3},{1,2},{2,1},{3,0},{4,7},{5,6},{6,5},{7,4},{8,11},{9,10},{10,... | collective-permute-start | bytes 786440 | tf_op jit(solution)/shard_map/ppermute | solution.py:515
  69.1 1.6 %collective-permute-start.20 = (f32[32,8,256]{2,1,0:T(8,128)S(1)}, f32[32,8,256]{2,1,0:T(8,128)S(1)}, u32[]{:S(2)}, u32[]{:S(2)}) collective-permute-start(f32[32,8,256]{2,1,0:T(8,128)S(1)} %get-tuple-element.42), channel_id=1, source_target_pairs={{0,1},{1,0},{2,3},{3,2},{4,5},{5,4},{6,7},{7,6},{8,9},{9,8},{10,11... | collective-permute-start | bytes 786440 | tf_op jit(solution)/shard_map/ppermute | solution.py:515
  70.7 13.3 %collective-permute-done.18.refs_1_ = f32[32,8,256]{2,1,0:T(8,128)S(1)} collective-permute-done((f32[32,8,256]{2,1,0:T(8,128)S(1)}, f32[32,8,256]{2,1,0:T(8,128)S(1)}, u32[]{:S(2)}, u32[]{:S(2)}) %collective-permute-start.18) | collective-permute-done | bytes 262176 | tf_op jit(solution)/shard_map/ppermute | solution.py:515
  83.9 7.0 %collective-permute-done.19.refs_2_ = f32[32,8,256]{2,1,0:T(8,128)S(1)} collective-permute-done((f32[32,8,256]{2,1,0:T(8,128)S(1)}, f32[32,8,256]{2,1,0:T(8,128)S(1)}, u32[]{:S(2)}, u32[]{:S(2)}) %collective-permute-start.19) | collective-permute-done | bytes 262176 | tf_op jit(solution)/shard_map/ppermute | solution.py:515
  90.9 0.0 collective-permute-done.20.refs_3_
  90.9 1.1 %shard_map.93 = f32[8,128,256]{2,1,0:T(8,128)} custom-call(f32[32,8,256]{2,1,0:T(8,128)S(1)} %get-tuple-element.39.refs_0_, f32[32,8,256]{2,1,0:T(8,128)S(1)} %collective-permute-done.18.refs_1_, f32[32,8,256]{2,1,0:T(8,128)S(1)} %collective-permute-done.19.refs_2_, f32[32,8,256]{2,1,0:T(8,128)S(1)} %collective-permute-done.20.refs_3_), custom_call_target="tpu_custom_call" | custom-call | tf_op jit(solution)/shard_map/pallas_call | solution.py:492
  (2 shorter events, 0.0 us)
Async XLA Ops:
  0.6 9.1 %copy-start = (f32[8,128,256]{2,1,0:T(8,128)S(1)}, f32[8,128,256]{2,1,0:T(8,128)}, u32[]{:S(2)}) copy-start(f32[8,128,256]{2,1,0:T(8,128)} %dirs.1) | copy-start | bytes 3145732
  3.8 7.8 %collective-permute-start = (f32[13,16,256]{2,1,0:T(8,128)}, f32[13,16,256]{2,1,0:T(8,128)S(1)}, u32[]{:S(2)}, u32[]{:S(2)}) collective-permute-start(f32[13,16,256]{2,1,0:T(8,128)} %get-tuple-element.23), channel_id=1, source_target_pairs={{0,16},{16,0},{1,17},{17,1},{2,18},{18,2},{3,19},{19,3},{4,20},{20... | collective-permute-start | bytes 638984 | tf_op jit(solution)/shard_map/ppermute | solution.py:566
  4.3 7.2 %collective-permute-start.1 = (f32[2,16,8,128]{3,2,1,0:T(8,128)}, f32[2,16,8,128]{3,2,1,0:T(8,128)S(1)}, u32[]{:S(2)}, u32[]{:S(2)}) collective-permute-start(f32[2,16,8,128]{3,2,1,0:T(8,128)} %get-tuple-element.24), channel_id=1, source_target_pairs={{0,4},{8,12},{4,0},{12,8},{1,5},{9,13},{5,1},{13,9},{2,6},{10,14},... | collective-permute-start | bytes 393224 | tf_op jit(solution)/shard_map/ppermute | solution.py:566
  4.3 7.2 %collective-permute-start.2 = (f32[2,16,8,128]{3,2,1,0:T(8,128)}, f32[2,16,8,128]{3,2,1,0:T(8,128)S(1)}, u32[]{:S(2)}, u32[]{:S(2)}) collective-permute-start(f32[2,16,8,128]{3,2,1,0:T(8,128)} %get-tuple-element.25), channel_id=1, source_target_pairs={{4,8},{8,4},{5,9},{9,5},{6,10},{10,6},{7,11},{11,7},{20,24},{24,20... | collective-permute-start | bytes 393224 | tf_op jit(solution)/shard_map/ppermute | solution.py:566
  5.0 6.5 %collective-permute-start.3 = (f32[2,2,8,128]{3,2,1,0:T(8,128)}, f32[2,2,8,128]{3,2,1,0:T(8,128)S(1)}, u32[]{:S(2)}, u32[]{:S(2)}) collective-permute-start(f32[2,2,8,128]{3,2,1,0:T(8,128)} %get-tuple-element.26), channel_id=1, source_target_pairs={{0,20},{8,28},{4,16},{12,24},{16,4},{24,12},{20,0},{28,8},{1,21},{... | collective-permute-start | bytes 49160 | tf_op jit(solution)/shard_map/ppermute | solution.py:566
  9.0 2.5 %collective-permute-start.4 = (f32[2,2,8,128]{3,2,1,0:T(8,128)}, f32[2,2,8,128]{3,2,1,0:T(8,128)S(1)}, u32[]{:S(2)}, u32[]{:S(2)}) collective-permute-start(f32[2,2,8,128]{3,2,1,0:T(8,128)} %get-tuple-element.27), channel_id=1, source_target_pairs={{4,24},{8,20},{20,8},{24,4},{5,25},{9,21},{21,9},{25,5},{6,26},{10... | collective-permute-start | bytes 49160 | tf_op jit(solution)/shard_map/ppermute | solution.py:566
  9.7 1.1 %copy-start.1 = (f32[5,128,256]{2,1,0:T(8,128)S(1)}, f32[5,128,256]{2,1,0:T(8,128)}, u32[]{:S(2)}) copy-start(f32[5,128,256]{2,1,0:T(8,128)} %get-tuple-element.28.fields) | copy-start | bytes 1966084
  24.7 14.6 %collective-permute-start.5 = (f32[22,8,256]{2,1,0:T(8,128)S(1)}, f32[22,8,256]{2,1,0:T(8,128)S(1)}, u32[]{:S(2)}, u32[]{:S(2)}) collective-permute-start(f32[22,8,256]{2,1,0:T(8,128)S(1)} %get-tuple-element.32), channel_id=1, source_target_pairs={{0,2},{1,3},{2,0},{3,1},{4,6},{5,7},{6,4},{7,5},{8,10},{9,11},{10,... | collective-permute-start | bytes 540680 | tf_op jit(solution)/shard_map/ppermute | solution.py:515
  25.1 23.0 %collective-permute-start.6 = (f32[22,8,256]{2,1,0:T(8,128)S(1)}, f32[22,8,256]{2,1,0:T(8,128)S(1)}, u32[]{:S(2)}, u32[]{:S(2)}) collective-permute-start(f32[22,8,256]{2,1,0:T(8,128)S(1)} %get-tuple-element.33), channel_id=1, source_target_pairs={{0,3},{1,2},{2,1},{3,0},{4,7},{5,6},{6,5},{7,4},{8,11},{9,10},{10,... | collective-permute-start | bytes 540680 | tf_op jit(solution)/shard_map/ppermute | solution.py:515
  27.8 20.3 %collective-permute-start.7 = (f32[22,8,256]{2,1,0:T(8,128)S(1)}, f32[22,8,256]{2,1,0:T(8,128)S(1)}, u32[]{:S(2)}, u32[]{:S(2)}) collective-permute-start(f32[22,8,256]{2,1,0:T(8,128)S(1)} %get-tuple-element.34), channel_id=1, source_target_pairs={{0,1},{1,0},{2,3},{3,2},{4,5},{5,4},{6,7},{7,6},{8,9},{9,8},{10,11... | collective-permute-start | bytes 540680 | tf_op jit(solution)/shard_map/ppermute | solution.py:515
  37.1 11.5 %collective-permute-start.8 = (f32[10,8,256]{2,1,0:T(8,128)S(1)}, f32[10,8,256]{2,1,0:T(8,128)S(1)}, u32[]{:S(2)}, u32[]{:S(2)}) collective-permute-start(f32[10,8,256]{2,1,0:T(8,128)S(1)} %get-tuple-element.36), channel_id=1, source_target_pairs={{0,2},{1,3},{2,0},{3,1},{4,6},{5,7},{6,4},{7,5},{8,10},{9,11},{10,... | collective-permute-start | bytes 245768 | tf_op jit(solution)/shard_map/ppermute | solution.py:515
  37.2 14.4 %collective-permute-start.9 = (f32[10,8,256]{2,1,0:T(8,128)S(1)}, f32[10,8,256]{2,1,0:T(8,128)S(1)}, u32[]{:S(2)}, u32[]{:S(2)}) collective-permute-start(f32[10,8,256]{2,1,0:T(8,128)S(1)} %get-tuple-element.37), channel_id=1, source_target_pairs={{0,3},{1,2},{2,1},{3,0},{4,7},{5,6},{6,5},{7,4},{8,11},{9,10},{10,... | collective-permute-start | bytes 245768 | tf_op jit(solution)/shard_map/ppermute | solution.py:515
  39.3 12.3 %collective-permute-start.10 = (f32[10,8,256]{2,1,0:T(8,128)S(1)}, f32[10,8,256]{2,1,0:T(8,128)S(1)}, u32[]{:S(2)}, u32[]{:S(2)}) collective-permute-start(f32[10,8,256]{2,1,0:T(8,128)S(1)} %get-tuple-element.38), channel_id=1, source_target_pairs={{0,1},{1,0},{2,3},{3,2},{4,5},{5,4},{6,7},{7,6},{8,9},{9,8},{10,11... | collective-permute-start | bytes 245768 | tf_op jit(solution)/shard_map/ppermute | solution.py:515
  52.1 4.1 %collective-permute-start.13 = (f32[32,32]{1,0:T(8,128)S(1)}, f32[32,32]{1,0:T(8,128)S(1)}, u32[]{:S(2)}, u32[]{:S(2)}) collective-permute-start(f32[32,32]{1,0:T(8,128)S(1)} %shard_map.91), channel_id=1, source_target_pairs={{0,3},{1,2},{2,1},{3,0},{4,7},{5,6},{6,5},{7,4},{8,11},{9,10},{10,... | collective-permute-start | bytes 12296 | tf_op jit(solution)/shard_map/ppermute | solution.py:535
  52.1 4.7 %collective-permute-start.12 = (f32[32,32]{1,0:T(8,128)S(1)}, f32[32,32]{1,0:T(8,128)S(1)}, u32[]{:S(2)}, u32[]{:S(2)}) collective-permute-start(f32[32,32]{1,0:T(8,128)S(1)} %shard_map.91), channel_id=1, source_target_pairs={{0,2},{1,3},{2,0},{3,1},{4,6},{5,7},{6,4},{7,5},{8,10},{9,11},{10,... | collective-permute-start | bytes 12296 | tf_op jit(solution)/shard_map/ppermute | solution.py:535
  54.2 3.7 %collective-permute-start.11 = (f32[32,32]{1,0:T(8,128)S(1)}, f32[32,32]{1,0:T(8,128)S(1)}, u32[]{:S(2)}, u32[]{:S(2)}) collective-permute-start(f32[32,32]{1,0:T(8,128)S(1)} %shard_map.91), channel_id=1, source_target_pairs={{0,1},{1,0},{2,3},{3,2},{4,5},{5,4},{6,7},{7,6},{8,9},{9,8},{10,11... | collective-permute-start | bytes 12296 | tf_op jit(solution)/shard_map/ppermute | solution.py:535
  57.9 1.2 %collective-permute-start.14 = (f32[32,32]{1,0:T(8,128)S(1)}, f32[32,32]{1,0:T(8,128)S(1)}, u32[]{:S(2)}, u32[]{:S(2)}) collective-permute-start(f32[32,32]{1,0:T(8,128)S(1)} %add_add_fusion), channel_id=1, source_target_pairs={{0,4},{1,5},{2,6},{3,7},{4,0},{5,1},{6,2},{7,3},{8,12},{9,13},{10,... | collective-permute-start | bytes 12296 | tf_op jit(solution)/shard_map/ppermute | solution.py:535
  59.1 4.7 %collective-permute-start.17 = (f32[32,32]{1,0:T(8,128)S(1)}, f32[32,32]{1,0:T(8,128)S(1)}, u32[]{:S(2)}, u32[]{:S(2)}) collective-permute-start(f32[32,32]{1,0:T(8,128)S(1)} %add.15.refs_0_), channel_id=1, source_target_pairs={{0,24},{1,25},{2,26},{3,27},{4,28},{5,29},{6,30},{7,31},{8,16},{9,... | collective-permute-start | bytes 12296 | tf_op jit(solution)/shard_map/ppermute | solution.py:535
  59.8 4.0 %collective-permute-start.16 = (f32[32,32]{1,0:T(8,128)S(1)}, f32[32,32]{1,0:T(8,128)S(1)}, u32[]{:S(2)}, u32[]{:S(2)}) collective-permute-start(f32[32,32]{1,0:T(8,128)S(1)} %add.15.refs_0_), channel_id=1, source_target_pairs={{0,16},{1,17},{2,18},{3,19},{4,20},{5,21},{6,22},{7,23},{8,24},{9,... | collective-permute-start | bytes 12296 | tf_op jit(solution)/shard_map/ppermute | solution.py:535
  61.0 3.7 %collective-permute-start.15 = (f32[32,32]{1,0:T(8,128)S(1)}, f32[32,32]{1,0:T(8,128)S(1)}, u32[]{:S(2)}, u32[]{:S(2)}) collective-permute-start(f32[32,32]{1,0:T(8,128)S(1)} %add.15.refs_0_), channel_id=1, source_target_pairs={{0,8},{1,9},{2,10},{3,11},{4,12},{5,13},{6,14},{7,15},{8,0},{9,1},... | collective-permute-start | bytes 12296 | tf_op jit(solution)/shard_map/ppermute | solution.py:535
  66.3 17.7 %collective-permute-start.18 = (f32[32,8,256]{2,1,0:T(8,128)S(1)}, f32[32,8,256]{2,1,0:T(8,128)S(1)}, u32[]{:S(2)}, u32[]{:S(2)}) collective-permute-start(f32[32,8,256]{2,1,0:T(8,128)S(1)} %get-tuple-element.40), channel_id=1, source_target_pairs={{0,2},{1,3},{2,0},{3,1},{4,6},{5,7},{6,4},{7,5},{8,10},{9,11},{10,... | collective-permute-start | bytes 786440 | tf_op jit(solution)/shard_map/ppermute | solution.py:515
  67.4 23.6 %collective-permute-start.19 = (f32[32,8,256]{2,1,0:T(8,128)S(1)}, f32[32,8,256]{2,1,0:T(8,128)S(1)}, u32[]{:S(2)}, u32[]{:S(2)}) collective-permute-start(f32[32,8,256]{2,1,0:T(8,128)S(1)} %get-tuple-element.41), channel_id=1, source_target_pairs={{0,3},{1,2},{2,1},{3,0},{4,7},{5,6},{6,5},{7,4},{8,11},{9,10},{10,... | collective-permute-start | bytes 786440 | tf_op jit(solution)/shard_map/ppermute | solution.py:515
  69.1 21.8 %collective-permute-start.20 = (f32[32,8,256]{2,1,0:T(8,128)S(1)}, f32[32,8,256]{2,1,0:T(8,128)S(1)}, u32[]{:S(2)}, u32[]{:S(2)}) collective-permute-start(f32[32,8,256]{2,1,0:T(8,128)S(1)} %get-tuple-element.42), channel_id=1, source_target_pairs={{0,1},{1,0},{2,3},{3,2},{4,5},{5,4},{6,7},{7,6},{8,9},{9,8},{10,11... | collective-permute-start | bytes 786440 | tf_op jit(solution)/shard_map/ppermute | solution.py:515
